TPU v7x, 32 devices: a whole 2x2x4 slice. The times are simulated.
32 devices in a mesh: scene: 2 (over x), row: 16 (over z, y, core).
Axes of the slice: x: 2, y: 2, z: 4, core: 2. Of those that a mesh axis runs over, the one named last changes fastest.
Arguments:
- echoes: bfloat16 [2048, 2, 8192], P(('scene', 'row')), parts along dimension 0, may hold values from -6 to 6
- range_replica: bfloat16 [2, 1024], replicated, may hold values from -0.125 to 0.125
- azimuth_replicas: bfloat16 [16, 2, 512], replicated, may hold values from -0.1875 to 0.1875
- replica_index: int32 [16384], P(('scene', 'row')), parts along dimension 0, may hold values from 0 to 15
- azimuth_extent: int32 [128], P('scene'), parts along dimension 0, may hold values from 0 to 16
- range_extent: int32 [1024], P('scene'), parts along dimension 0, may hold values from 0 to 16
Outputs:
- focused: bfloat16 [2048, 2, 8192], P('scene', None, 'row'), parts along dimension 0
- looked: float32 [1024, 64], P(('scene', 'row')), parts along dimension 0
There are 2 independent parts, one for each index of `scene`. A program takes and returns all parts, laid end to end along the dimension named above; an argument that names none is the same for every part. Nothing has to cross between parts.
All inputs are finite; a program needn't handle non-finite values.
Results may differ from a plain program's by a relative error of at most 0.0049.
Values may be sent and summed in bfloat16 or wider, within the bound.
No kernel may reach another device: no remote copies, remote signals or barrier semaphores. Data moves between devices by JAX's collectives and lax.ppermute only.
A program may use at most 128 MiB of HBM per device.

v0:
```python
import functools

import jax
import jax.numpy as jnp
import ml_dtypes
import numpy as np
from jax import lax
from jax.experimental import pallas as pl
from jax.experimental.pallas import tpu as pltpu
from jax.sharding import PartitionSpec as P

TILE = 16
RADIX = 4
F32 = jnp.float32
BF16 = jnp.bfloat16
VMEM_LIMIT = 56 << 20


def dot(a, b):
    return jnp.dot(a, b, preferred_element_type=F32)


def dot_nt(a, b):
    return lax.dot_general(a, b, (((1,), (1,)), ((), ())), preferred_element_type=F32)


def split(x):
    high = x.astype(BF16)
    low = (x - high.astype(F32)).astype(BF16)
    return high, low


@functools.lru_cache(maxsize=None)
def phase_matrices(length):
    part = length // RADIX
    k = np.arange(part)
    q = np.arange(RADIX)
    phase = (k[None, None, :] * (RADIX * k[None, :, None] + q[:, None, None])) % length
    angle = phase * (-2.0 * np.pi / length)
    re, im = np.cos(angle), np.sin(angle)
    full = np.concatenate([np.concatenate([re, -im], axis=2), np.concatenate([im, re], axis=2)], axis=1)

    def terms(matrix):
        high = matrix.astype(ml_dtypes.bfloat16)
        low = (matrix - high.astype(np.float64)).astype(ml_dtypes.bfloat16)
        return np.stack([high, low])

    return terms(full), terms(np.ascontiguousarray(full.transpose(0, 2, 1)))


def send_order(count):
    if count < 8:
        return list(range(1, count))
    quarter = count // 4
    order = []
    for low in range(quarter):
        order += [2 * quarter + low, 3 * quarter + low, quarter + low]
        if low:
            order.append(low)
    return order


def range_kernel(offsets, width, block, me_ref, x_ref, h_ref, *refs):
    outs, table = refs[:-1], refs[-1]
    rows = x_ref.shape[0]
    taps = h_ref.shape[1]
    count = x_ref.shape[2] // width
    replica = h_ref[...].astype(F32)
    for part in range(2):
        line = jnp.concatenate([replica[part : part + 1], jnp.zeros((1, block), F32)], axis=1)
        lines = jnp.broadcast_to(line, (block, taps + block))
        table[part] = pltpu.roll(lines, 0, 1, stride=1, stride_axis=0).astype(BF16)
    me = me_ref[0]
    for offset, out in zip(offsets, outs):
        owner = me ^ offset
        pieces = []
        for step in range(1 + -(-taps // width)):
            place = owner + step
            start = pl.multiple_of(jnp.minimum(place, count - 1) * width, width)
            piece = jnp.swapaxes(x_ref[:, :, pl.ds(start, width)], 0, 1)
            if step:
                piece = jnp.where(place < count, piece, jnp.zeros_like(piece))
            pieces.append(piece.reshape(2 * rows, width))
        window = jnp.concatenate(pieces, axis=1)
        subs = width // block
        stacked = jnp.concatenate(
            [window[:, j * block : j * block + block + taps] for j in range(subs)], axis=0
        )
        with_real = dot_nt(stacked, table[0])
        with_imag = dot_nt(stacked, table[1])
        for j in range(subs):
            at = 2 * rows * j
            re, im = slice(at, at + rows), slice(at + rows, at + 2 * rows)
            cells = slice(j * block, (j + 1) * block)
            out[0, :, cells] = (with_real[re] + with_imag[im]).astype(BF16)
            out[1, :, cells] = (with_real[im] - with_imag[re]).astype(BF16)


def compress(me, echoes, range_replica, offsets, width):
    rows = echoes.shape[0]
    taps = range_replica.shape[1]
    block = min(256, width)
    vmem = pl.BlockSpec(memory_space=pltpu.VMEM)
    flops = len(offsets) * 8 * rows * width * (taps + block)
    return pl.pallas_call(
        functools.partial(range_kernel, tuple(offsets), width, block),
        out_shape=[jax.ShapeDtypeStruct((2, rows, width), BF16)] * len(offsets),
        in_specs=[pl.BlockSpec(memory_space=pltpu.SMEM), vmem, vmem],
        out_specs=[vmem] * len(offsets),
        scratch_shapes=[pltpu.VMEM((2, block, taps + block), BF16)],
        compiler_params=pltpu.CompilerParams(vmem_limit_bytes=VMEM_LIMIT),
        cost_estimate=pl.CostEstimate(flops=flops, bytes_accessed=echoes.size * 4, transcendentals=0),
        name="range_compress",
    )(me, echoes, range_replica)


def butterfly(x, sign):
    (ar, ai), (br, bi), (cr, ci), (dr, di) = x
    pr, pi, mr, mi = ar + cr, ai + ci, ar - cr, ai - ci
    sr, si, tr, ti = br + dr, bi + di, br - dr, bi - di
    if sign < 0:
        tr, ti = ti, -tr
    else:
        tr, ti = -ti, tr
    return [(pr + sr, pi + si), (mr + tr, mi + ti), (pr - sr, pi - si), (mr - tr, mi - ti)]


def spectra_kernel(taps_ref, index_ref, matrix_ref, out_ref):
    part = matrix_ref.shape[-1] // 2
    length = part * RADIX
    replicas = taps_ref.shape[-1]
    width = index_ref.shape[1]
    tap_count = taps_ref.shape[1]
    zero = jnp.zeros((part, replicas), F32)
    pieces = []
    for q in range(RADIX):
        if (q + 1) * part <= tap_count:
            pieces.append(tuple(taps_ref[c, q * part : (q + 1) * part].astype(F32) for c in range(2)))
        else:
            pieces.append((zero, zero))
    chosen = lax.broadcasted_iota(jnp.int32, (replicas, width), 0) == index_ref[...]
    chosen = chosen.astype(F32).astype(BF16)
    for q, (re, im) in enumerate(butterfly(pieces, -1)):
        high, low = split(jnp.concatenate([re, im], axis=0))
        spectrum = dot(matrix_ref[0, q], high) + dot(matrix_ref[1, q], high) + dot(matrix_ref[0, q], low)
        high, low = split(spectrum * (1.0 / length))
        out_ref[q] = dot(high, chosen) + dot(low, chosen)


def azimuth_kernel(
    offsets, me_ref, forward_ref, inverse_ref, chosen_ref, pulse_ref, range_ref, *refs
):
    sources = refs[: len(offsets)]
    focused_ref, sums_ref, x_ref, v_ref, power_ref = refs[len(offsets) :]
    rows = sources[0].shape[1]
    length = x_ref.shape[1]
    part = length // RADIX
    me = me_ref[0]
    for offset, source in zip(offsets, sources):
        start = pl.multiple_of((me ^ offset) * rows, rows)
        for c in range(2):
            x_ref[c, pl.ds(start, rows), :] = source[c]
    x = [
        tuple(x_ref[c, q * part : (q + 1) * part, :].astype(F32) for c in range(2)) for q in range(RADIX)
    ]
    for q, (re, im) in enumerate(butterfly(x, -1)):
        high, low = split(jnp.concatenate([re, im], axis=0))
        spectrum = dot(forward_ref[0, q], high) + dot(forward_ref[1, q], high) + dot(forward_ref[0, q], low)
        sr, si = spectrum[:part], spectrum[part:]
        gr, gi = chosen_ref[q, :part], chosen_ref[q, part:]
        high, low = split(jnp.concatenate([sr * gr + si * gi, si * gr - sr * gi], axis=0))
        v_ref[q] = dot(inverse_ref[0, q], high) + dot(inverse_ref[1, q], high) + dot(inverse_ref[0, q], low)
    v = [(v_ref[q, :part], v_ref[q, part:]) for q in range(RADIX)]
    for q, (re, im) in enumerate(butterfly(v, 1)):
        span = slice(q * part, (q + 1) * part)
        both = jnp.stack([re.astype(BF16), im.astype(BF16)], axis=0)
        focused_ref[span] = jnp.swapaxes(both, 0, 1)
        high, low = split(re * re + im * im)
        power_ref[0, span] = high
        power_ref[1, span] = low
    pulse_mask = pulse_ref[...]
    high, low = split(dot(pulse_mask, power_ref[0]) + dot(pulse_mask, power_ref[1]))
    range_mask = range_ref[...]
    sums = dot_nt(range_mask, high) + dot_nt(range_mask, low)

    @pl.when(pl.program_id(0) == 0)
    def _():
        sums_ref[...] = sums

    @pl.when(pl.program_id(0) > 0)
    def _():
        sums_ref[...] += sums


def per_device(
    echoes, range_replica, azimuth_replicas, replica_index, azimuth_extent, range_extent
):
    count = lax.axis_size("row")
    device = lax.axis_index("row")
    me = device.astype(jnp.int32)[None]
    rows, _, samples = echoes.shape
    pulses = rows * count
    width = samples // count
    part = pulses // RADIX
    replicas = azimuth_replicas.shape[0]

    offsets = send_order(count) + [0]
    pieces = compress(me, echoes, range_replica, offsets, width)
    received = []
    for offset, piece in zip(offsets, pieces):
        if offset:
            piece = lax.ppermute(piece, "row", [(i, i ^ offset) for i in range(count)])
        received.append(piece)

    forward, inverse = (jnp.asarray(m) for m in phase_matrices(pulses))
    taps = jnp.transpose(azimuth_replicas, (1, 2, 0))
    chosen = pl.pallas_call(
        spectra_kernel,
        out_shape=jax.ShapeDtypeStruct((RADIX, 2 * part, width), F32),
        compiler_params=pltpu.CompilerParams(vmem_limit_bytes=VMEM_LIMIT),
        cost_estimate=pl.CostEstimate(flops=4 << 30, bytes_accessed=12 << 20, transcendentals=0),
        name="replica_spectra",
    )(taps, replica_index[None, :], forward)

    pulse_tiles = pulses // TILE
    pulse_start = jnp.arange(pulse_tiles, dtype=jnp.int32) * TILE - azimuth_extent
    pulse_stop = pulse_start + TILE + 2 * azimuth_extent
    at = jnp.arange(pulses, dtype=jnp.int32)[None, :]
    pulse_mask = ((at >= pulse_start[:, None]) & (at < pulse_stop[:, None])).astype(BF16)
    pulse_count = jnp.minimum(pulse_stop, pulses) - jnp.maximum(pulse_start, 0)

    tiles = width // TILE
    mask_rows = -(-(tiles + 2) // 16) * 16
    place = jnp.arange(mask_rows, dtype=jnp.int32)
    tile = device * tiles + jnp.where(place == tiles, -1, jnp.where(place == tiles + 1, tiles, place))
    exists = (place < tiles + 2) & (tile >= 0) & (tile < tiles * count)
    extent = range_extent[jnp.clip(tile, 0, tiles * count - 1)]
    range_start = tile * TILE - extent
    range_stop = range_start + TILE + 2 * extent
    at = device * width + jnp.arange(width, dtype=jnp.int32)[None, :]
    range_mask = (
        exists[:, None] & (at >= range_start[:, None]) & (at < range_stop[:, None])
    ).astype(BF16)
    range_count = (jnp.minimum(range_stop, samples) - jnp.maximum(range_start, 0))[:tiles]
    cells = (range_count[:, None] * pulse_count[None, :]).astype(F32)

    chunk = min(width, 256)
    steps = width // chunk
    whole = lambda shape: pl.BlockSpec(shape, lambda i: (0,) * len(shape), pipeline_mode=pl.Buffered(1))
    focused, sums = pl.pallas_call(
        functools.partial(azimuth_kernel, tuple(offsets)),
        grid=(steps,),
        out_shape=[
            jax.ShapeDtypeStruct((pulses, 2, width), BF16),
            jax.ShapeDtypeStruct((mask_rows, pulse_tiles), F32),
        ],
        in_specs=[
            pl.BlockSpec(memory_space=pltpu.SMEM),
            whole((2, RADIX, 2 * part, 2 * part)),
            whole((2, RADIX, 2 * part, 2 * part)),
            pl.BlockSpec((RADIX, 2 * part, chunk), lambda i: (0, 0, i)),
            whole((pulse_tiles, pulses)),
            pl.BlockSpec((mask_rows, chunk), lambda i: (0, i)),
        ]
        + [pl.BlockSpec((2, rows, chunk), lambda i: (0, 0, i))] * count,
        out_specs=[
            pl.BlockSpec((pulses, 2, chunk), lambda i: (0, 0, i)),
            pl.BlockSpec((mask_rows, pulse_tiles), lambda i: (0, 0)),
        ],
        scratch_shapes=[
            pltpu.VMEM((2, pulses, chunk), BF16),
            pltpu.VMEM((RADIX, 2 * part, chunk), F32),
            pltpu.VMEM((2, pulses, chunk), BF16),
        ],
        compiler_params=pltpu.CompilerParams(vmem_limit_bytes=VMEM_LIMIT),
        name="azimuth_focus",
    )(me, forward, inverse, chosen, pulse_mask, range_mask, *received)

    to_left = lax.ppermute(sums[tiles : tiles + 1], "row", [(i, i - 1) for i in range(1, count)])
    to_right = lax.ppermute(sums[tiles + 1 : tiles + 2], "row", [(i, i + 1) for i in range(count - 1)])
    pad = jnp.zeros((tiles - 2, pulse_tiles), F32)
    edges = jnp.concatenate([to_right, pad, to_left], axis=0)
    looked = (sums[:tiles] + edges) / cells
    return focused, looked


def solution(mesh):
    return jax.shard_map(
        per_device,
        mesh=mesh,
        in_specs=(
            P(("scene", "row"), None, None),
            P(),
            P(),
            P(("scene", "row")),
            P("scene"),
            P("scene"),
        ),
        out_specs=(P("scene", None, "row"), P(("scene", "row"), None)),
        check_vma=False,
    )
```

profile of v0, /device:TPU:13, one launch (start us, length us, event | category | flops | bytes accessed | tf_op | source)
XLA Modules:
  0.0 94.1 jit_solution(4320329584051245714)
XLA Ops:
  0.7 9.3 %range_compress.1 = (bf16[2,64,512]{2,1,0:T(8,128)(2,1)}, bf16[2,64,512]{2,1,0:T(8,128)(2,1)}, bf16[2,64,512]{2,1,0:T(8,128)(2,1)}, bf16[2,64,512]{2,1,0:T(8,128...) custom-call(s32[1]{0:T(128)} %bitcast.me_ref, ...), custom_call_target="tpu_custom_call" | custom-call | flops 5368709120 | bytes 4194304 | tf_op jit(solution)/shard_map/range_compress/pallas_call | solution.py:105
  10.0 2.3 %collective-permute-start = (bf16[2,64,512]{2,1,0:T(8,128)(2,1)}, bf16[2,64,512]{2,1,0:T(8,128)(2,1)S(1)}, u32[]{:S(2)}, u32[]{:S(2)}) collective-permute-start(bf16[2,64,512]{2,1,0:T(8,128)(2,1)} %get-tuple-element.20), channel_id=1, source_target_pairs={{0,8},{1,9},{2,10},{3,11},{4,12},{5,13},{6,14},{7,15},{8,0},{9,1},... | collective-permute-start | bytes 393224 | tf_op jit(solution)/shard_map/ppermute | solution.py:212
  12.3 0.3 collective-permute-start.10
  12.6 4.6 %collective-permute-start.11 = (bf16[2,64,512]{2,1,0:T(8,128)(2,1)}, bf16[2,64,512]{2,1,0:T(8,128)(2,1)S(1)}, u32[]{:S(2)}, u32[]{:S(2)}) collective-permute-start(bf16[2,64,512]{2,1,0:T(8,128)(2,1)} %get-tuple-element.31), channel_id=1, source_target_pairs={{0,11},{1,10},{2,9},{3,8},{4,15},{5,14},{6,13},{7,12},{8,3},{9,2},... | collective-permute-start | bytes 393224 | tf_op jit(solution)/shard_map/ppermute | solution.py:212
  17.2 0.8 gather_fusion
  18.1 0.9 copy.11
  18.9 0.8 fusion.1.pulse_ref
  19.7 9.3 %replica_spectra.1.chosen_ref = f32[4,512,512]{2,1,0:T(8,128)} custom-call(bf16[2,512,16]{2,1,0:T(8,128)(2,1)} %bitcast.6, s32[1,512]{1,0:T(1,128)} %bitcast.8, bf16[2,4,512,512]{3,2,1,0:T(8,128)(2,1)} %constant.9.clone.matrix_ref.forward_ref), custom_call_target="tpu_custom_call" | custom-call | flops 4294967296 | bytes 12582912 | tf_op jit(solution)/shard_map/replica_spectra/pallas_call | solution.py:217
  29.1 2.2 %collective-permute-start.13 = (bf16[2,64,512]{2,1,0:T(8,128)(2,1)S(1)}, bf16[2,64,512]{2,1,0:T(8,128)(2,1)S(1)}, u32[]{:S(2)}, u32[]{:S(2)}) collective-permute-start(bf16[2,64,512]{2,1,0:T(8,128)(2,1)S(1)} %copy-done.27), channel_id=1, source_target_pairs={{0,7},{1,6},{2,5},{3,4},{4,3},{5,2},{6,1},{7,0},{8,15},{9,14},{10,... | collective-permute-start | bytes 393224 | tf_op jit(solution)/shard_map/ppermute | solution.py:212
  31.4 0.5 collective-permute-start.14
  31.9 0.3 collective-permute-start.2
  32.2 0.4 collective-permute-done.11.refs_11_
  32.6 3.4 %collective-permute-start.3 = (bf16[2,64,512]{2,1,0:T(8,128)(2,1)S(1)}, bf16[2,64,512]{2,1,0:T(8,128)(2,1)S(1)}, u32[]{:S(2)}, u32[]{:S(2)}) collective-permute-start(bf16[2,64,512]{2,1,0:T(8,128)(2,1)S(1)} %copy-done.24), channel_id=1, source_target_pairs={{0,9},{1,8},{2,11},{3,10},{4,13},{5,12},{6,15},{7,14},{8,1},{9,0},... | collective-permute-start | bytes 393224 | tf_op jit(solution)/shard_map/ppermute | solution.py:212
  36.1 1.1 %collective-permute-done.12.refs_12_ = bf16[2,64,512]{2,1,0:T(8,128)(2,1)S(1)} collective-permute-done((bf16[2,64,512]{2,1,0:T(8,128)(2,1)}, bf16[2,64,512]{2,1,0:T(8,128)(2,1)S(1)}, u32[]{:S(2)}, u32[]{:S(2)}) %collective-permute-start.12) | collective-permute-done | bytes 131104 | tf_op jit(solution)/shard_map/ppermute | solution.py:212
  37.2 3.2 %collective-permute-start.4 = (bf16[2,64,512]{2,1,0:T(8,128)(2,1)S(1)}, bf16[2,64,512]{2,1,0:T(8,128)(2,1)S(1)}, u32[]{:S(2)}, u32[]{:S(2)}) collective-permute-start(bf16[2,64,512]{2,1,0:T(8,128)(2,1)S(1)} %copy-done.23), channel_id=1, source_target_pairs={{0,13},{1,12},{2,15},{3,14},{4,9},{5,8},{6,11},{7,10},{8,5},{9,4},... | collective-permute-start | bytes 393224 | tf_op jit(solution)/shard_map/ppermute | solution.py:212
  40.4 0.1 collective-permute-start.5
  40.5 0.3 collective-permute-done.14.refs_14_
  40.8 0.3 collective-permute-start.6
  41.1 2.2 %collective-permute-start.7 = (bf16[2,64,512]{2,1,0:T(8,128)(2,1)S(1)}, bf16[2,64,512]{2,1,0:T(8,128)(2,1)S(1)}, u32[]{:S(2)}, u32[]{:S(2)}) collective-permute-start(bf16[2,64,512]{2,1,0:T(8,128)(2,1)S(1)} %copy-done.20), channel_id=1, source_target_pairs={{0,10},{1,11},{2,8},{3,9},{4,14},{5,15},{6,12},{7,13},{8,2},{9,3},... | collective-permute-start | bytes 393224 | tf_op jit(solution)/shard_map/ppermute | solution.py:212
  43.3 2.2 %collective-permute-done.3.refs_3_ = bf16[2,64,512]{2,1,0:T(8,128)(2,1)S(1)} collective-permute-done((bf16[2,64,512]{2,1,0:T(8,128)(2,1)S(1)}, bf16[2,64,512]{2,1,0:T(8,128)(2,1)S(1)}, u32[]{:S(2)}, u32[]{:S(2)}) %collective-permute-start.3) | collective-permute-done | bytes 131104 | tf_op jit(solution)/shard_map/ppermute | solution.py:212
  45.5 8.3 %collective-permute-done.4.refs_4_ = bf16[2,64,512]{2,1,0:T(8,128)(2,1)S(1)} collective-permute-done((bf16[2,64,512]{2,1,0:T(8,128)(2,1)S(1)}, bf16[2,64,512]{2,1,0:T(8,128)(2,1)S(1)}, u32[]{:S(2)}, u32[]{:S(2)}) %collective-permute-start.4) | collective-permute-done | bytes 131104 | tf_op jit(solution)/shard_map/ppermute | solution.py:212
  53.8 0.7 and_convert_fusion.range_ref
  54.6 2.2 %collective-permute-done.7.refs_7_ = bf16[2,64,512]{2,1,0:T(8,128)(2,1)S(1)} collective-permute-done((bf16[2,64,512]{2,1,0:T(8,128)(2,1)S(1)}, bf16[2,64,512]{2,1,0:T(8,128)(2,1)S(1)}, u32[]{:S(2)}, u32[]{:S(2)}) %collective-permute-start.7) | collective-permute-done | bytes 131104 | tf_op jit(solution)/shard_map/ppermute | solution.py:212
  56.8 5.9 %collective-permute-done.8.refs_8_ = bf16[2,64,512]{2,1,0:T(8,128)(2,1)S(1)} collective-permute-done((bf16[2,64,512]{2,1,0:T(8,128)(2,1)S(1)}, bf16[2,64,512]{2,1,0:T(8,128)(2,1)S(1)}, u32[]{:S(2)}, u32[]{:S(2)}) %collective-permute-start.8) | collective-permute-done | bytes 131104 | tf_op jit(solution)/shard_map/ppermute | solution.py:212
  62.8 0.5 copy-done.14
  63.4 17.8 %azimuth_focus.1 = (bf16[1024,2,512]{2,1,0:T(2,128)(2,1)}, f32[48,64]{1,0:T(8,128)}) custom-call(s32[1]{0:T(128)} %bitcast.me_ref, bf16[2,4,512,512]{3,2,1,0:T(8,128)(2,1)} %constant.9.clone.matrix_ref.forward_ref, bf16[2,4,512,512]{3,2,1,0:T(8,128)(2,1)} %constant.10.clone.inverse_ref, f32[4,512,512]{2,1,0:T(8,128)} %replica_spectra.1.chosen_ref, ...), custom_call_target="tpu_custom_call" | custom-call | tf_op jit(solution)/shard_map/azimuth_focus/pallas_call | solution.py:250
  81.2 0.8 fusion.7
  81.9 5.0 %collective-permute-start.15 = (f32[1,64]{1,0:T(1,128)S(1)}, f32[1,64]{1,0:T(1,128)S(1)}, u32[]{:S(2)}, u32[]{:S(2)}) collective-permute-start(f32[1,64]{1,0:T(1,128)S(1)} %get-tuple-element.40), channel_id=1, source_target_pairs={{0,1},{1,2},{2,3},{3,4},{4,5},{5,6},{6,7},{7,8},{8,9},{9,10},{10,1... | collective-permute-start | bytes 776 | tf_op jit(solution)/shard_map/ppermute | solution.py:280
  86.9 1.9 %collective-permute-start.16 = (f32[1,64]{1,0:T(1,128)S(1)}, f32[1,64]{1,0:T(1,128)S(1)}, u32[]{:S(2)}, u32[]{:S(2)}) collective-permute-start(f32[1,64]{1,0:T(1,128)S(1)} %get-tuple-element.41), channel_id=1, source_target_pairs={{1,0},{2,1},{3,2},{4,3},{5,4},{6,5},{7,6},{8,7},{9,8},{10,9},{11,1... | collective-permute-start | bytes 776 | tf_op jit(solution)/shard_map/ppermute | solution.py:279
  88.9 0.1 pad.1.clone
  88.9 3.7 %collective-permute-done.16 = f32[1,64]{1,0:T(1,128)S(1)} collective-permute-done((f32[1,64]{1,0:T(1,128)S(1)}, f32[1,64]{1,0:T(1,128)S(1)}, u32[]{:S(2)}, u32[]{:S(2)}) %collective-permute-start.16) | collective-permute-done | bytes 288 | tf_op jit(solution)/shard_map/ppermute | solution.py:279
  92.7 1.4 %fusion.2 = f32[32,64]{1,0:T(8,128)} fusion(f32[1,64]{1,0:T(1,128)S(1)} %collective-permute-done.16, f32[1,64]{1,0:T(1,128)S(1)} %collective-permute-done.15, f32[48,64]{1,0:T(8,128)} %get-tuple-element.37, f32[32]{0:T(128)S(1)} %pad.1.clone, s32[64]{0:T(128)S(1)} %get-tuple-element.42, s32[32]{0:T(128)S(1)} %bitcast.7), kind=kLoop, calls=%fused_computation.7 | loop fusion | flops 12288 | bytes 17408 | tf_op jit(solution)/shard_map/div | solution.py:283
  (76 shorter events, 0.3 us)
Async XLA Ops:
  0.7 17.4 %copy-start.16 = (bf16[16,2,512]{2,1,0:T(2,128)(2,1)S(1)}, bf16[16,2,512]{2,1,0:T(2,128)(2,1)}, u32[]{:S(2)}) copy-start(bf16[16,2,512]{2,1,0:T(2,128)(2,1)} %param.10) | copy-start | bytes 98308
  10.0 19.1 %collective-permute-start = (bf16[2,64,512]{2,1,0:T(8,128)(2,1)}, bf16[2,64,512]{2,1,0:T(8,128)(2,1)S(1)}, u32[]{:S(2)}, u32[]{:S(2)}) collective-permute-start(bf16[2,64,512]{2,1,0:T(8,128)(2,1)} %get-tuple-element.20), channel_id=1, source_target_pairs={{0,8},{1,9},{2,10},{3,11},{4,12},{5,13},{6,14},{7,15},{8,0},{9,1},... | collective-permute-start | bytes 393224 | tf_op jit(solution)/shard_map/ppermute | solution.py:212
  12.3 19.0 %collective-permute-start.1 = (bf16[2,64,512]{2,1,0:T(8,128)(2,1)}, bf16[2,64,512]{2,1,0:T(8,128)(2,1)S(1)}, u32[]{:S(2)}, u32[]{:S(2)}) collective-permute-start(bf16[2,64,512]{2,1,0:T(8,128)(2,1)} %get-tuple-element.21), channel_id=1, source_target_pairs={{0,12},{1,13},{2,14},{3,15},{4,8},{5,9},{6,10},{7,11},{8,4},{9,5},... | collective-permute-start | bytes 393224 | tf_op jit(solution)/shard_map/ppermute | solution.py:212
  12.3 19.6 %collective-permute-start.10 = (bf16[2,64,512]{2,1,0:T(8,128)(2,1)}, bf16[2,64,512]{2,1,0:T(8,128)(2,1)S(1)}, u32[]{:S(2)}, u32[]{:S(2)}) collective-permute-start(bf16[2,64,512]{2,1,0:T(8,128)(2,1)} %get-tuple-element.30), channel_id=1, source_target_pairs={{0,2},{1,3},{2,0},{3,1},{4,6},{5,7},{6,4},{7,5},{8,10},{9,11},{10,... | collective-permute-start | bytes 393224 | tf_op jit(solution)/shard_map/ppermute | solution.py:212
  12.6 20.0 %collective-permute-start.11 = (bf16[2,64,512]{2,1,0:T(8,128)(2,1)}, bf16[2,64,512]{2,1,0:T(8,128)(2,1)S(1)}, u32[]{:S(2)}, u32[]{:S(2)}) collective-permute-start(bf16[2,64,512]{2,1,0:T(8,128)(2,1)} %get-tuple-element.31), channel_id=1, source_target_pairs={{0,11},{1,10},{2,9},{3,8},{4,15},{5,14},{6,13},{7,12},{8,3},{9,2},... | collective-permute-start | bytes 393224 | tf_op jit(solution)/shard_map/ppermute | solution.py:212
  17.2 20.0 %collective-permute-start.12 = (bf16[2,64,512]{2,1,0:T(8,128)(2,1)}, bf16[2,64,512]{2,1,0:T(8,128)(2,1)S(1)}, u32[]{:S(2)}, u32[]{:S(2)}) collective-permute-start(bf16[2,64,512]{2,1,0:T(8,128)(2,1)} %get-tuple-element.32), channel_id=1, source_target_pairs={{0,15},{1,14},{2,13},{3,12},{4,11},{5,10},{6,9},{7,8},{8,7},{9,6},... | collective-permute-start | bytes 393224 | tf_op jit(solution)/shard_map/ppermute | solution.py:212
  19.7 17.5 %copy-start.23 = (bf16[2,64,512]{2,1,0:T(8,128)(2,1)S(1)}, bf16[2,64,512]{2,1,0:T(8,128)(2,1)}, u32[]{:S(2)}) copy-start(bf16[2,64,512]{2,1,0:T(8,128)(2,1)} %get-tuple-element.24) | copy-start | bytes 393220
  19.7 20.7 %copy-start.22 = (bf16[2,64,512]{2,1,0:T(8,128)(2,1)S(1)}, bf16[2,64,512]{2,1,0:T(8,128)(2,1)}, u32[]{:S(2)}) copy-start(bf16[2,64,512]{2,1,0:T(8,128)(2,1)} %get-tuple-element.25) | copy-start | bytes 393220
  19.7 21.1 %copy-start.21 = (bf16[2,64,512]{2,1,0:T(8,128)(2,1)S(1)}, bf16[2,64,512]{2,1,0:T(8,128)(2,1)}, u32[]{:S(2)}) copy-start(bf16[2,64,512]{2,1,0:T(8,128)(2,1)} %get-tuple-element.26) | copy-start | bytes 393220
  19.7 21.4 %copy-start.20 = (bf16[2,64,512]{2,1,0:T(8,128)(2,1)S(1)}, bf16[2,64,512]{2,1,0:T(8,128)(2,1)}, u32[]{:S(2)}) copy-start(bf16[2,64,512]{2,1,0:T(8,128)(2,1)} %get-tuple-element.27) | copy-start | bytes 393220
  19.7 25.8 %copy-start.19 = (bf16[2,64,512]{2,1,0:T(8,128)(2,1)S(1)}, bf16[2,64,512]{2,1,0:T(8,128)(2,1)}, u32[]{:S(2)}) copy-start(bf16[2,64,512]{2,1,0:T(8,128)(2,1)} %get-tuple-element.28) | copy-start | bytes 393220
  19.7 34.1 %copy-start.18 = (bf16[2,64,512]{2,1,0:T(8,128)(2,1)S(1)}, bf16[2,64,512]{2,1,0:T(8,128)(2,1)}, u32[]{:S(2)}) copy-start(bf16[2,64,512]{2,1,0:T(8,128)(2,1)} %get-tuple-element.29) | copy-start | bytes 393220
  29.1 33.6 %copy-start.1 = (bf16[2,64,512]{2,1,0:T(8,128)(2,1)}, bf16[2,64,512]{2,1,0:T(8,128)(2,1)S(1)}, u32[]{:S(2)}) copy-start(bf16[2,64,512]{2,1,0:T(8,128)(2,1)S(1)} %collective-permute-done.refs_0_) | copy-start | bytes 393220
  29.1 11.3 %collective-permute-start.13 = (bf16[2,64,512]{2,1,0:T(8,128)(2,1)S(1)}, bf16[2,64,512]{2,1,0:T(8,128)(2,1)S(1)}, u32[]{:S(2)}, u32[]{:S(2)}) collective-permute-start(bf16[2,64,512]{2,1,0:T(8,128)(2,1)S(1)} %copy-done.27), channel_id=1, source_target_pairs={{0,7},{1,6},{2,5},{3,4},{4,3},{5,2},{6,1},{7,0},{8,15},{9,14},{10,... | collective-permute-start | bytes 393224 | tf_op jit(solution)/shard_map/ppermute | solution.py:212
  31.4 31.4 %copy-start.2 = (bf16[2,64,512]{2,1,0:T(8,128)(2,1)}, bf16[2,64,512]{2,1,0:T(8,128)(2,1)S(1)}, u32[]{:S(2)}) copy-start(bf16[2,64,512]{2,1,0:T(8,128)(2,1)S(1)} %collective-permute-done.1.refs_1_) | copy-start | bytes 393220
  31.4 9.5 %collective-permute-start.14 = (bf16[2,64,512]{2,1,0:T(8,128)(2,1)S(1)}, bf16[2,64,512]{2,1,0:T(8,128)(2,1)S(1)}, u32[]{:S(2)}, u32[]{:S(2)}) collective-permute-start(bf16[2,64,512]{2,1,0:T(8,128)(2,1)S(1)} %copy-done.26), channel_id=1, source_target_pairs={{0,3},{1,2},{2,1},{3,0},{4,7},{5,6},{6,5},{7,4},{8,11},{9,10},{10,... | collective-permute-start | bytes 393224 | tf_op jit(solution)/shard_map/ppermute | solution.py:212
  31.9 30.8 %copy-start.3 = (bf16[2,64,512]{2,1,0:T(8,128)(2,1)}, bf16[2,64,512]{2,1,0:T(8,128)(2,1)S(1)}, u32[]{:S(2)}) copy-start(bf16[2,64,512]{2,1,0:T(8,128)(2,1)S(1)} %collective-permute-done.10.refs_10_) | copy-start | bytes 393220
  31.9 9.2 %collective-permute-start.2 = (bf16[2,64,512]{2,1,0:T(8,128)(2,1)S(1)}, bf16[2,64,512]{2,1,0:T(8,128)(2,1)S(1)}, u32[]{:S(2)}, u32[]{:S(2)}) collective-permute-start(bf16[2,64,512]{2,1,0:T(8,128)(2,1)S(1)} %copy-done.25), channel_id=1, source_target_pairs={{0,4},{1,5},{2,6},{3,7},{4,0},{5,1},{6,2},{7,3},{8,12},{9,13},{10,... | collective-permute-start | bytes 393224 | tf_op jit(solution)/shard_map/ppermute | solution.py:212
  32.6 30.1 %copy-start.4 = (bf16[2,64,512]{2,1,0:T(8,128)(2,1)}, bf16[2,64,512]{2,1,0:T(8,128)(2,1)S(1)}, u32[]{:S(2)}) copy-start(bf16[2,64,512]{2,1,0:T(8,128)(2,1)S(1)} %collective-permute-done.11.refs_11_) | copy-start | bytes 393220
  32.6 12.9 %collective-permute-start.3 = (bf16[2,64,512]{2,1,0:T(8,128)(2,1)S(1)}, bf16[2,64,512]{2,1,0:T(8,128)(2,1)S(1)}, u32[]{:S(2)}, u32[]{:S(2)}) collective-permute-start(bf16[2,64,512]{2,1,0:T(8,128)(2,1)S(1)} %copy-done.24), channel_id=1, source_target_pairs={{0,9},{1,8},{2,11},{3,10},{4,13},{5,12},{6,15},{7,14},{8,1},{9,0},... | collective-permute-start | bytes 393224 | tf_op jit(solution)/shard_map/ppermute | solution.py:212
  37.2 25.5 %copy-start.5 = (bf16[2,64,512]{2,1,0:T(8,128)(2,1)}, bf16[2,64,512]{2,1,0:T(8,128)(2,1)S(1)}, u32[]{:S(2)}) copy-start(bf16[2,64,512]{2,1,0:T(8,128)(2,1)S(1)} %collective-permute-done.12.refs_12_) | copy-start | bytes 393220
  37.2 16.6 %collective-permute-start.4 = (bf16[2,64,512]{2,1,0:T(8,128)(2,1)S(1)}, bf16[2,64,512]{2,1,0:T(8,128)(2,1)S(1)}, u32[]{:S(2)}, u32[]{:S(2)}) collective-permute-start(bf16[2,64,512]{2,1,0:T(8,128)(2,1)S(1)} %copy-done.23), channel_id=1, source_target_pairs={{0,13},{1,12},{2,15},{3,14},{4,9},{5,8},{6,11},{7,10},{8,5},{9,4},... | collective-permute-start | bytes 393224 | tf_op jit(solution)/shard_map/ppermute | solution.py:212
  40.4 22.4 %copy-start.6 = (bf16[2,64,512]{2,1,0:T(8,128)(2,1)}, bf16[2,64,512]{2,1,0:T(8,128)(2,1)S(1)}, u32[]{:S(2)}) copy-start(bf16[2,64,512]{2,1,0:T(8,128)(2,1)S(1)} %collective-permute-done.13.refs_13_) | copy-start | bytes 393220
  40.4 14.1 %collective-permute-start.5 = (bf16[2,64,512]{2,1,0:T(8,128)(2,1)S(1)}, bf16[2,64,512]{2,1,0:T(8,128)(2,1)S(1)}, u32[]{:S(2)}, u32[]{:S(2)}) collective-permute-start(bf16[2,64,512]{2,1,0:T(8,128)(2,1)S(1)} %copy-done.22), channel_id=1, source_target_pairs={{0,5},{1,4},{2,7},{3,6},{4,1},{5,0},{6,3},{7,2},{8,13},{9,12},{10,... | collective-permute-start | bytes 393224 | tf_op jit(solution)/shard_map/ppermute | solution.py:212
  40.8 21.9 %copy-start.7 = (bf16[2,64,512]{2,1,0:T(8,128)(2,1)}, bf16[2,64,512]{2,1,0:T(8,128)(2,1)S(1)}, u32[]{:S(2)}) copy-start(bf16[2,64,512]{2,1,0:T(8,128)(2,1)S(1)} %collective-permute-done.14.refs_14_) | copy-start | bytes 393220
  40.8 13.7 %collective-permute-start.6 = (bf16[2,64,512]{2,1,0:T(8,128)(2,1)S(1)}, bf16[2,64,512]{2,1,0:T(8,128)(2,1)S(1)}, u32[]{:S(2)}, u32[]{:S(2)}) collective-permute-start(bf16[2,64,512]{2,1,0:T(8,128)(2,1)S(1)} %copy-done.21), channel_id=1, source_target_pairs={{0,1},{1,0},{2,3},{3,2},{4,5},{5,4},{6,7},{7,6},{8,9},{9,8},{10,11... | collective-permute-start | bytes 393224 | tf_op jit(solution)/shard_map/ppermute | solution.py:212
  41.1 21.6 %copy-start.8 = (bf16[2,64,512]{2,1,0:T(8,128)(2,1)}, bf16[2,64,512]{2,1,0:T(8,128)(2,1)S(1)}, u32[]{:S(2)}) copy-start(bf16[2,64,512]{2,1,0:T(8,128)(2,1)S(1)} %collective-permute-done.2.refs_2_) | copy-start | bytes 393220
  41.1 15.6 %collective-permute-start.7 = (bf16[2,64,512]{2,1,0:T(8,128)(2,1)S(1)}, bf16[2,64,512]{2,1,0:T(8,128)(2,1)S(1)}, u32[]{:S(2)}, u32[]{:S(2)}) collective-permute-start(bf16[2,64,512]{2,1,0:T(8,128)(2,1)S(1)} %copy-done.20), channel_id=1, source_target_pairs={{0,10},{1,11},{2,8},{3,9},{4,14},{5,15},{6,12},{7,13},{8,2},{9,3},... | collective-permute-start | bytes 393224 | tf_op jit(solution)/shard_map/ppermute | solution.py:212
  45.5 17.2 %collective-permute-start.8 = (bf16[2,64,512]{2,1,0:T(8,128)(2,1)S(1)}, bf16[2,64,512]{2,1,0:T(8,128)(2,1)S(1)}, u32[]{:S(2)}, u32[]{:S(2)}) collective-permute-start(bf16[2,64,512]{2,1,0:T(8,128)(2,1)S(1)} %copy-done.19), channel_id=1, source_target_pairs={{0,14},{1,15},{2,12},{3,13},{4,10},{5,11},{6,8},{7,9},{8,6},{9,7},... | collective-permute-start | bytes 393224 | tf_op jit(solution)/shard_map/ppermute | solution.py:212
  53.8 8.9 %collective-permute-start.9 = (bf16[2,64,512]{2,1,0:T(8,128)(2,1)S(1)}, bf16[2,64,512]{2,1,0:T(8,128)(2,1)S(1)}, u32[]{:S(2)}, u32[]{:S(2)}) collective-permute-start(bf16[2,64,512]{2,1,0:T(8,128)(2,1)S(1)} %copy-done.18), channel_id=1, source_target_pairs={{0,6},{1,7},{2,4},{3,5},{4,2},{5,3},{6,0},{7,1},{8,14},{9,15},{10,... | collective-permute-start | bytes 393224 | tf_op jit(solution)/shard_map/ppermute | solution.py:212
  81.9 7.0 %collective-permute-start.15 = (f32[1,64]{1,0:T(1,128)S(1)}, f32[1,64]{1,0:T(1,128)S(1)}, u32[]{:S(2)}, u32[]{:S(2)}) collective-permute-start(f32[1,64]{1,0:T(1,128)S(1)} %get-tuple-element.40), channel_id=1, source_target_pairs={{0,1},{1,2},{2,3},{3,4},{4,5},{5,6},{6,7},{7,8},{8,9},{9,10},{10,1... | collective-permute-start | bytes 776 | tf_op jit(solution)/shard_map/ppermute | solution.py:280
  86.9 5.8 %collective-permute-start.16 = (f32[1,64]{1,0:T(1,128)S(1)}, f32[1,64]{1,0:T(1,128)S(1)}, u32[]{:S(2)}, u32[]{:S(2)}) collective-permute-start(f32[1,64]{1,0:T(1,128)S(1)} %get-tuple-element.41), channel_id=1, source_target_pairs={{1,0},{2,1},{3,2},{4,3},{5,4},{6,5},{7,6},{8,7},{9,8},{10,9},{11,1... | collective-permute-start | bytes 776 | tf_op jit(solution)/shard_map/ppermute | solution.py:279
  (13 other events, 130.4 us)
where the time goes:
time: 94.4 us; the launch traced here: 94.1 us
  Pallas kernels  36.4 us (39%)
  starting transfers between devices  26.4 us (28%)
  waiting for transfers between devices  24.2 us (26%)
  local copies, waits for them, and re-layouts  3.16 us (3%)
  other arithmetic  2.92 us (3%)
  between operations  0.96 us (1%)
    ppermute x15, waiting for transfers between devices, per_device(): piece = lax.ppermute(piece, 'row', [(i, i ^ offset) for i in range(count)])  20.5 us
    ppermute x15, starting transfers between devices, per_device(): piece = lax.ppermute(piece, 'row', [(i, i ^ offset) for i in range(count)])  19.5 us
    pallas_call x1, Pallas kernels, per_device(): pl.pallas_call(functools.partial(azimuth_kernel, tuple(offsets)), grid=(s...  17.8 us
    pallas_call x1, Pallas kernels, per_device(): pl.pallas_call(spectra_kernel, out_shape=jax.ShapeDtypeStruct((RADIX, 2 *...  9.34 us
    pallas_call x1, Pallas kernels, compress(): pl.pallas_call(functools.partial(range_kernel, tuple(offsets), width, blo...  9.33 us
    ppermute x1, starting transfers between devices, per_device(): lax.ppermute(sums[tiles + 1:tiles + 2], 'row', [(i, i + 1) for i in range...  5.01 us
    ppermute x1, waiting for transfers between devices, per_device(): lax.ppermute(sums[tiles:tiles + 1], 'row', [(i, i - 1) for i in range(1,...  3.74 us
    ppermute x1, starting transfers between devices, per_device(): lax.ppermute(sums[tiles:tiles + 1], 'row', [(i, i - 1) for i in range(1,...  1.92 us
  transfers between devices with their start and end apart: 17, of which 8 were waited for; matrix products, arithmetic and copies ran while one was open for 3% of the time, Pallas kernels for 10%

commit v1 on v0

v1 whole, which is shorter than its diff:
```python
import functools

import jax
import jax.numpy as jnp
import ml_dtypes
import numpy as np
from jax import lax
from jax.experimental import pallas as pl
from jax.experimental.pallas import tpu as pltpu
from jax.sharding import PartitionSpec as P

TILE = 16
RADIX = 4
CELL = 128
F32 = jnp.float32
BF16 = jnp.bfloat16
RANGE_VMEM = 24 << 20
FOCUS_VMEM = 24 << 20


def dot(a, b):
    return jnp.dot(a, b, preferred_element_type=F32)


def dot_nt(a, b):
    return lax.dot_general(a, b, (((1,), (1,)), ((), ())), preferred_element_type=F32)


def split(x):
    high = x.astype(BF16)
    low = (x - high.astype(F32)).astype(BF16)
    return high, low


def twice(x):
    return jnp.concatenate([x, x], axis=0)


def two_terms(matrix):
    high = matrix.astype(ml_dtypes.bfloat16)
    low = (matrix - high.astype(np.float64)).astype(ml_dtypes.bfloat16)
    return np.concatenate([high, low], axis=2)


@functools.lru_cache(maxsize=None)
def phase_matrices(length):
    part = length // RADIX
    index = np.arange(part)
    k = index.reshape(part // RADIX, RADIX).T.reshape(-1)
    step = np.arange(RADIX)[:, None, None]
    phase = (k[None, :, None] * (RADIX * index[None, None, :] + step)) % length
    angle = phase * (-2.0 * np.pi / length)
    forward = two_terms(np.concatenate([np.cos(angle), np.sin(angle)], axis=1))
    phase = (index[None, :, None] * (RADIX * index[None, None, :] + step)) % length
    angle = phase * (2.0 * np.pi / length)
    inverse = two_terms(np.concatenate([np.cos(angle), np.sin(angle)], axis=1))
    return forward, inverse


def complex_product(matrix, x):
    product = dot(matrix, twice(x))
    rows, lanes = product.shape[0] // 2, product.shape[1] // 2
    real = product[:rows, :lanes] - product[rows:, lanes:]
    imag = product[:rows, lanes:] + product[rows:, :lanes]
    return real, imag


def butterfly(x, sign):
    (ar, ai), (br, bi), (cr, ci), (dr, di) = x
    pr, pi, mr, mi = ar + cr, ai + ci, ar - cr, ai - ci
    sr, si, tr, ti = br + dr, bi + di, br - dr, bi - di
    if sign < 0:
        tr, ti = ti, -tr
    else:
        tr, ti = -ti, tr
    return [(pr + sr, pi + si), (mr + tr, mi + ti), (pr - sr, pi - si), (mr - tr, mi - ti)]


def spectrum_part(values, r):
    rows = values[0][0].shape[0] // RADIX
    span = slice(r * rows, (r + 1) * rows)
    parts = butterfly([(re[span], im[span]) for re, im in values], -1)
    return [jnp.concatenate([p[c] for p in parts], axis=0) for c in range(2)]


def table_kernel(h_ref, table):
    block = table.shape[1]
    taps = h_ref.shape[1]
    replica = h_ref[...].astype(F32)
    for part in range(2):
        line = jnp.concatenate([replica[part : part + 1], jnp.zeros((1, block), F32)], axis=1)
        lines = jnp.broadcast_to(line, (block, taps + block))
        table[part] = pltpu.roll(lines, 0, 1, stride=1, stride_axis=0).astype(BF16)


def windows(x_refs, base, width, blocks, count):
    pieces = []
    for step in range(blocks):
        place = base + step
        start = pl.multiple_of(jnp.minimum(place, count - 1) * width, width)
        pieces.append([x_ref.at[:, :, pl.ds(start, width)] for x_ref in x_refs])
    return pieces


def pulse_order(total, swapped):
    row = lax.broadcasted_iota(jnp.int32, (2 * total, 2 * total), 0)
    column = lax.broadcasted_iota(jnp.int32, (2 * total, 2 * total), 1)
    quarter = total // RADIX
    pulse = RADIX * (row % quarter) + (row % total) // quarter
    source = 2 * pulse + row // total
    source = jnp.where(swapped, (source + total) % (2 * total), source)
    return (column == source).astype(F32).astype(BF16)


def correlate(window, table, width, early_out, late_out):
    block = table.shape[1]
    taps = table.shape[2] - block
    total = window.shape[0] // 2
    stacked = jnp.concatenate(
        [window[:, j * block : j * block + block + taps] for j in range(width // block)], axis=0
    )
    with_real = dot_nt(stacked, table[0])
    with_imag = dot_nt(stacked, table[1])
    placed = [0, 0]
    for cell in range(width // CELL):
        at = 2 * total * (cell * CELL // block)
        re, im = slice(at, at + total), slice(at + total, at + 2 * total)
        lanes = slice(cell * CELL % block, cell * CELL % block + CELL)
        real = with_real[re, lanes] + with_imag[im, lanes]
        imag = with_real[im, lanes] - with_imag[re, lanes]
        late = late_out is not None and cell in LATE
        out = late_out if late else early_out
        place = placed[late]
        placed[late] += 1
        out[:, 2 * CELL * place : 2 * CELL * (place + 1)] = jnp.concatenate(
            [real.astype(BF16), imag.astype(BF16)], axis=1
        )


def first_range_kernel(offsets, width, me_ref, x_hbm, h_ref, *refs):
    outs, table, x_ref, sems = refs[:-3], refs[-3], refs[-2], refs[-1]
    rows = x_hbm.shape[0]
    count = x_hbm.shape[2] // width
    blocks = x_ref.shape[0]
    me = me_ref[0]
    base = me ^ offsets[0]
    base = base - base % 2
    copies = []
    for step, (piece,) in enumerate(windows([x_hbm], base, width, blocks, count)):
        copies.append(pltpu.make_async_copy(piece, x_ref.at[step], sems.at[step]))
    for copy in copies:
        copy.start()
    table_kernel(h_ref, table)
    order = pulse_order(rows, False)
    for copy in copies:
        copy.wait()
    pieces = []
    for step in range(blocks):
        piece = x_ref[step].reshape(2 * rows, width)
        pieces.append(jnp.where(base + step < count, piece, jnp.zeros_like(piece)))
    window = dot(order, jnp.concatenate(pieces, axis=1)).astype(BF16)
    reach = window.shape[1] - width
    for offset, out in zip(offsets, outs):
        odd = (me ^ offset) % 2
        mine = jnp.where(odd == 0, window[:, :reach], window[:, width:])
        correlate(mine, table, width, out, None)


def range_kernel(offsets, late, width, me_ref, x_ref, sibling_ref, table, after_ref, *outs):
    del after_ref
    rows = x_ref.shape[0]
    taps = table.shape[2] - table.shape[1]
    count = x_ref.shape[2] // width
    me = me_ref[0]
    order = pulse_order(2 * rows, me % 2 == 1)
    outs = iter(outs)
    for offset in offsets:
        owner = me ^ offset
        pieces = []
        for step, piece in enumerate(
            windows([x_ref, sibling_ref], owner, width, 1 + -(-taps // width), count)
        ):
            piece = jnp.concatenate([part[...].reshape(2 * rows, width) for part in piece], axis=0)
            if step:
                piece = jnp.where(owner + step < count, piece, jnp.zeros_like(piece))
            pieces.append(piece)
        window = dot(order, jnp.concatenate(pieces, axis=1)).astype(BF16)
        early_out = next(outs)
        late_out = next(outs) if offset in late else None
        correlate(window, table, width, early_out, late_out)


LATE = (1, 2)


def range_cost(offsets, total, width, taps):
    return pl.CostEstimate(
        flops=len(offsets) * 16 * total * width * (taps + 256),
        bytes_accessed=len(offsets) * 4 * total * width * 3,
        transcendentals=0,
    )


def compress_first(me, echoes, replica, offsets, width):
    rows = echoes.shape[0]
    block = min(256, width)
    taps = replica.shape[1]
    blocks = 2 + -(-taps // width)
    vmem = pl.BlockSpec(memory_space=pltpu.VMEM)
    outs = pl.pallas_call(
        functools.partial(first_range_kernel, tuple(offsets), width),
        out_shape=[jax.ShapeDtypeStruct((rows, 2 * width), BF16)] * len(offsets)
        + [jax.ShapeDtypeStruct((2, block, taps + block), BF16)],
        in_specs=[pl.BlockSpec(memory_space=pltpu.SMEM), pl.BlockSpec(memory_space=pl.ANY), vmem],
        out_specs=[vmem] * (len(offsets) + 1),
        scratch_shapes=[pltpu.VMEM((blocks, rows, 2, width), BF16), pltpu.SemaphoreType.DMA((blocks,))],
        compiler_params=pltpu.CompilerParams(vmem_limit_bytes=RANGE_VMEM),
        cost_estimate=range_cost(offsets, rows, width, taps),
        name="range_compress_first",
    )(me, echoes, replica)
    return dict(zip(offsets, outs)), outs[-1]


def compress(me, echoes, sibling, table, after, offsets, late, width):
    total = 2 * echoes.shape[0]
    vmem = pl.BlockSpec(memory_space=pltpu.VMEM)
    shapes = []
    for offset in offsets:
        if offset in late:
            shapes += [(total, 2 * (width - len(LATE) * CELL)), (total, 2 * len(LATE) * CELL)]
        else:
            shapes += [(total, 2 * width)]
    outs = pl.pallas_call(
        functools.partial(range_kernel, tuple(offsets), late, width),
        out_shape=[jax.ShapeDtypeStruct(shape, BF16) for shape in shapes],
        in_specs=[pl.BlockSpec(memory_space=pltpu.SMEM), vmem, vmem, vmem, pl.BlockSpec(memory_space=pl.ANY)],
        out_specs=[vmem] * len(shapes),
        compiler_params=pltpu.CompilerParams(vmem_limit_bytes=RANGE_VMEM),
        cost_estimate=range_cost(offsets, total, width, table.shape[2] - table.shape[1]),
        name="range_compress",
    )(me, echoes, sibling, table, after)
    outs = iter(outs)
    return {offset: (next(outs), next(outs) if offset in late else None) for offset in offsets}


def column(line, select):
    return jnp.sum(jnp.where(select, line, 0.0), axis=1, keepdims=True)


def tables_kernel(
    me_ref, taps_ref, azimuth_ref, range_ref, matrix_ref, after_ref,
    spectra_ref, pulse_ref, mask_ref, inside_ref,
):
    del after_ref
    part = matrix_ref.shape[1] // 2
    length = part * RADIX
    replicas, _, tap_count = taps_ref.shape
    row = lax.broadcasted_iota(jnp.int32, (2 * CELL, 2 * replicas), 0)
    source = lax.broadcasted_iota(jnp.int32, (2 * CELL, 2 * replicas), 1)
    place = (row % CELL < replicas) & (source == 2 * (row % CELL) + row // CELL)
    taps = taps_ref[...].reshape(2 * replicas, tap_count)
    taps = dot(place.astype(F32).astype(BF16), taps).astype(BF16)
    m = lax.broadcasted_iota(jnp.int32, (part, tap_count), 0)
    tap = lax.broadcasted_iota(jnp.int32, (part, tap_count), 1)
    values = []
    for q in range(RADIX):
        pick = (tap == RADIX * m + q).astype(F32).astype(BF16)
        values.append(complex_product(matrix_ref[q], dot_nt(pick, taps).astype(BF16)))
    for r in range(RADIX):
        spectrum = jnp.concatenate(spectrum_part(values, r), axis=0) * (1.0 / length)
        high, low = split(spectrum)
        spectra_ref[r] = jnp.concatenate([high[:, :replicas], low[:, :replicas]], axis=1)

    def mask(starts, stops, first, shape):
        at = (first + lax.broadcasted_iota(jnp.int32, shape, 1)).astype(F32)
        return ((at >= starts) & (at < stops)).astype(F32).astype(BF16)

    pulse_tiles = azimuth_ref.shape[1]
    extents = azimuth_ref[...].astype(F32)
    row = lax.broadcasted_iota(jnp.int32, (pulse_tiles, pulse_tiles), 0)
    lane = lax.broadcasted_iota(jnp.int32, (pulse_tiles, pulse_tiles), 1)
    extent = column(extents, row == lane)
    start = (TILE * lax.broadcasted_iota(jnp.int32, (pulse_tiles, 1), 0)).astype(F32)
    pulse_ref[...] = mask(start - extent, start + TILE + extent, 0, pulse_ref.shape)
    start = (TILE * lax.broadcasted_iota(jnp.int32, (1, pulse_tiles), 1)).astype(F32)
    pulse_count = jnp.minimum(start + TILE + extents, 1.0 * length) - jnp.maximum(start - extents, 0.0)

    tiles = inside_ref.shape[0]
    mask_rows, width = mask_ref.shape
    total = range_ref.shape[1]
    row = lax.broadcasted_iota(jnp.int32, (mask_rows, 1), 0)
    tile = me_ref[0] * tiles + jnp.where(row == tiles, -1, jnp.where(row == tiles + 1, tiles, row))
    exists = (row < tiles + 2) & (tile >= 0) & (tile < total)
    lane = lax.broadcasted_iota(jnp.int32, (mask_rows, total), 1)
    extent = column(range_ref[...].astype(F32), lane == tile)
    start = (TILE * tile).astype(F32) - extent
    stop = (TILE * tile + TILE).astype(F32) + extent
    mask_ref[...] = mask(start, jnp.where(exists, stop, start), me_ref[0] * width, mask_ref.shape)
    count = jnp.minimum(stop, 1.0 * TILE * total) - jnp.maximum(start, 0.0)
    inside_ref[...] = count[:tiles] * pulse_count


def make_tables(me, azimuth_replicas, azimuth_extent, range_extent, matrix, after, width):
    part = matrix.shape[1] // 2
    replicas = azimuth_replicas.shape[0]
    pulse_tiles = azimuth_extent.shape[0]
    tiles = width // TILE
    mask_rows = -(-(tiles + 2) // 16) * 16
    vmem = pl.BlockSpec(memory_space=pltpu.VMEM)
    shapes = [
        ((RADIX, 2 * part, 2 * replicas), BF16),
        ((pulse_tiles, RADIX * part), BF16),
        ((mask_rows, width), BF16),
        ((tiles, pulse_tiles), F32),
    ]
    return pl.pallas_call(
        tables_kernel,
        out_shape=[jax.ShapeDtypeStruct(*shape) for shape in shapes],
        in_specs=[pl.BlockSpec(memory_space=pltpu.SMEM)] + [vmem] * 4 + [pl.BlockSpec(memory_space=pl.ANY)],
        out_specs=[vmem] * 4,
        compiler_params=pltpu.CompilerParams(vmem_limit_bytes=RANGE_VMEM),
        cost_estimate=pl.CostEstimate(flops=1 << 31, bytes_accessed=4 << 20, transcendentals=0),
        name="tables",
    )(me, azimuth_replicas, azimuth_extent[None, :], range_extent[None, :], matrix, after)


def focus_kernel(
    offsets, places, cells, first, me_ref, forward_ref, inverse_ref, spectra_ref, index_ref, pulse_ref, range_ref, *refs
):
    sources, refs = refs[: len(offsets)], refs[len(offsets) :]
    if first:
        focused_ref, sums_ref, left_ref, right_ref, x_ref, v_ref, w_ref, power_ref = refs
        tiles = sums_ref.shape[0]
    else:
        _, early_ref, from_left_ref, from_right_ref, inside_ref = refs[:5]
        focused_ref, looked_ref, x_ref, v_ref, w_ref, power_ref = refs[5:]
        tiles = looked_ref.shape[0]
    total = max(source.shape[0] for source in sources)
    length = focused_ref.shape[0]
    part = length // RADIX
    quarter = total // RADIX
    direct = x_ref.shape[0] == RADIX
    me = me_ref[0]
    step = pl.program_id(0)

    def lanes_of(values, size):
        place = values[0]
        for n in range(1, len(values)):
            place = jnp.where(step == n, values[n], place)
        return pl.ds(pl.multiple_of(place * size, size), size)

    cell = lanes_of(cells, CELL)
    for offset, source in zip(offsets, sources):
        at = lanes_of(places[offset], 2 * CELL)
        rows = source.shape[0]
        owner = (me ^ offset) // (2 * rows // total)
        rows = rows // RADIX if direct else rows
        start = pl.multiple_of(owner * rows, rows)
        if direct:
            for q in range(RADIX):
                x_ref[q, pl.ds(start, rows), :] = source[q * rows : (q + 1) * rows, at]
        else:
            x_ref[pl.ds(start, rows), :] = source[:, at]
    for q in range(RADIX):
        if direct:
            x = x_ref[q]
        else:
            m = lax.broadcasted_iota(jnp.int32, (part, length), 0)
            column = lax.broadcasted_iota(jnp.int32, (part, length), 1)
            pick = column == (m // quarter) * total + q * quarter + m % quarter
            x = dot(pick.astype(F32).astype(BF16), x_ref[...]).astype(BF16)
        v_ref[q, 0], v_ref[q, 1] = complex_product(forward_ref[q], x)
    replicas = spectra_ref.shape[2] // 2
    row = lax.broadcasted_iota(jnp.int32, (2 * replicas, CELL), 0)
    chosen = (row % replicas == index_ref[:, cell]).astype(F32).astype(BF16)
    for r in range(RADIX):
        sr, si = spectrum_part([(v_ref[q, 0], v_ref[q, 1]) for q in range(RADIX)], r)
        replica = dot(spectra_ref[r], chosen)
        gr, gi = replica[:part], replica[part:]
        y = jnp.concatenate([sr * gr + si * gi, si * gr - sr * gi], axis=1).astype(BF16)
        w_ref[r, 0], w_ref[r, 1] = complex_product(inverse_ref[r], y)
    w = [(w_ref[r, 0], w_ref[r, 1]) for r in range(RADIX)]
    for q, (re, im) in enumerate(butterfly(w, 1)):
        span = slice(q * part, (q + 1) * part)
        both = jnp.stack([re.astype(BF16), im.astype(BF16)], axis=0)
        focused_ref[span] = jnp.swapaxes(both, 0, 1)
        power_ref[span] = jnp.concatenate(split(re * re + im * im), axis=1)
    sums = dot(pulse_ref[...], power_ref[...])
    high, low = split(sums[:, :CELL] + sums[:, CELL:])
    range_mask = range_ref[:, cell]
    sums = dot_nt(
        jnp.concatenate([range_mask, range_mask], axis=1), jnp.concatenate([high, low], axis=1)
    )
    if first:

        @pl.when(step == 0)
        def _():
            sums_ref[...] = sums[:tiles]
            left_ref[...] = sums[tiles : tiles + 1]
            right_ref[...] = sums[tiles + 1 : tiles + 2]

        @pl.when(step > 0)
        def _():
            sums_ref[...] += sums[:tiles]
            left_ref[...] += sums[tiles : tiles + 1]
            right_ref[...] += sums[tiles + 1 : tiles + 2]

    else:

        @pl.when(step == 0)
        def _():
            row = lax.broadcasted_iota(jnp.int32, looked_ref.shape, 0)
            looked_ref[...] = (
                early_ref[...]
                + sums[:tiles]
                + jnp.where(row == 0, from_left_ref[...], 0.0)
                + jnp.where(row == tiles - 1, from_right_ref[...], 0.0)
            )

        @pl.when(step > 0)
        def _():
            looked_ref[...] += sums[:tiles]

        @pl.when(step == len(cells) - 1)
        def _():
            looked_ref[...] /= inside_ref[...]


def focus(first, cells, places, pulses, width, tiles, tables, sources, more):
    me, forward, inverse, spectra, index, pulse_mask, range_mask = tables
    pulse_tiles = pulse_mask.shape[0]
    part = pulses // RADIX
    offsets = list(sources)

    def cell_of(step):
        place = cells[0]
        for n in range(1, len(cells)):
            place = jnp.where(step == n, cells[n], place)
        return place

    def whole(shape):
        return pl.BlockSpec(shape, lambda i: (0,) * len(shape))

    vmem = pl.BlockSpec(memory_space=pltpu.VMEM)
    in_specs = [pl.BlockSpec(memory_space=pltpu.SMEM)] + [vmem] * (6 + len(offsets))
    focused_shape = jax.ShapeDtypeStruct((pulses, 2, width), BF16)
    focused_spec = pl.BlockSpec((pulses, 2, CELL), lambda i: (0, 0, cell_of(i)))
    looks = (tiles, pulse_tiles)
    edge = (1, pulse_tiles)
    if first:
        out_shape = [focused_shape] + [jax.ShapeDtypeStruct(s, F32) for s in (looks, edge, edge)]
        out_specs = [focused_spec, whole(looks), whole(edge), whole(edge)]
        aliases = {}
    else:
        in_specs += [pl.BlockSpec(memory_space=pl.ANY)] + [vmem] * 4
        out_shape = [focused_shape, jax.ShapeDtypeStruct(looks, F32)]
        out_specs = [focused_spec, whole(looks)]
        aliases = {7 + len(offsets): 0}
    direct = all(source.shape[0] % (16 * RADIX) == 0 for source in sources.values())
    x_shape = (RADIX, part, 2 * CELL) if direct else (pulses, 2 * CELL)
    return pl.pallas_call(
        functools.partial(focus_kernel, tuple(offsets), places, tuple(cells), first),
        grid=(len(cells),),
        out_shape=out_shape,
        in_specs=in_specs,
        out_specs=out_specs,
        scratch_shapes=[
            pltpu.VMEM(x_shape, BF16),
            pltpu.VMEM((RADIX, 2, part, CELL), F32),
            pltpu.VMEM((RADIX, 2, part, CELL), F32),
            pltpu.VMEM((pulses, 2 * CELL), BF16),
        ],
        input_output_aliases=aliases,
        compiler_params=pltpu.CompilerParams(vmem_limit_bytes=FOCUS_VMEM),
        cost_estimate=pl.CostEstimate(
            flops=len(cells) << 31, bytes_accessed=len(cells) << 21, transcendentals=0
        ),
        name="azimuth_focus",
    )(me, forward, inverse, spectra, index, pulse_mask, range_mask, *sources.values(), *more)


def per_device(
    echoes, range_replica, azimuth_replicas, replica_index, azimuth_extent, range_extent
):
    count = lax.axis_size("row")
    device = lax.axis_index("row")
    me = device.astype(jnp.int32)[None]
    rows, _, samples = echoes.shape
    pulses = rows * count
    width = samples // count
    cells = list(range(width // CELL))
    chunked = len(cells) == RADIX

    def send(piece, offset):
        if offset == 0:
            return piece
        return lax.ppermute(piece, "row", [(i, i ^ offset) for i in range(count)])

    sibling = send(echoes, 1)
    far = list(range(count // 2, count, 2))
    near = list(range(2, count // 2, 2))
    alone = [far[0], far[0] + 1] if chunked else [0]
    if chunked:
        far = far[1:]
    late = frozenset(far) if chunked else frozenset()
    half = len(far) // 2
    far = far[half:] + far[:half]
    near = near[half:] + near[:half]
    alone, table = compress_first(me, echoes, range_replica, alone, width)
    after = table
    pieces = {}
    if chunked:
        pieces = {offset: (piece, None) for offset, piece in alone.items()}
        pieces.update(compress(me, echoes, sibling, table, after, far[:1], late, width))
        after = pieces[far[0]][1]
        far = far[1:]
    rest = []
    while near or far:
        rest += far[:1] + near[:1]
        near, far = near[1:], far[1:]
    pieces.update(compress(me, echoes, sibling, table, after, rest + [0], late, width))
    received = {offset: send(piece, offset) for offset, (piece, _) in pieces.items()}
    received_late = {offset: send(pieces[offset][1], offset) for offset in pieces if offset in late}

    forward, inverse = (jnp.asarray(m) for m in phase_matrices(pulses))
    tiles = width // TILE
    spectra, pulse_mask, range_mask, inside = make_tables(
        me, azimuth_replicas, azimuth_extent, range_extent, forward, pieces[0][0], width
    )
    tables = (me, forward, inverse, spectra, replica_index[None, :], pulse_mask, range_mask)
    early = [cell for cell in cells if not (chunked and cell in LATE)]
    places = {offset: list(range(len(early))) if offset in late else early for offset in received}
    focused, sums, left, right = focus(
        True, early, places, pulses, width, tiles, tables, received, ()
    )
    from_right = lax.ppermute(left, "row", [(i, i - 1) for i in range(1, count)])
    from_left = lax.ppermute(right, "row", [(i, i + 1) for i in range(count - 1)])
    if not chunked:
        pad = jnp.zeros((tiles - 2, sums.shape[1]), F32)
        edges = jnp.concatenate([from_left, pad, from_right], axis=0)
        return focused, (sums + edges) / inside
    places = {offset: list(range(len(LATE))) if offset in late else LATE for offset in received}
    sources = {offset: received_late.get(offset, received[offset]) for offset in received}
    more = (focused, sums, from_left, from_right, inside)
    focused, looked = focus(
        False, LATE, places, pulses, width, tiles, tables, sources, more
    )
    return focused, looked


def solution(mesh):
    return jax.shard_map(
        per_device,
        mesh=mesh,
        in_specs=(
            P(("scene", "row"), None, None),
            P(),
            P(),
            P(("scene", "row")),
            P("scene"),
            P("scene"),
        ),
        out_specs=(P("scene", None, "row"), P(("scene", "row"), None)),
        check_vma=False,
    )
```

time: 94.4 us -> 67.7 us (0.72)
  Pallas kernels: 36.4 us -> 22.8 us
  waiting for transfers between devices: 24.2 us -> 14.5 us
  other arithmetic: 2.92 us -> 0 us
    pallas_call x3 -> x6, Pallas kernels: 36.4 us -> 22.8 us  [the longest x2 12.1 us: focus(): pl.pallas_call(functools.partial(focus_kernel, tuple(offsets), places, tu...]
    ppermute x17 -> x14, waiting for transfers between devices: 24.2 us -> 14.5 us  [the longest x12 10.7 us: send(): return lax.ppermute(piece, 'row', [(i, i ^ offset) for i in range(count)])]
    convert_element_type x2 -> x0, other arithmetic: 1.47 us -> none  [the longest x1 0.76 us: per_device(): ((at >= pulse_start[:, None]) & (at < pulse_stop[:, None])).astype(BF16)]
    div x1 -> x0, other arithmetic: 1.4 us -> none  [per_device(): looked = (sums[:tiles] + edges) / cells]
    unnamed x57 -> x16, local copies, waits for them, and re-layouts: 1.54 us -> 2.32 us
    ppermute x17 -> x14, starting transfers between devices: 26.4 us -> 27 us  [the longest x12 18.5 us: send(): return lax.ppermute(piece, 'row', [(i, i ^ offset) for i in range(count)])]
  transfers between devices with their start and end apart: 17 -> 14, of which waited for: 8 -> 3; matrix products, arithmetic and copies ran while one was open for 3% -> 0% of each run, Pallas kernels for 10% -> 25%
where the time goes in v1:
time: 67.7 us; the launch traced here: 67.4 us
  starting transfers between devices  27 us (40%)
  Pallas kernels  22.8 us (34%)
  waiting for transfers between devices  14.5 us (21%)
  local copies, waits for them, and re-layouts  2.32 us (3%)
  between operations  0.79 us (1%)
    ppermute x12, starting transfers between devices, send(): return lax.ppermute(piece, 'row', [(i, i ^ offset) for i in range(count)])  18.5 us
    pallas_call x2, Pallas kernels, focus(): pl.pallas_call(functools.partial(focus_kernel, tuple(offsets), places, tu...  12.1 us
    ppermute x12, waiting for transfers between devices, send(): return lax.ppermute(piece, 'row', [(i, i ^ offset) for i in range(count)])  10.7 us
    pallas_call x2, Pallas kernels, compress(): pl.pallas_call(functools.partial(range_kernel, tuple(offsets), late, widt...  7.36 us
    ppermute x1, starting transfers between devices, per_device(): lax.ppermute(right, 'row', [(i, i + 1) for i in range(count - 1)])  6.59 us
    ppermute x1, waiting for transfers between devices, per_device(): lax.ppermute(left, 'row', [(i, i - 1) for i in range(1, count)])  3.79 us
    unnamed x16, local copies, waits for them, and re-layouts  2.32 us
    ppermute x1, starting transfers between devices, per_device(): lax.ppermute(left, 'row', [(i, i - 1) for i in range(1, count)])  1.92 us
  transfers between devices with their start and end apart: 14, of which 3 were waited for; matrix products, arithmetic and copies ran while one was open for 0% of the time, Pallas kernels for 25%

profile of v1, /device:TPU:13, one launch (start us, length us, event | category | flops | bytes accessed | tf_op | source)
XLA Modules:
  0.0 67.4 jit_solution(513491635771278687)
XLA Ops:
  0.6 0.7 %collective-permute-start = (bf16[64,2,8192]{2,1,0:T(2,128)(2,1)}, bf16[64,2,8192]{2,1,0:T(2,128)(2,1)S(1)}, u32[]{:S(2)}, u32[]{:S(2)}) collective-permute-start(bf16[64,2,8192]{2,1,0:T(2,128)(2,1)} %x_ref.3), channel_id=1, source_target_pairs={{0,1},{1,0},{2,3},{3,2},{4,5},{5,4},{6,7},{7,6},{8,9},{9,8},{10,11... | collective-permute-start | bytes 6291464 | tf_op jit(solution)/shard_map/ppermute | solution.py:497
  1.4 1.6 %copy-done = bf16[64,2,8192]{2,1,0:T(2,128)(2,1)S(1)} copy-done((bf16[64,2,8192]{2,1,0:T(2,128)(2,1)S(1)}, bf16[64,2,8192]{2,1,0:T(2,128)(2,1)}, u32[]{:S(2)}) %copy-start) | copy-done | bytes 2097176
  3.0 0.7 %copy-done.2 = bf16[2,1024]{1,0:T(2,128)(2,1)S(1)} copy-done((bf16[2,1024]{1,0:T(2,128)(2,1)S(1)}, bf16[2,1024]{1,0:T(2,128)(2,1)}, u32[]{:S(2)}) %copy-start.2) | copy-done | bytes 4120
  3.6 1.5 %range_compress_first.1 = (bf16[64,1024]{1,0:T(8,128)(2,1)S(1)}, bf16[64,1024]{1,0:T(8,128)(2,1)S(1)}, bf16[2,256,1280]{2,1,0:T(8,128)(2,1)S(1)}) custom-call(s32[1]{0:T(128)} %bitcast.me_ref, bf16[64,2,8192]{2,1,0:T(2,128)(2,1)S(1)} %copy-done, bf16[2,1024]{1,0:T(2,128)(2,1)S(1)} %copy-done.2), custom_call_target="tpu_custom_call" | custom-call | flops 1342177280 | bytes 786432 | tf_op jit(solution)/shard_map/range_compress_first/pallas_call | solution.py:210
  5.1 2.4 %collective-permute-start.1 = (bf16[64,1024]{1,0:T(8,128)(2,1)S(1)}, bf16[64,1024]{1,0:T(8,128)(2,1)S(1)}, u32[]{:S(2)}, u32[]{:S(2)}) collective-permute-start(bf16[64,1024]{1,0:T(8,128)(2,1)S(1)} %get-tuple-element.29), channel_id=1, source_target_pairs={{0,8},{1,9},{2,10},{3,11},{4,12},{5,13},{6,14},{7,15},{8,0},{9,1},... | collective-permute-start | bytes 393224 | tf_op jit(solution)/shard_map/ppermute | solution.py:497
  7.5 0.2 collective-permute-start.2
  7.7 0.0 collective-permute-done.sibling_ref
  7.8 1.2 %range_compress.2 = (bf16[128,512]{1,0:T(8,128)(2,1)S(1)}, bf16[128,512]{1,0:T(8,128)(2,1)S(1)}) custom-call(s32[1]{0:T(128)} %bitcast.me_ref, bf16[64,2,8192]{2,1,0:T(2,128)(2,1)S(1)} %copy-done, bf16[64,2,8192]{2,1,0:T(2,128)(2,1)S(1)} %collective-permute-done.sibling_ref, bf16[2,256,1280]{2,1,0:T(8,128)(2,1)S(1)} %get-tuple-element.23.table.after_ref, ...), custom_call_target="tpu_custom_call" | custom-call | flops 1342177280 | bytes 786432 | tf_op jit(solution)/shard_map/range_compress/pallas_call | solution.py:233
  9.0 0.0 copy-start.1
  9.0 0.0 copy-start.3
  9.0 0.0 copy-start.5
  9.0 0.0 copy-start.6
  9.0 6.2 %range_compress.3 = (bf16[128,512]{1,0:T(8,128)(2,1)S(1)}, bf16[128,512]{1,0:T(8,128)(2,1)S(1)}, bf16[128,1024]{1,0:T(8,128)(2,1)S(1)}, bf16[128,512]{1,0:T(8,12...) custom-call(s32[1]{0:T(128)} %bitcast.me_ref, ...), custom_call_target="tpu_custom_call" | custom-call | flops 8053063680 | bytes 4718592 | tf_op jit(solution)/shard_map/range_compress/pallas_call | solution.py:233
  15.2 1.3 %collective-permute-start.10 = (bf16[128,512]{1,0:T(8,128)(2,1)S(1)}, bf16[128,512]{1,0:T(8,128)(2,1)S(1)}, u32[]{:S(2)}, u32[]{:S(2)}) collective-permute-start(bf16[128,512]{1,0:T(8,128)(2,1)S(1)} %get-tuple-element.37), channel_id=1, source_target_pairs={{0,14},{1,15},{2,12},{3,13},{4,10},{5,11},{6,8},{7,9},{8,6},{9,7},... | collective-permute-start | bytes 393224 | tf_op jit(solution)/shard_map/ppermute | solution.py:497
  16.5 2.2 %collective-permute-start.5 = (bf16[128,1024]{1,0:T(8,128)(2,1)S(1)}, bf16[128,1024]{1,0:T(8,128)(2,1)S(1)}, u32[]{:S(2)}, u32[]{:S(2)}) collective-permute-start(bf16[128,1024]{1,0:T(8,128)(2,1)S(1)} %get-tuple-element.32), channel_id=1, source_target_pairs={{0,4},{1,5},{2,6},{3,7},{4,0},{5,1},{6,2},{7,3},{8,12},{9,13},{10,... | collective-permute-start | bytes 786440 | tf_op jit(solution)/shard_map/ppermute | solution.py:497
  18.7 0.9 %collective-permute-start.7 = (bf16[128,1024]{1,0:T(8,128)(2,1)S(1)}, bf16[128,1024]{1,0:T(8,128)(2,1)S(1)}, u32[]{:S(2)}, u32[]{:S(2)}) collective-permute-start(bf16[128,1024]{1,0:T(8,128)(2,1)S(1)} %get-tuple-element.34), channel_id=1, source_target_pairs={{0,6},{1,7},{2,4},{3,5},{4,2},{5,3},{6,0},{7,1},{8,14},{9,15},{10,... | collective-permute-start | bytes 786440 | tf_op jit(solution)/shard_map/ppermute | solution.py:497
  19.6 0.3 collective-permute-start.8
  19.9 2.3 %collective-permute-start.11 = (bf16[128,512]{1,0:T(8,128)(2,1)S(1)}, bf16[128,512]{1,0:T(8,128)(2,1)S(1)}, u32[]{:S(2)}, u32[]{:S(2)}) collective-permute-start(bf16[128,512]{1,0:T(8,128)(2,1)S(1)} %get-tuple-element.38), channel_id=1, source_target_pairs={{0,10},{1,11},{2,8},{3,9},{4,14},{5,15},{6,12},{7,13},{8,2},{9,3},... | collective-permute-start | bytes 393224 | tf_op jit(solution)/shard_map/ppermute | solution.py:497
  22.2 2.6 %collective-permute-done.10.refs_3_ = bf16[128,512]{1,0:T(8,128)(2,1)S(1)} collective-permute-done((bf16[128,512]{1,0:T(8,128)(2,1)S(1)}, bf16[128,512]{1,0:T(8,128)(2,1)S(1)}, u32[]{:S(2)}, u32[]{:S(2)}) %collective-permute-start.10) | collective-permute-done | bytes 131104 | tf_op jit(solution)/shard_map/ppermute | solution.py:497
  24.8 2.1 %collective-permute-start.9 = (bf16[128,512]{1,0:T(8,128)(2,1)S(1)}, bf16[128,512]{1,0:T(8,128)(2,1)S(1)}, u32[]{:S(2)}, u32[]{:S(2)}) collective-permute-start(bf16[128,512]{1,0:T(8,128)(2,1)S(1)} %get-tuple-element.36), channel_id=1, source_target_pairs={{0,12},{1,13},{2,14},{3,15},{4,8},{5,9},{6,10},{7,11},{8,4},{9,5},... | collective-permute-start | bytes 393224 | tf_op jit(solution)/shard_map/ppermute | solution.py:497
  26.9 0.0 copy-start.4
  26.9 0.0 copy-start.7
  27.0 1.9 %tables.1 = (bf16[4,512,32]{2,1,0:T(8,128)(2,1)S(1)}, bf16[64,1024]{1,0:T(8,128)(2,1)S(1)}, bf16[48,512]{1,0:T(8,128)(2,1)S(1)}, f32[32,64]{1,0:T(8,128)S(1)}) custom-call(s32[1]{0:T(128)} %bitcast.me_ref, bf16[16,2,512]{2,1,0:T(2,128)(2,1)S(1)} %copy-done.1, s32[1,64]{1,0:T(1,128)S(1)} %bitcast.7, s32[1,512]{1,0:T(1,128)S(1)} %bitcast.4, ...), custom_call_target="tpu_custom_call" | custom-call | flops 2147483648 | bytes 4194304 | tf_op jit(solution)/shard_map/tables/pallas_call | solution.py:316
  28.9 8.1 %collective-permute-done.11.refs_5_ = bf16[128,512]{1,0:T(8,128)(2,1)S(1)} collective-permute-done((bf16[128,512]{1,0:T(8,128)(2,1)S(1)}, bf16[128,512]{1,0:T(8,128)(2,1)S(1)}, u32[]{:S(2)}, u32[]{:S(2)}) %collective-permute-start.11) | collective-permute-done | bytes 131104 | tf_op jit(solution)/shard_map/ppermute | solution.py:497
  36.9 1.5 %collective-permute-start.3 = (bf16[128,512]{1,0:T(8,128)(2,1)S(1)}, bf16[128,512]{1,0:T(8,128)(2,1)S(1)}, u32[]{:S(2)}, u32[]{:S(2)}) collective-permute-start(bf16[128,512]{1,0:T(8,128)(2,1)S(1)} %get-tuple-element.24.after_ref), channel_id=1, source_target_pairs={{0,12},{1,13},{2,14},{3,15},{4,8},{5,9},{6,10},{7,11},{8,4},{9,5},... | collective-permute-start | bytes 393224 | tf_op jit(solution)/shard_map/ppermute | solution.py:497
  38.4 0.0 collective-permute-start.4
  38.5 4.5 %collective-permute-start.6 = (bf16[128,512]{1,0:T(8,128)(2,1)S(1)}, bf16[128,512]{1,0:T(8,128)(2,1)S(1)}, u32[]{:S(2)}, u32[]{:S(2)}) collective-permute-start(bf16[128,512]{1,0:T(8,128)(2,1)S(1)} %get-tuple-element.33), channel_id=1, source_target_pairs={{0,10},{1,11},{2,8},{3,9},{4,14},{5,15},{6,12},{7,13},{8,2},{9,3},... | collective-permute-start | bytes 393224 | tf_op jit(solution)/shard_map/ppermute | solution.py:497
  43.0 6.1 %azimuth_focus.2 = (bf16[1024,2,512]{2,1,0:T(2,128)(2,1)}, f32[32,64]{1,0:T(8,128)S(1)}, f32[1,64]{1,0:T(1,128)S(1)}, f32[1,64]{1,0:T(1,128)S(1)}) custom-call(s32[1]{0:T(128)} %bitcast.me_ref, bf16[4,512,512]{2,1,0:T(8,128)(2,1)S(1)} %copy-done.6, bf16[4,512,512]{2,1,0:T(8,128)(2,1)S(1)} %copy-done.7, ...), custom_call_target="tpu_custom_call" | custom-call | flops 4294967296 | bytes 4194304 | tf_op jit(solution)/shard_map/azimuth_focus/pallas_call | solution.py:461
  49.0 6.6 %collective-permute-start.12 = (f32[1,64]{1,0:T(1,128)S(1)}, f32[1,64]{1,0:T(1,128)S(1)}, u32[]{:S(2)}, u32[]{:S(2)}) collective-permute-start(f32[1,64]{1,0:T(1,128)S(1)} %get-tuple-element.41), channel_id=1, source_target_pairs={{0,1},{1,2},{2,3},{3,4},{4,5},{5,6},{6,7},{7,8},{8,9},{9,10},{10,1... | collective-permute-start | bytes 776 | tf_op jit(solution)/shard_map/ppermute | solution.py:537
  55.6 1.9 %collective-permute-start.13 = (f32[1,64]{1,0:T(1,128)S(1)}, f32[1,64]{1,0:T(1,128)S(1)}, u32[]{:S(2)}, u32[]{:S(2)}) collective-permute-start(f32[1,64]{1,0:T(1,128)S(1)} %get-tuple-element.42), channel_id=1, source_target_pairs={{1,0},{2,1},{3,2},{4,3},{5,4},{6,5},{7,6},{8,7},{9,8},{10,9},{11,1... | collective-permute-start | bytes 776 | tf_op jit(solution)/shard_map/ppermute | solution.py:536
  57.6 3.8 %collective-permute-done.13.refs_12_ = f32[1,64]{1,0:T(1,128)S(1)} collective-permute-done((f32[1,64]{1,0:T(1,128)S(1)}, f32[1,64]{1,0:T(1,128)S(1)}, u32[]{:S(2)}, u32[]{:S(2)}) %collective-permute-start.13) | collective-permute-done | bytes 288 | tf_op jit(solution)/shard_map/ppermute | solution.py:536
  61.4 6.0 %azimuth_focus.3 = (bf16[1024,2,512]{2,1,0:T(2,128)(2,1)}, f32[32,64]{1,0:T(8,128)}) custom-call(s32[1]{0:T(128)} %bitcast.me_ref, bf16[4,512,512]{2,1,0:T(8,128)(2,1)S(1)} %copy-done.6, bf16[4,512,512]{2,1,0:T(8,128)(2,1)S(1)} %copy-done.7, bf16[4,512,32]{2,1,0:T(8,128)(2,1)S(1)} %get-tuple-element.26.spectra_ref, ...), custom_call_target="tpu_custom_call", output_to_operand_aliasing={{0}: (16, {})} | custom-call | flops 4294967296 | bytes 4194304 | tf_op jit(solution)/shard_map/azimuth_focus/pallas_call | solution.py:461
  (18 shorter events, 0.0 us)
Async XLA Ops:
  0.6 7.1 %collective-permute-start = (bf16[64,2,8192]{2,1,0:T(2,128)(2,1)}, bf16[64,2,8192]{2,1,0:T(2,128)(2,1)S(1)}, u32[]{:S(2)}, u32[]{:S(2)}) collective-permute-start(bf16[64,2,8192]{2,1,0:T(2,128)(2,1)} %x_ref.3), channel_id=1, source_target_pairs={{0,1},{1,0},{2,3},{3,2},{4,5},{5,4},{6,7},{7,6},{8,9},{9,8},{10,11... | collective-permute-start | bytes 6291464 | tf_op jit(solution)/shard_map/ppermute | solution.py:497
  1.4 1.6 %copy-start = (bf16[64,2,8192]{2,1,0:T(2,128)(2,1)S(1)}, bf16[64,2,8192]{2,1,0:T(2,128)(2,1)}, u32[]{:S(2)}) copy-start(bf16[64,2,8192]{2,1,0:T(2,128)(2,1)} %x_ref.3) | copy-start | bytes 6291460
  3.0 0.7 %copy-start.2 = (bf16[2,1024]{1,0:T(2,128)(2,1)S(1)}, bf16[2,1024]{1,0:T(2,128)(2,1)}, u32[]{:S(2)}) copy-start(bf16[2,1024]{1,0:T(2,128)(2,1)} %h_ref.1) | copy-start | bytes 12292
  5.1 14.5 %collective-permute-start.1 = (bf16[64,1024]{1,0:T(8,128)(2,1)S(1)}, bf16[64,1024]{1,0:T(8,128)(2,1)S(1)}, u32[]{:S(2)}, u32[]{:S(2)}) collective-permute-start(bf16[64,1024]{1,0:T(8,128)(2,1)S(1)} %get-tuple-element.29), channel_id=1, source_target_pairs={{0,8},{1,9},{2,10},{3,11},{4,12},{5,13},{6,14},{7,15},{8,0},{9,1},... | collective-permute-start | bytes 393224 | tf_op jit(solution)/shard_map/ppermute | solution.py:497
  7.5 12.4 %collective-permute-start.2 = (bf16[64,1024]{1,0:T(8,128)(2,1)S(1)}, bf16[64,1024]{1,0:T(8,128)(2,1)S(1)}, u32[]{:S(2)}, u32[]{:S(2)}) collective-permute-start(bf16[64,1024]{1,0:T(8,128)(2,1)S(1)} %get-tuple-element.30), channel_id=1, source_target_pairs={{0,9},{1,8},{2,11},{3,10},{4,13},{5,12},{6,15},{7,14},{8,1},{9,0},... | collective-permute-start | bytes 393224 | tf_op jit(solution)/shard_map/ppermute | solution.py:497
  9.0 18.0 %copy-start.1 = (bf16[16,2,512]{2,1,0:T(2,128)(2,1)S(1)}, bf16[16,2,512]{2,1,0:T(2,128)(2,1)}, u32[]{:S(2)}) copy-start(bf16[16,2,512]{2,1,0:T(2,128)(2,1)} %taps_ref.1) | copy-start | bytes 98308
  9.0 17.9 %copy-start.3 = (s32[512]{0:T(512)S(1)}, s32[512]{0:T(512)}, u32[]{:S(2)}) copy-start(s32[512]{0:T(512)} %param.13) | copy-start | bytes 6148
  9.0 17.9 %copy-start.5 = (s32[64]{0:T(128)S(1)}, s32[64]{0:T(128)}, u32[]{:S(2)}) copy-start(s32[64]{0:T(128)} %param.12) | copy-start | bytes 772
  9.0 17.9 %copy-start.6 = (bf16[4,512,512]{2,1,0:T(8,128)(2,1)S(1)}, bf16[4,512,512]{2,1,0:T(8,128)(2,1)}, u32[]{:S(2)}) copy-start(bf16[4,512,512]{2,1,0:T(8,128)(2,1)} %constant.8.clone.matrix_ref.forward_ref) | copy-start | bytes 6291460
  15.2 9.6 %collective-permute-start.10 = (bf16[128,512]{1,0:T(8,128)(2,1)S(1)}, bf16[128,512]{1,0:T(8,128)(2,1)S(1)}, u32[]{:S(2)}, u32[]{:S(2)}) collective-permute-start(bf16[128,512]{1,0:T(8,128)(2,1)S(1)} %get-tuple-element.37), channel_id=1, source_target_pairs={{0,14},{1,15},{2,12},{3,13},{4,10},{5,11},{6,8},{7,9},{8,6},{9,7},... | collective-permute-start | bytes 393224 | tf_op jit(solution)/shard_map/ppermute | solution.py:497
  16.5 22.0 %collective-permute-start.5 = (bf16[128,1024]{1,0:T(8,128)(2,1)S(1)}, bf16[128,1024]{1,0:T(8,128)(2,1)S(1)}, u32[]{:S(2)}, u32[]{:S(2)}) collective-permute-start(bf16[128,1024]{1,0:T(8,128)(2,1)S(1)} %get-tuple-element.32), channel_id=1, source_target_pairs={{0,4},{1,5},{2,6},{3,7},{4,0},{5,1},{6,2},{7,3},{8,12},{9,13},{10,... | collective-permute-start | bytes 786440 | tf_op jit(solution)/shard_map/ppermute | solution.py:497
  18.7 24.3 %collective-permute-start.7 = (bf16[128,1024]{1,0:T(8,128)(2,1)S(1)}, bf16[128,1024]{1,0:T(8,128)(2,1)S(1)}, u32[]{:S(2)}, u32[]{:S(2)}) collective-permute-start(bf16[128,1024]{1,0:T(8,128)(2,1)S(1)} %get-tuple-element.34), channel_id=1, source_target_pairs={{0,6},{1,7},{2,4},{3,5},{4,2},{5,3},{6,0},{7,1},{8,14},{9,15},{10,... | collective-permute-start | bytes 786440 | tf_op jit(solution)/shard_map/ppermute | solution.py:497
  19.6 23.3 %collective-permute-start.8 = (bf16[128,1024]{1,0:T(8,128)(2,1)S(1)}, bf16[128,1024]{1,0:T(8,128)(2,1)S(1)}, u32[]{:S(2)}, u32[]{:S(2)}) collective-permute-start(bf16[128,1024]{1,0:T(8,128)(2,1)S(1)} %get-tuple-element.35), channel_id=1, source_target_pairs={{0,2},{1,3},{2,0},{3,1},{4,6},{5,7},{6,4},{7,5},{8,10},{9,11},{10,... | collective-permute-start | bytes 786440 | tf_op jit(solution)/shard_map/ppermute | solution.py:497
  19.9 17.0 %collective-permute-start.11 = (bf16[128,512]{1,0:T(8,128)(2,1)S(1)}, bf16[128,512]{1,0:T(8,128)(2,1)S(1)}, u32[]{:S(2)}, u32[]{:S(2)}) collective-permute-start(bf16[128,512]{1,0:T(8,128)(2,1)S(1)} %get-tuple-element.38), channel_id=1, source_target_pairs={{0,10},{1,11},{2,8},{3,9},{4,14},{5,15},{6,12},{7,13},{8,2},{9,3},... | collective-permute-start | bytes 393224 | tf_op jit(solution)/shard_map/ppermute | solution.py:497
  24.8 13.6 %collective-permute-start.9 = (bf16[128,512]{1,0:T(8,128)(2,1)S(1)}, bf16[128,512]{1,0:T(8,128)(2,1)S(1)}, u32[]{:S(2)}, u32[]{:S(2)}) collective-permute-start(bf16[128,512]{1,0:T(8,128)(2,1)S(1)} %get-tuple-element.36), channel_id=1, source_target_pairs={{0,12},{1,13},{2,14},{3,15},{4,8},{5,9},{6,10},{7,11},{8,4},{9,5},... | collective-permute-start | bytes 393224 | tf_op jit(solution)/shard_map/ppermute | solution.py:497
  26.9 16.0 %copy-start.4 = (s32[512]{0:T(512)S(1)}, s32[512]{0:T(512)}, u32[]{:S(2)}) copy-start(s32[512]{0:T(512)} %param.11) | copy-start | bytes 6148
  26.9 16.0 %copy-start.7 = (bf16[4,512,512]{2,1,0:T(8,128)(2,1)S(1)}, bf16[4,512,512]{2,1,0:T(8,128)(2,1)}, u32[]{:S(2)}) copy-start(bf16[4,512,512]{2,1,0:T(8,128)(2,1)} %constant.9.clone.inverse_ref) | copy-start | bytes 6291460
  36.9 20.7 %collective-permute-start.3 = (bf16[128,512]{1,0:T(8,128)(2,1)S(1)}, bf16[128,512]{1,0:T(8,128)(2,1)S(1)}, u32[]{:S(2)}, u32[]{:S(2)}) collective-permute-start(bf16[128,512]{1,0:T(8,128)(2,1)S(1)} %get-tuple-element.24.after_ref), channel_id=1, source_target_pairs={{0,12},{1,13},{2,14},{3,15},{4,8},{5,9},{6,10},{7,11},{8,4},{9,5},... | collective-permute-start | bytes 393224 | tf_op jit(solution)/shard_map/ppermute | solution.py:497
  38.4 19.2 %collective-permute-start.4 = (bf16[128,512]{1,0:T(8,128)(2,1)S(1)}, bf16[128,512]{1,0:T(8,128)(2,1)S(1)}, u32[]{:S(2)}, u32[]{:S(2)}) collective-permute-start(bf16[128,512]{1,0:T(8,128)(2,1)S(1)} %get-tuple-element.31), channel_id=1, source_target_pairs={{0,14},{1,15},{2,12},{3,13},{4,10},{5,11},{6,8},{7,9},{8,6},{9,7},... | collective-permute-start | bytes 393224 | tf_op jit(solution)/shard_map/ppermute | solution.py:497
  38.5 19.1 %collective-permute-start.6 = (bf16[128,512]{1,0:T(8,128)(2,1)S(1)}, bf16[128,512]{1,0:T(8,128)(2,1)S(1)}, u32[]{:S(2)}, u32[]{:S(2)}) collective-permute-start(bf16[128,512]{1,0:T(8,128)(2,1)S(1)} %get-tuple-element.33), channel_id=1, source_target_pairs={{0,10},{1,11},{2,8},{3,9},{4,14},{5,15},{6,12},{7,13},{8,2},{9,3},... | collective-permute-start | bytes 393224 | tf_op jit(solution)/shard_map/ppermute | solution.py:497
  49.0 8.6 %collective-permute-start.12 = (f32[1,64]{1,0:T(1,128)S(1)}, f32[1,64]{1,0:T(1,128)S(1)}, u32[]{:S(2)}, u32[]{:S(2)}) collective-permute-start(f32[1,64]{1,0:T(1,128)S(1)} %get-tuple-element.41), channel_id=1, source_target_pairs={{0,1},{1,2},{2,3},{3,4},{4,5},{5,6},{6,7},{7,8},{8,9},{9,10},{10,1... | collective-permute-start | bytes 776 | tf_op jit(solution)/shard_map/ppermute | solution.py:537
  55.6 5.8 %collective-permute-start.13 = (f32[1,64]{1,0:T(1,128)S(1)}, f32[1,64]{1,0:T(1,128)S(1)}, u32[]{:S(2)}, u32[]{:S(2)}) collective-permute-start(f32[1,64]{1,0:T(1,128)S(1)} %get-tuple-element.42), channel_id=1, source_target_pairs={{1,0},{2,1},{3,2},{4,3},{5,4},{6,5},{7,6},{8,7},{9,8},{10,9},{11,1... | collective-permute-start | bytes 776 | tf_op jit(solution)/shard_map/ppermute | solution.py:536

commit v2 on v1

--- a/solution.py
+++ b/solution.py
@@ -14,8 +14,11 @@
 CELL = 128
 F32 = jnp.float32
 BF16 = jnp.bfloat16
+FIRST_VMEM = 24 << 20
 RANGE_VMEM = 24 << 20
+GATE_VMEM = 1 << 20
 FOCUS_VMEM = 24 << 20
+SMALL_COST = pl.CostEstimate(flops=1 << 20, bytes_accessed=1 << 16, transcendentals=0)
 
 
 def dot(a, b):
@@ -49,11 +52,10 @@
     k = index.reshape(part // RADIX, RADIX).T.reshape(-1)
     step = np.arange(RADIX)[:, None, None]
     phase = (k[None, :, None] * (RADIX * index[None, None, :] + step)) % length
-    angle = phase * (-2.0 * np.pi / length)
-    forward = two_terms(np.concatenate([np.cos(angle), np.sin(angle)], axis=1))
-    phase = (index[None, :, None] * (RADIX * index[None, None, :] + step)) % length
     angle = phase * (2.0 * np.pi / length)
-    inverse = two_terms(np.concatenate([np.cos(angle), np.sin(angle)], axis=1))
+    cos, sin = np.cos(angle), np.sin(angle)
+    forward = two_terms(np.concatenate([cos, -sin], axis=1))
+    inverse = two_terms(np.concatenate([cos, sin], axis=2).reshape(RADIX, part, 2, part).transpose(0, 2, 3, 1).reshape(RADIX, 2 * part, part))
     return forward, inverse
 
 
@@ -85,11 +87,8 @@
 
 def table_kernel(h_ref, table):
     block = table.shape[1]
-    taps = h_ref.shape[1]
-    replica = h_ref[...].astype(F32)
     for part in range(2):
-        line = jnp.concatenate([replica[part : part + 1], jnp.zeros((1, block), F32)], axis=1)
-        lines = jnp.broadcast_to(line, (block, taps + block))
+        lines = jnp.broadcast_to(h_ref[part : part + 1], (block, h_ref.shape[1]))
         table[part] = pltpu.roll(lines, 0, 1, stride=1, stride_axis=0).astype(BF16)
 
 
@@ -138,7 +137,7 @@
 
 
 def first_range_kernel(offsets, width, me_ref, x_hbm, h_ref, *refs):
-    outs, table, x_ref, sems = refs[:-3], refs[-3], refs[-2], refs[-1]
+    outs, (table, x_ref, sems) = refs[:-3], refs[-3:]
     rows = x_hbm.shape[0]
     count = x_hbm.shape[2] // width
     blocks = x_ref.shape[0]
@@ -166,8 +165,10 @@
         correlate(mine, table, width, out, None)
 
 
-def range_kernel(offsets, late, width, me_ref, x_ref, sibling_ref, table, after_ref, *outs):
+def range_kernel(offsets, late, width, me_ref, x_ref, sibling_ref, h_ref, after_ref, *refs):
     del after_ref
+    outs, table = refs[:-1], refs[-1]
+    table_kernel(h_ref, table)
     rows = x_ref.shape[0]
     taps = table.shape[2] - table.shape[1]
     count = x_ref.shape[2] // width
@@ -193,36 +194,37 @@
 LATE = (1, 2)
 
 
-def range_cost(offsets, total, width, taps):
-    return pl.CostEstimate(
-        flops=len(offsets) * 16 * total * width * (taps + 256),
-        bytes_accessed=len(offsets) * 4 * total * width * 3,
-        transcendentals=0,
-    )
-
-
 def compress_first(me, echoes, replica, offsets, width):
     rows = echoes.shape[0]
     block = min(256, width)
-    taps = replica.shape[1]
+    taps = replica.shape[1] - block
     blocks = 2 + -(-taps // width)
     vmem = pl.BlockSpec(memory_space=pltpu.VMEM)
     outs = pl.pallas_call(
         functools.partial(first_range_kernel, tuple(offsets), width),
-        out_shape=[jax.ShapeDtypeStruct((rows, 2 * width), BF16)] * len(offsets)
-        + [jax.ShapeDtypeStruct((2, block, taps + block), BF16)],
+        out_shape=[jax.ShapeDtypeStruct((rows, 2 * width), BF16)] * len(offsets),
         in_specs=[pl.BlockSpec(memory_space=pltpu.SMEM), pl.BlockSpec(memory_space=pl.ANY), vmem],
-        out_specs=[vmem] * (len(offsets) + 1),
-        scratch_shapes=[pltpu.VMEM((blocks, rows, 2, width), BF16), pltpu.SemaphoreType.DMA((blocks,))],
-        compiler_params=pltpu.CompilerParams(vmem_limit_bytes=RANGE_VMEM),
-        cost_estimate=range_cost(offsets, rows, width, taps),
+        out_specs=[vmem] * len(offsets),
+        scratch_shapes=[
+            pltpu.VMEM((2, block, taps + block), BF16),
+            pltpu.VMEM((blocks, rows, 2, width), BF16),
+            pltpu.SemaphoreType.DMA((blocks,)),
+        ],
+        compiler_params=pltpu.CompilerParams(vmem_limit_bytes=FIRST_VMEM),
+        cost_estimate=pl.CostEstimate(
+            flops=len(offsets) * 16 * rows * width * (taps + 256),
+            bytes_accessed=len(offsets) * 4 * rows * width * 3,
+            transcendentals=0,
+        ),
         name="range_compress_first",
     )(me, echoes, replica)
-    return dict(zip(offsets, outs)), outs[-1]
-
-
-def compress(me, echoes, sibling, table, after, offsets, late, width):
+    return dict(zip(offsets, outs))
+
+
+def compress(me, echoes, sibling, replica, after, offsets, late, width):
     total = 2 * echoes.shape[0]
+    block = min(256, width)
+    taps = replica.shape[1] - block
     vmem = pl.BlockSpec(memory_space=pltpu.VMEM)
     shapes = []
     for offset in offsets:
@@ -235,12 +237,35 @@
         out_shape=[jax.ShapeDtypeStruct(shape, BF16) for shape in shapes],
         in_specs=[pl.BlockSpec(memory_space=pltpu.SMEM), vmem, vmem, vmem, pl.BlockSpec(memory_space=pl.ANY)],
         out_specs=[vmem] * len(shapes),
+        scratch_shapes=[pltpu.VMEM((2, block, taps + block), BF16)],
         compiler_params=pltpu.CompilerParams(vmem_limit_bytes=RANGE_VMEM),
-        cost_estimate=range_cost(offsets, total, width, table.shape[2] - table.shape[1]),
+        cost_estimate=pl.CostEstimate(
+            flops=len(offsets) * 16 * total * width * (taps + block),
+            bytes_accessed=len(offsets) * 4 * total * width * 3,
+            transcendentals=0,
+        ),
         name="range_compress",
-    )(me, echoes, sibling, table, after)
+    )(me, echoes, sibling, replica, after)
     outs = iter(outs)
     return {offset: (next(outs), next(outs) if offset in late else None) for offset in offsets}
+
+
+def gate_kernel(*refs):
+    del refs
+
+
+def gate(pieces, after):
+    anywhere = pl.BlockSpec(memory_space=pl.ANY)
+    return pl.pallas_call(
+        gate_kernel,
+        out_shape=[jax.ShapeDtypeStruct(piece.shape, piece.dtype) for piece in pieces],
+        in_specs=[anywhere] * (len(pieces) + len(after)),
+        out_specs=[anywhere] * len(pieces),
+        input_output_aliases={n: n for n in range(len(pieces))},
+        compiler_params=pltpu.CompilerParams(vmem_limit_bytes=GATE_VMEM),
+        cost_estimate=SMALL_COST,
+        name="gate",
+    )(*pieces, *after)
 
 
 def column(line, select):
@@ -271,8 +296,8 @@
         high, low = split(spectrum)
         spectra_ref[r] = jnp.concatenate([high[:, :replicas], low[:, :replicas]], axis=1)
 
-    def mask(starts, stops, first, shape):
-        at = (first + lax.broadcasted_iota(jnp.int32, shape, 1)).astype(F32)
+    def mask(starts, stops, at):
+        at = at.astype(F32)
         return ((at >= starts) & (at < stops)).astype(F32).astype(BF16)
 
     pulse_tiles = azimuth_ref.shape[1]
@@ -281,7 +306,8 @@
     lane = lax.broadcasted_iota(jnp.int32, (pulse_tiles, pulse_tiles), 1)
     extent = column(extents, row == lane)
     start = (TILE * lax.broadcasted_iota(jnp.int32, (pulse_tiles, 1), 0)).astype(F32)
-    pulse_ref[...] = mask(start - extent, start + TILE + extent, 0, pulse_ref.shape)
+    lane = lax.broadcasted_iota(jnp.int32, pulse_ref.shape, 1)
+    pulse_ref[...] = mask(start - extent, start + TILE + extent, RADIX * (lane % part) + lane // part)
     start = (TILE * lax.broadcasted_iota(jnp.int32, (1, pulse_tiles), 1)).astype(F32)
     pulse_count = jnp.minimum(start + TILE + extents, 1.0 * length) - jnp.maximum(start - extents, 0.0)
 
@@ -295,7 +321,8 @@
     extent = column(range_ref[...].astype(F32), lane == tile)
     start = (TILE * tile).astype(F32) - extent
     stop = (TILE * tile + TILE).astype(F32) + extent
-    mask_ref[...] = mask(start, jnp.where(exists, stop, start), me_ref[0] * width, mask_ref.shape)
+    lane = lax.broadcasted_iota(jnp.int32, mask_ref.shape, 1)
+    mask_ref[...] = mask(start, jnp.where(exists, stop, start), me_ref[0] * width + lane)
     count = jnp.minimum(stop, 1.0 * TILE * total) - jnp.maximum(start, 0.0)
     inside_ref[...] = count[:tiles] * pulse_count
 
@@ -324,106 +351,114 @@
     )(me, azimuth_replicas, azimuth_extent[None, :], range_extent[None, :], matrix, after)
 
 
-def focus_kernel(
-    offsets, places, cells, first, me_ref, forward_ref, inverse_ref, spectra_ref, index_ref, pulse_ref, range_ref, *refs
-):
-    sources, refs = refs[: len(offsets)], refs[len(offsets) :]
-    if first:
-        focused_ref, sums_ref, left_ref, right_ref, x_ref, v_ref, w_ref, power_ref = refs
-        tiles = sums_ref.shape[0]
-    else:
-        _, early_ref, from_left_ref, from_right_ref, inside_ref = refs[:5]
-        focused_ref, looked_ref, x_ref, v_ref, w_ref, power_ref = refs[5:]
-        tiles = looked_ref.shape[0]
-    total = max(source.shape[0] for source in sources)
-    length = focused_ref.shape[0]
-    part = length // RADIX
-    quarter = total // RADIX
+def gather_pulses(offsets, places, n, sources, me, total, x_ref):
     direct = x_ref.shape[0] == RADIX
-    me = me_ref[0]
-    step = pl.program_id(0)
-
-    def lanes_of(values, size):
-        place = values[0]
-        for n in range(1, len(values)):
-            place = jnp.where(step == n, values[n], place)
-        return pl.ds(pl.multiple_of(place * size, size), size)
-
-    cell = lanes_of(cells, CELL)
     for offset, source in zip(offsets, sources):
-        at = lanes_of(places[offset], 2 * CELL)
+        at = slice(2 * CELL * places[offset][n], 2 * CELL * (places[offset][n] + 1))
         rows = source.shape[0]
         owner = (me ^ offset) // (2 * rows // total)
         rows = rows // RADIX if direct else rows
         start = pl.multiple_of(owner * rows, rows)
         if direct:
             for q in range(RADIX):
-                x_ref[q, pl.ds(start, rows), :] = source[q * rows : (q + 1) * rows, at]
+                span = slice(q * rows, (q + 1) * rows)
+                x_ref[q, pl.ds(start, rows), :] = source[span, at]
         else:
             x_ref[pl.ds(start, rows), :] = source[:, at]
-    for q in range(RADIX):
-        if direct:
-            x = x_ref[q]
-        else:
-            m = lax.broadcasted_iota(jnp.int32, (part, length), 0)
-            column = lax.broadcasted_iota(jnp.int32, (part, length), 1)
-            pick = column == (m // quarter) * total + q * quarter + m % quarter
-            x = dot(pick.astype(F32).astype(BF16), x_ref[...]).astype(BF16)
-        v_ref[q, 0], v_ref[q, 1] = complex_product(forward_ref[q], x)
+
+
+def pulses_of(x_ref, q, total, part):
+    if x_ref.shape[0] == RADIX:
+        return x_ref[q]
+    quarter = total // RADIX
+    m = lax.broadcasted_iota(jnp.int32, (part, x_ref.shape[0]), 0)
+    row = lax.broadcasted_iota(jnp.int32, (part, x_ref.shape[0]), 1)
+    pick = row == (m // quarter) * total + q * quarter + m % quarter
+    return dot(pick.astype(F32).astype(BF16), x_ref[...]).astype(BF16)
+
+
+def focus_kernel(
+    offsets, places, cells, first, me_ref, forward_ref, inverse_ref, spectra_ref, index_ref, pulse_ref, range_ref, *refs
+):
+    sources, refs = refs[: len(offsets)], refs[len(offsets) :]
+    if first:
+        focused_hbm, sums_ref, left_ref, right_ref = refs[:4]
+        tiles = sums_ref.shape[0]
+    else:
+        _, early_ref, from_left_ref, from_right_ref, inside_ref, focused_hbm, looked_ref = refs[:7]
+        tiles = looked_ref.shape[0]
+    x_ref, v_ref, s_ref, power_ref, image_ref, sems = refs[-6:]
+    total = max(source.shape[0] for source in sources)
+    part = v_ref.shape[3]
+    me = me_ref[0]
+    steps = range(len(cells))
+    for n in steps:
+        gather_pulses(offsets, places, n, sources, me, total, x_ref.at[n])
     replicas = spectra_ref.shape[2] // 2
     row = lax.broadcasted_iota(jnp.int32, (2 * replicas, CELL), 0)
-    chosen = (row % replicas == index_ref[:, cell]).astype(F32).astype(BF16)
-    for r in range(RADIX):
-        sr, si = spectrum_part([(v_ref[q, 0], v_ref[q, 1]) for q in range(RADIX)], r)
-        replica = dot(spectra_ref[r], chosen)
-        gr, gi = replica[:part], replica[part:]
-        y = jnp.concatenate([sr * gr + si * gi, si * gr - sr * gi], axis=1).astype(BF16)
-        w_ref[r, 0], w_ref[r, 1] = complex_product(inverse_ref[r], y)
-    w = [(w_ref[r, 0], w_ref[r, 1]) for r in range(RADIX)]
-    for q, (re, im) in enumerate(butterfly(w, 1)):
-        span = slice(q * part, (q + 1) * part)
-        both = jnp.stack([re.astype(BF16), im.astype(BF16)], axis=0)
-        focused_ref[span] = jnp.swapaxes(both, 0, 1)
-        power_ref[span] = jnp.concatenate(split(re * re + im * im), axis=1)
+
+    def transform(n):
+        for q in range(RADIX):
+            x = pulses_of(x_ref.at[n], q, total, part)
+            v_ref[n, q, 0], v_ref[n, q, 1] = complex_product(forward_ref[q], x)
+
+    def correlate_cell(n):
+        lanes = slice(cells[n] * CELL, (cells[n] + 1) * CELL)
+        chosen = (row % replicas == index_ref[:, lanes]).astype(F32).astype(BF16)
+        rows = part // RADIX
+        for r in range(RADIX):
+            span = slice(r * rows, (r + 1) * rows)
+            x = butterfly([(v_ref[n, q, 0, span], v_ref[n, q, 1, span]) for q in range(RADIX)], -1)
+            replica = dot(spectra_ref[r], chosen)
+            y = []
+            for j, (sr, si) in enumerate(x):
+                gr = replica[j * rows : (j + 1) * rows]
+                gi = replica[part + j * rows : part + (j + 1) * rows]
+                y.append((sr * gr + si * gi, si * gr - sr * gi))
+            for q, (re, im) in enumerate(butterfly(y, 1)):
+                s_ref[n, q, span, :CELL] = re.astype(BF16)
+                s_ref[n, q, span, CELL:] = im.astype(BF16)
+
+    copies = []
+
+    def finish(n):
+        lanes = slice(cells[n] * CELL, (cells[n] + 1) * CELL)
+        for q in range(RADIX):
+            re, im = complex_product(inverse_ref[q], s_ref[n, q])
+            both = jnp.stack([re.astype(BF16), im.astype(BF16)], axis=0)
+            image_ref[n, q] = jnp.swapaxes(both, 0, 1)
+            copy = pltpu.make_async_copy(
+                image_ref.at[n, q], focused_hbm.at[:, q, :, lanes], sems.at[n, q]
+            )
+            copy.start()
+            copies.append(copy)
+            power = (re * re + im * im).astype(BF16)
+            power_ref[q * part : (q + 1) * part, n * CELL : (n + 1) * CELL] = power
+
+    for n in steps:
+        transform(n)
+    for n in steps:
+        correlate_cell(n)
+    for n in steps:
+        finish(n)
     sums = dot(pulse_ref[...], power_ref[...])
-    high, low = split(sums[:, :CELL] + sums[:, CELL:])
-    range_mask = range_ref[:, cell]
-    sums = dot_nt(
-        jnp.concatenate([range_mask, range_mask], axis=1), jnp.concatenate([high, low], axis=1)
-    )
+    high, low = split(sums)
+    mask = jnp.concatenate([range_ref[:, cell * CELL : (cell + 1) * CELL] for cell in cells], axis=1)
+    sums = dot_nt(jnp.concatenate([mask, mask], axis=1), jnp.concatenate([high, low], axis=1))
     if first:
-
-        @pl.when(step == 0)
-        def _():
-            sums_ref[...] = sums[:tiles]
-            left_ref[...] = sums[tiles : tiles + 1]
-            right_ref[...] = sums[tiles + 1 : tiles + 2]
-
-        @pl.when(step > 0)
-        def _():
-            sums_ref[...] += sums[:tiles]
-            left_ref[...] += sums[tiles : tiles + 1]
-            right_ref[...] += sums[tiles + 1 : tiles + 2]
-
+        sums_ref[...] = sums[:tiles]
+        left_ref[...] = sums[tiles : tiles + 1]
+        right_ref[...] = sums[tiles + 1 : tiles + 2]
     else:
-
-        @pl.when(step == 0)
-        def _():
-            row = lax.broadcasted_iota(jnp.int32, looked_ref.shape, 0)
-            looked_ref[...] = (
-                early_ref[...]
-                + sums[:tiles]
-                + jnp.where(row == 0, from_left_ref[...], 0.0)
-                + jnp.where(row == tiles - 1, from_right_ref[...], 0.0)
-            )
-
-        @pl.when(step > 0)
-        def _():
-            looked_ref[...] += sums[:tiles]
-
-        @pl.when(step == len(cells) - 1)
-        def _():
-            looked_ref[...] /= inside_ref[...]
+        row = lax.broadcasted_iota(jnp.int32, looked_ref.shape, 0)
+        looked_ref[...] = (
+            early_ref[...]
+            + sums[:tiles]
+            + jnp.where(row == 0, from_left_ref[...], 0.0)
+            + jnp.where(row == tiles - 1, from_right_ref[...], 0.0)
+        ) / inside_ref[...]
+    for copy in copies:
+        copy.wait()
 
 
 def focus(first, cells, places, pulses, width, tiles, tables, sources, more):
@@ -431,46 +466,31 @@
     pulse_tiles = pulse_mask.shape[0]
     part = pulses // RADIX
     offsets = list(sources)
-
-    def cell_of(step):
-        place = cells[0]
-        for n in range(1, len(cells)):
-            place = jnp.where(step == n, cells[n], place)
-        return place
-
-    def whole(shape):
-        return pl.BlockSpec(shape, lambda i: (0,) * len(shape))
-
     vmem = pl.BlockSpec(memory_space=pltpu.VMEM)
+    anywhere = pl.BlockSpec(memory_space=pl.ANY)
     in_specs = [pl.BlockSpec(memory_space=pltpu.SMEM)] + [vmem] * (6 + len(offsets))
-    focused_shape = jax.ShapeDtypeStruct((pulses, 2, width), BF16)
-    focused_spec = pl.BlockSpec((pulses, 2, CELL), lambda i: (0, 0, cell_of(i)))
-    looks = (tiles, pulse_tiles)
-    edge = (1, pulse_tiles)
+    shapes = [jax.ShapeDtypeStruct((part, RADIX, 2, width), BF16)]
+    shapes += [jax.ShapeDtypeStruct((tiles, pulse_tiles), F32)]
     if first:
-        out_shape = [focused_shape] + [jax.ShapeDtypeStruct(s, F32) for s in (looks, edge, edge)]
-        out_specs = [focused_spec, whole(looks), whole(edge), whole(edge)]
-        aliases = {}
+        shapes += [jax.ShapeDtypeStruct((1, pulse_tiles), F32)] * 2
     else:
-        in_specs += [pl.BlockSpec(memory_space=pl.ANY)] + [vmem] * 4
-        out_shape = [focused_shape, jax.ShapeDtypeStruct(looks, F32)]
-        out_specs = [focused_spec, whole(looks)]
-        aliases = {7 + len(offsets): 0}
+        in_specs += [anywhere] + [vmem] * 4
     direct = all(source.shape[0] % (16 * RADIX) == 0 for source in sources.values())
     x_shape = (RADIX, part, 2 * CELL) if direct else (pulses, 2 * CELL)
     return pl.pallas_call(
         functools.partial(focus_kernel, tuple(offsets), places, tuple(cells), first),
-        grid=(len(cells),),
-        out_shape=out_shape,
+        out_shape=shapes,
         in_specs=in_specs,
-        out_specs=out_specs,
+        out_specs=[anywhere] + [vmem] * (len(shapes) - 1),
         scratch_shapes=[
-            pltpu.VMEM(x_shape, BF16),
-            pltpu.VMEM((RADIX, 2, part, CELL), F32),
-            pltpu.VMEM((RADIX, 2, part, CELL), F32),
-            pltpu.VMEM((pulses, 2 * CELL), BF16),
+            pltpu.VMEM((len(cells),) + x_shape, BF16),
+            pltpu.VMEM((len(cells), RADIX, 2, part, CELL), F32),
+            pltpu.VMEM((len(cells), RADIX, part, 2 * CELL), BF16),
+            pltpu.VMEM((pulses, len(cells) * CELL), BF16),
+            pltpu.VMEM((len(cells), RADIX, part, 2, CELL), BF16),
+            pltpu.SemaphoreType.DMA((len(cells), RADIX)),
         ],
-        input_output_aliases=aliases,
+        input_output_aliases={} if first else {7 + len(offsets): 0},
         compiler_params=pltpu.CompilerParams(vmem_limit_bytes=FOCUS_VMEM),
         cost_estimate=pl.CostEstimate(
             flops=len(cells) << 31, bytes_accessed=len(cells) << 21, transcendentals=0
@@ -489,7 +509,7 @@
     pulses = rows * count
     width = samples // count
     cells = list(range(width // CELL))
-    chunked = len(cells) == RADIX
+    chunked = len(cells) == RADIX and count == 16
 
     def send(piece, offset):
         if offset == 0:
@@ -497,35 +517,26 @@
         return lax.ppermute(piece, "row", [(i, i ^ offset) for i in range(count)])
 
     sibling = send(echoes, 1)
-    far = list(range(count // 2, count, 2))
-    near = list(range(2, count // 2, 2))
-    alone = [far[0], far[0] + 1] if chunked else [0]
+    replica = jnp.pad(range_replica.astype(F32), ((0, 0), (0, min(256, width))))
     if chunked:
-        far = far[1:]
-    late = frozenset(far) if chunked else frozenset()
-    half = len(far) // 2
-    far = far[half:] + far[:half]
-    near = near[half:] + near[:half]
-    alone, table = compress_first(me, echoes, range_replica, alone, width)
-    after = table
-    pieces = {}
-    if chunked:
-        pieces = {offset: (piece, None) for offset, piece in alone.items()}
-        pieces.update(compress(me, echoes, sibling, table, after, far[:1], late, width))
-        after = pieces[far[0]][1]
-        far = far[1:]
-    rest = []
-    while near or far:
-        rest += far[:1] + near[:1]
-        near, far = near[1:], far[1:]
-    pieces.update(compress(me, echoes, sibling, table, after, rest + [0], late, width))
-    received = {offset: send(piece, offset) for offset, (piece, _) in pieces.items()}
-    received_late = {offset: send(pieces[offset][1], offset) for offset in pieces if offset in late}
+        late = ()
+        late = (12, 10, 14)
+        first = compress_first(me, echoes, replica, [8, 9], width)
+        received = {offset: send(piece, offset) for offset, piece in first.items()}
+        pieces = compress(me, echoes, sibling, replica, first[8], [12], late, width)
+        others = [10, 2, 14, 4, 6, 0]
+        pieces.update(compress(me, echoes, sibling, replica, pieces[12][1], others, late, width))
+        received.update({offset: send(pieces[offset][0], offset) for offset in [12] + others})
+        received_late = {offset: send(pieces[offset][1], offset) for offset in late}
+    else:
+        late = ()
+        pieces = compress(me, echoes, sibling, replica, me, list(range(2, count, 2)) + [0], late, width)
+        received = {offset: send(piece, offset) for offset, (piece, _) in pieces.items()}
 
     forward, inverse = (jnp.asarray(m) for m in phase_matrices(pulses))
     tiles = width // TILE
     spectra, pulse_mask, range_mask, inside = make_tables(
-        me, azimuth_replicas, azimuth_extent, range_extent, forward, pieces[0][0], width
+        me, azimuth_replicas, azimuth_extent, range_extent, forward, received[0], width
     )
     tables = (me, forward, inverse, spectra, replica_index[None, :], pulse_mask, range_mask)
     early = [cell for cell in cells if not (chunked and cell in LATE)]
@@ -538,14 +549,14 @@
     if not chunked:
         pad = jnp.zeros((tiles - 2, sums.shape[1]), F32)
         edges = jnp.concatenate([from_left, pad, from_right], axis=0)
-        return focused, (sums + edges) / inside
+        return focused.reshape(pulses, 2, width), (sums + edges) / inside
     places = {offset: list(range(len(LATE))) if offset in late else LATE for offset in received}
     sources = {offset: received_late.get(offset, received[offset]) for offset in received}
     more = (focused, sums, from_left, from_right, inside)
     focused, looked = focus(
         False, LATE, places, pulses, width, tiles, tables, sources, more
     )
-    return focused, looked
+    return focused.reshape(pulses, 2, width), looked
 
 
 def solution(mesh):

time: 67.7 us -> 64.8 us (0.957)
  waiting for transfers between devices: 14.5 us -> 12.1 us
  Pallas kernels: 22.8 us -> 21 us
  starting transfers between devices: 27 us -> 28.2 us
  other arithmetic: 0 us -> 0.69 us
  local copies, waits for them, and re-layouts: 2.32 us -> 1.63 us
    ppermute x12, starting transfers between devices: 18.5 us -> 20.5 us  [send(): return lax.ppermute(piece, 'row', [(i, i ^ offset) for i in range(count)])]
    pallas_call x2, Pallas kernels: 12.1 us -> 10.2 us  [focus(): pl.pallas_call(functools.partial(focus_kernel, tuple(offsets), places, tu...]
    ppermute x12, waiting for transfers between devices: 10.7 us -> 9.15 us  [send(): return lax.ppermute(piece, 'row', [(i, i ^ offset) for i in range(count)])]
    ppermute x1, waiting for transfers between devices: 3.79 us -> 2.92 us  [per_device(): lax.ppermute(left, 'row', [(i, i - 1) for i in range(1, count)])]
    ppermute x1, starting transfers between devices: 6.59 us -> 5.75 us  [per_device(): lax.ppermute(right, 'row', [(i, i + 1) for i in range(count - 1)])]
    pad x0 -> x1, other arithmetic: none -> 0.69 us  [per_device(): replica = jnp.pad(range_replica.astype(F32), ((0, 0), (0, min(256, width))))]
    unnamed x16 -> x14, local copies, waits for them, and re-layouts: 2.32 us -> 1.63 us
  transfers between devices with their start and end apart: 14 -> 14, of which waited for: 3 -> 6; matrix products, arithmetic and copies ran while one was open for 0% -> 1% of each run, Pallas kernels for 25% -> 24%
where the time goes in v2:
time: 64.8 us; the launch traced here: 64.5 us
  starting transfers between devices  28.2 us (44%)
  Pallas kernels  21 us (32%)
  waiting for transfers between devices  12.1 us (19%)
  local copies, waits for them, and re-layouts  1.63 us (3%)
  between operations  0.94 us (1%)
  other arithmetic  0.69 us (1%)
    ppermute x12, starting transfers between devices, send(): return lax.ppermute(piece, 'row', [(i, i ^ offset) for i in range(count)])  20.5 us
    pallas_call x2, Pallas kernels, focus(): pl.pallas_call(functools.partial(focus_kernel, tuple(offsets), places, tu...  10.2 us
    ppermute x12, waiting for transfers between devices, send(): return lax.ppermute(piece, 'row', [(i, i ^ offset) for i in range(count)])  9.15 us
    pallas_call x2, Pallas kernels, compress(): pl.pallas_call(functools.partial(range_kernel, tuple(offsets), late, widt...  7.47 us
    ppermute x1, starting transfers between devices, per_device(): lax.ppermute(right, 'row', [(i, i + 1) for i in range(count - 1)])  5.75 us
    ppermute x1, waiting for transfers between devices, per_device(): lax.ppermute(left, 'row', [(i, i - 1) for i in range(1, count)])  2.92 us
    ppermute x1, starting transfers between devices, per_device(): lax.ppermute(left, 'row', [(i, i - 1) for i in range(1, count)])  1.92 us
    pallas_call x1, Pallas kernels, make_tables(): pl.pallas_call(tables_kernel, out_shape=[jax.ShapeDtypeStruct(*shape) for...  1.91 us
  transfers between devices with their start and end apart: 14, of which 6 were waited for; matrix products, arithmetic and copies ran while one was open for 1% of the time, Pallas kernels for 24%

profile of v2, /device:TPU:13, one launch (start us, length us, event | category | flops | bytes accessed | tf_op | source)
XLA Modules:
  0.0 64.5 jit_solution(14509496363578775003)
XLA Ops:
  0.6 0.7 %collective-permute-start = (bf16[64,2,8192]{2,1,0:T(2,128)(2,1)}, bf16[64,2,8192]{2,1,0:T(2,128)(2,1)S(1)}, u32[]{:S(2)}, u32[]{:S(2)}) collective-permute-start(bf16[64,2,8192]{2,1,0:T(2,128)(2,1)} %x_ref.3), channel_id=1, source_target_pairs={{0,1},{1,0},{2,3},{3,2},{4,5},{5,4},{6,7},{7,6},{8,9},{9,8},{10,11... | collective-permute-start | bytes 6291464 | tf_op jit(solution)/shard_map/ppermute | solution.py:517
  1.4 0.7 %pad_convert_fusion.h_ref = f32[2,1280]{1,0:T(2,128)S(1)} fusion(bf16[2,1024]{1,0:T(2,128)(2,1)} %param.9), kind=kLoop, calls=%fused_computation | loop fusion | flops 2560 | bytes 14336 | tf_op jit(solution)/shard_map/jit(_pad)/pad | solution.py:520
  2.1 1.6 %copy-done = bf16[64,2,8192]{2,1,0:T(2,128)(2,1)S(1)} copy-done((bf16[64,2,8192]{2,1,0:T(2,128)(2,1)S(1)}, bf16[64,2,8192]{2,1,0:T(2,128)(2,1)}, u32[]{:S(2)}) %copy-start) | copy-done | bytes 2097176
  3.7 1.5 %range_compress_first.1 = (bf16[64,1024]{1,0:T(8,128)(2,1)S(1)}, bf16[64,1024]{1,0:T(8,128)(2,1)S(1)}) custom-call(s32[1]{0:T(128)} %bitcast.me_ref, bf16[64,2,8192]{2,1,0:T(2,128)(2,1)S(1)} %copy-done, f32[2,1280]{1,0:T(2,128)S(1)} %pad_convert_fusion.h_ref), custom_call_target="tpu_custom_call" | custom-call | flops 1342177280 | bytes 786432 | tf_op jit(solution)/shard_map/range_compress_first/pallas_call | solution.py:203
  5.2 2.3 %collective-permute-start.2 = (bf16[64,1024]{1,0:T(8,128)(2,1)S(1)}, bf16[64,1024]{1,0:T(8,128)(2,1)S(1)}, u32[]{:S(2)}, u32[]{:S(2)}) collective-permute-start(bf16[64,1024]{1,0:T(8,128)(2,1)S(1)} %get-tuple-element.30), channel_id=1, source_target_pairs={{0,9},{1,8},{2,11},{3,10},{4,13},{5,12},{6,15},{7,14},{8,1},{9,0},... | collective-permute-start | bytes 393224 | tf_op jit(solution)/shard_map/ppermute | solution.py:517
  7.4 0.2 collective-permute-start.1
  7.6 1.2 %range_compress.2 = (bf16[128,512]{1,0:T(8,128)(2,1)S(1)}, bf16[128,512]{1,0:T(8,128)(2,1)S(1)}) custom-call(s32[1]{0:T(128)} %bitcast.me_ref, bf16[64,2,8192]{2,1,0:T(2,128)(2,1)S(1)} %copy-done, bf16[64,2,8192]{2,1,0:T(2,128)(2,1)S(1)} %collective-permute-done.sibling_ref, f32[2,1280]{1,0:T(2,128)S(1)} %pad_convert_fusion.h_ref, ...), custom_call_target="tpu_custom_call" | custom-call | flops 1342177280 | bytes 786432 | tf_op jit(solution)/shard_map/range_compress/pallas_call | solution.py:235
  8.9 0.0 copy-start.1
  8.9 0.0 copy-start.2
  8.9 0.0 copy-start.4
  8.9 0.0 copy-start.5
  8.9 6.2 %range_compress.3 = (bf16[128,512]{1,0:T(8,128)(2,1)S(1)}, bf16[128,512]{1,0:T(8,128)(2,1)S(1)}, bf16[128,1024]{1,0:T(8,128)(2,1)S(1)}, bf16[128,512]{1,0:T(8,12...) custom-call(s32[1]{0:T(128)} %bitcast.me_ref, ...), custom_call_target="tpu_custom_call" | custom-call | flops 8053063680 | bytes 4718592 | tf_op jit(solution)/shard_map/range_compress/pallas_call | solution.py:235
  15.1 2.2 %collective-permute-start.10 = (bf16[128,512]{1,0:T(8,128)(2,1)S(1)}, bf16[128,512]{1,0:T(8,128)(2,1)S(1)}, u32[]{:S(2)}, u32[]{:S(2)}) collective-permute-start(bf16[128,512]{1,0:T(8,128)(2,1)S(1)} %get-tuple-element.37), channel_id=1, source_target_pairs={{0,10},{1,11},{2,8},{3,9},{4,14},{5,15},{6,12},{7,13},{8,2},{9,3},... | collective-permute-start | bytes 393224 | tf_op jit(solution)/shard_map/ppermute | solution.py:517
  17.3 1.3 %collective-permute-start.5 = (bf16[128,1024]{1,0:T(8,128)(2,1)S(1)}, bf16[128,1024]{1,0:T(8,128)(2,1)S(1)}, u32[]{:S(2)}, u32[]{:S(2)}) collective-permute-start(bf16[128,1024]{1,0:T(8,128)(2,1)S(1)} %get-tuple-element.32), channel_id=1, source_target_pairs={{0,2},{1,3},{2,0},{3,1},{4,6},{5,7},{6,4},{7,5},{8,10},{9,11},{10,... | collective-permute-start | bytes 786440 | tf_op jit(solution)/shard_map/ppermute | solution.py:517
  18.6 0.2 collective-permute-start.7
  18.7 1.2 %collective-permute-start.8 = (bf16[128,1024]{1,0:T(8,128)(2,1)S(1)}, bf16[128,1024]{1,0:T(8,128)(2,1)S(1)}, u32[]{:S(2)}, u32[]{:S(2)}) collective-permute-start(bf16[128,1024]{1,0:T(8,128)(2,1)S(1)} %get-tuple-element.35), channel_id=1, source_target_pairs={{0,6},{1,7},{2,4},{3,5},{4,2},{5,3},{6,0},{7,1},{8,14},{9,15},{10,... | collective-permute-start | bytes 786440 | tf_op jit(solution)/shard_map/ppermute | solution.py:517
  20.0 1.8 %collective-permute-done.1.refs_0_ = bf16[64,1024]{1,0:T(8,128)(2,1)S(1)} collective-permute-done((bf16[64,1024]{1,0:T(8,128)(2,1)S(1)}, bf16[64,1024]{1,0:T(8,128)(2,1)S(1)}, u32[]{:S(2)}, u32[]{:S(2)}) %collective-permute-start.1) | collective-permute-done | bytes 131104 | tf_op jit(solution)/shard_map/ppermute | solution.py:517
  21.8 2.9 %collective-permute-done.10.refs_3_ = bf16[128,512]{1,0:T(8,128)(2,1)S(1)} collective-permute-done((bf16[128,512]{1,0:T(8,128)(2,1)S(1)}, bf16[128,512]{1,0:T(8,128)(2,1)S(1)}, u32[]{:S(2)}, u32[]{:S(2)}) %collective-permute-start.10) | collective-permute-done | bytes 131104 | tf_op jit(solution)/shard_map/ppermute | solution.py:517
  24.7 0.0 copy-start.3
  24.7 0.0 copy-start.6
  24.8 1.9 %tables.1 = (bf16[4,512,32]{2,1,0:T(8,128)(2,1)S(1)}, bf16[64,1024]{1,0:T(8,128)(2,1)S(1)}, bf16[48,512]{1,0:T(8,128)(2,1)S(1)}, f32[32,64]{1,0:T(8,128)S(1)}) custom-call(s32[1]{0:T(128)} %bitcast.me_ref, bf16[16,2,512]{2,1,0:T(2,128)(2,1)S(1)} %copy-done.1, s32[1,64]{1,0:T(1,128)S(1)} %bitcast.8, s32[1,512]{1,0:T(1,128)S(1)} %bitcast.5, ...), custom_call_target="tpu_custom_call" | custom-call | flops 2147483648 | bytes 4194304 | tf_op jit(solution)/shard_map/tables/pallas_call | solution.py:343
  26.7 2.3 %collective-permute-done.11.refs_5_ = bf16[128,512]{1,0:T(8,128)(2,1)S(1)} collective-permute-done((bf16[128,512]{1,0:T(8,128)(2,1)S(1)}, bf16[128,512]{1,0:T(8,128)(2,1)S(1)}, u32[]{:S(2)}, u32[]{:S(2)}) %collective-permute-start.11) | collective-permute-done | bytes 131104 | tf_op jit(solution)/shard_map/ppermute | solution.py:517
  28.9 2.2 %collective-permute-start.3 = (bf16[128,512]{1,0:T(8,128)(2,1)S(1)}, bf16[128,512]{1,0:T(8,128)(2,1)S(1)}, u32[]{:S(2)}, u32[]{:S(2)}) collective-permute-start(bf16[128,512]{1,0:T(8,128)(2,1)S(1)} %get-tuple-element.25.after_ref), channel_id=1, source_target_pairs={{0,12},{1,13},{2,14},{3,15},{4,8},{5,9},{6,10},{7,11},{8,4},{9,5},... | collective-permute-start | bytes 393224 | tf_op jit(solution)/shard_map/ppermute | solution.py:517
  31.1 1.3 %collective-permute-done.9.refs_2_ = bf16[128,512]{1,0:T(8,128)(2,1)S(1)} collective-permute-done((bf16[128,512]{1,0:T(8,128)(2,1)S(1)}, bf16[128,512]{1,0:T(8,128)(2,1)S(1)}, u32[]{:S(2)}, u32[]{:S(2)}) %collective-permute-start.9) | collective-permute-done | bytes 131104 | tf_op jit(solution)/shard_map/ppermute | solution.py:517
  32.3 8.4 %collective-permute-start.4 = (bf16[128,512]{1,0:T(8,128)(2,1)S(1)}, bf16[128,512]{1,0:T(8,128)(2,1)S(1)}, u32[]{:S(2)}, u32[]{:S(2)}) collective-permute-start(bf16[128,512]{1,0:T(8,128)(2,1)S(1)} %get-tuple-element.31), channel_id=1, source_target_pairs={{0,10},{1,11},{2,8},{3,9},{4,14},{5,15},{6,12},{7,13},{8,2},{9,3},... | collective-permute-start | bytes 393224 | tf_op jit(solution)/shard_map/ppermute | solution.py:517
  40.7 2.0 %collective-permute-start.6 = (bf16[128,512]{1,0:T(8,128)(2,1)S(1)}, bf16[128,512]{1,0:T(8,128)(2,1)S(1)}, u32[]{:S(2)}, u32[]{:S(2)}) collective-permute-start(bf16[128,512]{1,0:T(8,128)(2,1)S(1)} %get-tuple-element.33), channel_id=1, source_target_pairs={{0,14},{1,15},{2,12},{3,13},{4,10},{5,11},{6,8},{7,9},{8,6},{9,7},... | collective-permute-start | bytes 393224 | tf_op jit(solution)/shard_map/ppermute | solution.py:517
  42.7 4.9 %azimuth_focus.2 = (bf16[256,4,2,512]{3,2,1,0:T(2,128)(2,1)}, f32[32,64]{1,0:T(8,128)S(1)}, f32[1,64]{1,0:T(1,128)S(1)}, f32[1,64]{1,0:T(1,128)S(1)}) custom-call(s32[1]{0:T(128)} %bitcast.me_ref, bf16[4,512,512]{2,1,0:T(8,128)(2,1)S(1)} %copy-done.5, bf16[4,512,512]{2,1,0:T(8,128)(2,1)S(1)} %copy-done.6, ...), custom_call_target="tpu_custom_call" | custom-call | flops 4294967296 | bytes 4194304 | tf_op jit(solution)/shard_map/azimuth_focus/pallas_call | solution.py:480
  47.6 5.7 %collective-permute-start.12 = (f32[1,64]{1,0:T(1,128)S(1)}, f32[1,64]{1,0:T(1,128)S(1)}, u32[]{:S(2)}, u32[]{:S(2)}) collective-permute-start(f32[1,64]{1,0:T(1,128)S(1)} %get-tuple-element.41), channel_id=1, source_target_pairs={{0,1},{1,2},{2,3},{3,4},{4,5},{5,6},{6,7},{7,8},{8,9},{9,10},{10,1... | collective-permute-start | bytes 776 | tf_op jit(solution)/shard_map/ppermute | solution.py:548
  53.3 1.9 %collective-permute-start.13 = (f32[1,64]{1,0:T(1,128)S(1)}, f32[1,64]{1,0:T(1,128)S(1)}, u32[]{:S(2)}, u32[]{:S(2)}) collective-permute-start(f32[1,64]{1,0:T(1,128)S(1)} %get-tuple-element.42), channel_id=1, source_target_pairs={{1,0},{2,1},{3,2},{4,3},{5,4},{6,5},{7,6},{8,7},{9,8},{10,9},{11,1... | collective-permute-start | bytes 776 | tf_op jit(solution)/shard_map/ppermute | solution.py:547
  55.3 0.9 %collective-permute-done.6.refs_5_ = bf16[128,512]{1,0:T(8,128)(2,1)S(1)} collective-permute-done((bf16[128,512]{1,0:T(8,128)(2,1)S(1)}, bf16[128,512]{1,0:T(8,128)(2,1)S(1)}, u32[]{:S(2)}, u32[]{:S(2)}) %collective-permute-start.6) | collective-permute-done | bytes 131104 | tf_op jit(solution)/shard_map/ppermute | solution.py:517
  56.2 2.9 %collective-permute-done.13.refs_12_ = f32[1,64]{1,0:T(1,128)S(1)} collective-permute-done((f32[1,64]{1,0:T(1,128)S(1)}, f32[1,64]{1,0:T(1,128)S(1)}, u32[]{:S(2)}, u32[]{:S(2)}) %collective-permute-start.13) | collective-permute-done | bytes 288 | tf_op jit(solution)/shard_map/ppermute | solution.py:547
  59.1 5.3 %azimuth_focus.3 = (bf16[256,4,2,512]{3,2,1,0:T(2,128)(2,1)}, f32[32,64]{1,0:T(8,128)}) custom-call(s32[1]{0:T(128)} %bitcast.me_ref, bf16[4,512,512]{2,1,0:T(8,128)(2,1)S(1)} %copy-done.5, bf16[4,512,512]{2,1,0:T(8,128)(2,1)S(1)} %copy-done.6, bf16[4,512,32]{2,1,0:T(8,128)(2,1)S(1)} %get-tuple-element.27.spectra_ref, ...), custom_call_target="tpu_custom_call", output_to_operand_aliasing={{0}: (16, {})} | custom-call | flops 4294967296 | bytes 4194304 | tf_op jit(solution)/shard_map/azimuth_focus/pallas_call | solution.py:480
  (17 shorter events, 0.0 us)
Async XLA Ops:
  0.6 7.0 %collective-permute-start = (bf16[64,2,8192]{2,1,0:T(2,128)(2,1)}, bf16[64,2,8192]{2,1,0:T(2,128)(2,1)S(1)}, u32[]{:S(2)}, u32[]{:S(2)}) collective-permute-start(bf16[64,2,8192]{2,1,0:T(2,128)(2,1)} %x_ref.3), channel_id=1, source_target_pairs={{0,1},{1,0},{2,3},{3,2},{4,5},{5,4},{6,7},{7,6},{8,9},{9,8},{10,11... | collective-permute-start | bytes 6291464 | tf_op jit(solution)/shard_map/ppermute | solution.py:517
  2.1 1.6 %copy-start = (bf16[64,2,8192]{2,1,0:T(2,128)(2,1)S(1)}, bf16[64,2,8192]{2,1,0:T(2,128)(2,1)}, u32[]{:S(2)}) copy-start(bf16[64,2,8192]{2,1,0:T(2,128)(2,1)} %x_ref.3) | copy-start | bytes 6291460
  5.2 13.6 %collective-permute-start.2 = (bf16[64,1024]{1,0:T(8,128)(2,1)S(1)}, bf16[64,1024]{1,0:T(8,128)(2,1)S(1)}, u32[]{:S(2)}, u32[]{:S(2)}) collective-permute-start(bf16[64,1024]{1,0:T(8,128)(2,1)S(1)} %get-tuple-element.30), channel_id=1, source_target_pairs={{0,9},{1,8},{2,11},{3,10},{4,13},{5,12},{6,15},{7,14},{8,1},{9,0},... | collective-permute-start | bytes 393224 | tf_op jit(solution)/shard_map/ppermute | solution.py:517
  7.4 14.4 %collective-permute-start.1 = (bf16[64,1024]{1,0:T(8,128)(2,1)S(1)}, bf16[64,1024]{1,0:T(8,128)(2,1)S(1)}, u32[]{:S(2)}, u32[]{:S(2)}) collective-permute-start(bf16[64,1024]{1,0:T(8,128)(2,1)S(1)} %get-tuple-element.24.after_ref), channel_id=1, source_target_pairs={{0,8},{1,9},{2,10},{3,11},{4,12},{5,13},{6,14},{7,15},{8,0},{9,1},... | collective-permute-start | bytes 393224 | tf_op jit(solution)/shard_map/ppermute | solution.py:517
  8.9 15.9 %copy-start.1 = (bf16[16,2,512]{2,1,0:T(2,128)(2,1)S(1)}, bf16[16,2,512]{2,1,0:T(2,128)(2,1)}, u32[]{:S(2)}) copy-start(bf16[16,2,512]{2,1,0:T(2,128)(2,1)} %taps_ref.1) | copy-start | bytes 98308
  8.9 15.8 %copy-start.2 = (s32[512]{0:T(512)S(1)}, s32[512]{0:T(512)}, u32[]{:S(2)}) copy-start(s32[512]{0:T(512)} %param.13) | copy-start | bytes 6148
  8.9 15.8 %copy-start.4 = (s32[64]{0:T(128)S(1)}, s32[64]{0:T(128)}, u32[]{:S(2)}) copy-start(s32[64]{0:T(128)} %param.12) | copy-start | bytes 772
  8.9 15.8 %copy-start.5 = (bf16[4,512,512]{2,1,0:T(8,128)(2,1)S(1)}, bf16[4,512,512]{2,1,0:T(8,128)(2,1)}, u32[]{:S(2)}) copy-start(bf16[4,512,512]{2,1,0:T(8,128)(2,1)} %constant.12.clone.matrix_ref.forward_ref) | copy-start | bytes 6291460
  15.1 9.6 %collective-permute-start.10 = (bf16[128,512]{1,0:T(8,128)(2,1)S(1)}, bf16[128,512]{1,0:T(8,128)(2,1)S(1)}, u32[]{:S(2)}, u32[]{:S(2)}) collective-permute-start(bf16[128,512]{1,0:T(8,128)(2,1)S(1)} %get-tuple-element.37), channel_id=1, source_target_pairs={{0,10},{1,11},{2,8},{3,9},{4,14},{5,15},{6,12},{7,13},{8,2},{9,3},... | collective-permute-start | bytes 393224 | tf_op jit(solution)/shard_map/ppermute | solution.py:517
  17.3 23.4 %collective-permute-start.5 = (bf16[128,1024]{1,0:T(8,128)(2,1)S(1)}, bf16[128,1024]{1,0:T(8,128)(2,1)S(1)}, u32[]{:S(2)}, u32[]{:S(2)}) collective-permute-start(bf16[128,1024]{1,0:T(8,128)(2,1)S(1)} %get-tuple-element.32), channel_id=1, source_target_pairs={{0,2},{1,3},{2,0},{3,1},{4,6},{5,7},{6,4},{7,5},{8,10},{9,11},{10,... | collective-permute-start | bytes 786440 | tf_op jit(solution)/shard_map/ppermute | solution.py:517
  18.6 24.1 %collective-permute-start.7 = (bf16[128,1024]{1,0:T(8,128)(2,1)S(1)}, bf16[128,1024]{1,0:T(8,128)(2,1)S(1)}, u32[]{:S(2)}, u32[]{:S(2)}) collective-permute-start(bf16[128,1024]{1,0:T(8,128)(2,1)S(1)} %get-tuple-element.34), channel_id=1, source_target_pairs={{0,4},{1,5},{2,6},{3,7},{4,0},{5,1},{6,2},{7,3},{8,12},{9,13},{10,... | collective-permute-start | bytes 786440 | tf_op jit(solution)/shard_map/ppermute | solution.py:517
  18.7 23.9 %collective-permute-start.8 = (bf16[128,1024]{1,0:T(8,128)(2,1)S(1)}, bf16[128,1024]{1,0:T(8,128)(2,1)S(1)}, u32[]{:S(2)}, u32[]{:S(2)}) collective-permute-start(bf16[128,1024]{1,0:T(8,128)(2,1)S(1)} %get-tuple-element.35), channel_id=1, source_target_pairs={{0,6},{1,7},{2,4},{3,5},{4,2},{5,3},{6,0},{7,1},{8,14},{9,15},{10,... | collective-permute-start | bytes 786440 | tf_op jit(solution)/shard_map/ppermute | solution.py:517
  21.8 7.1 %collective-permute-start.11 = (bf16[128,512]{1,0:T(8,128)(2,1)S(1)}, bf16[128,512]{1,0:T(8,128)(2,1)S(1)}, u32[]{:S(2)}, u32[]{:S(2)}) collective-permute-start(bf16[128,512]{1,0:T(8,128)(2,1)S(1)} %get-tuple-element.38), channel_id=1, source_target_pairs={{0,14},{1,15},{2,12},{3,13},{4,10},{5,11},{6,8},{7,9},{8,6},{9,7},... | collective-permute-start | bytes 393224 | tf_op jit(solution)/shard_map/ppermute | solution.py:517
  24.7 7.6 %collective-permute-start.9 = (bf16[128,512]{1,0:T(8,128)(2,1)S(1)}, bf16[128,512]{1,0:T(8,128)(2,1)S(1)}, u32[]{:S(2)}, u32[]{:S(2)}) collective-permute-start(bf16[128,512]{1,0:T(8,128)(2,1)S(1)} %get-tuple-element.36), channel_id=1, source_target_pairs={{0,12},{1,13},{2,14},{3,15},{4,8},{5,9},{6,10},{7,11},{8,4},{9,5},... | collective-permute-start | bytes 393224 | tf_op jit(solution)/shard_map/ppermute | solution.py:517
  24.7 18.0 %copy-start.3 = (s32[512]{0:T(512)S(1)}, s32[512]{0:T(512)}, u32[]{:S(2)}) copy-start(s32[512]{0:T(512)} %param.11) | copy-start | bytes 6148
  24.7 18.0 %copy-start.6 = (bf16[4,512,512]{2,1,0:T(8,128)(2,1)S(1)}, bf16[4,512,512]{2,1,0:T(8,128)(2,1)}, u32[]{:S(2)}) copy-start(bf16[4,512,512]{2,1,0:T(8,128)(2,1)} %constant.13.clone.inverse_ref) | copy-start | bytes 6291460
  28.9 27.2 %collective-permute-start.3 = (bf16[128,512]{1,0:T(8,128)(2,1)S(1)}, bf16[128,512]{1,0:T(8,128)(2,1)S(1)}, u32[]{:S(2)}, u32[]{:S(2)}) collective-permute-start(bf16[128,512]{1,0:T(8,128)(2,1)S(1)} %get-tuple-element.25.after_ref), channel_id=1, source_target_pairs={{0,12},{1,13},{2,14},{3,15},{4,8},{5,9},{6,10},{7,11},{8,4},{9,5},... | collective-permute-start | bytes 393224 | tf_op jit(solution)/shard_map/ppermute | solution.py:517
  32.3 22.9 %collective-permute-start.4 = (bf16[128,512]{1,0:T(8,128)(2,1)S(1)}, bf16[128,512]{1,0:T(8,128)(2,1)S(1)}, u32[]{:S(2)}, u32[]{:S(2)}) collective-permute-start(bf16[128,512]{1,0:T(8,128)(2,1)S(1)} %get-tuple-element.31), channel_id=1, source_target_pairs={{0,10},{1,11},{2,8},{3,9},{4,14},{5,15},{6,12},{7,13},{8,2},{9,3},... | collective-permute-start | bytes 393224 | tf_op jit(solution)/shard_map/ppermute | solution.py:517
  40.7 15.4 %collective-permute-start.6 = (bf16[128,512]{1,0:T(8,128)(2,1)S(1)}, bf16[128,512]{1,0:T(8,128)(2,1)S(1)}, u32[]{:S(2)}, u32[]{:S(2)}) collective-permute-start(bf16[128,512]{1,0:T(8,128)(2,1)S(1)} %get-tuple-element.33), channel_id=1, source_target_pairs={{0,14},{1,15},{2,12},{3,13},{4,10},{5,11},{6,8},{7,9},{8,6},{9,7},... | collective-permute-start | bytes 393224 | tf_op jit(solution)/shard_map/ppermute | solution.py:517
  47.6 8.6 %collective-permute-start.12 = (f32[1,64]{1,0:T(1,128)S(1)}, f32[1,64]{1,0:T(1,128)S(1)}, u32[]{:S(2)}, u32[]{:S(2)}) collective-permute-start(f32[1,64]{1,0:T(1,128)S(1)} %get-tuple-element.41), channel_id=1, source_target_pairs={{0,1},{1,2},{2,3},{3,4},{4,5},{5,6},{6,7},{7,8},{8,9},{9,10},{10,1... | collective-permute-start | bytes 776 | tf_op jit(solution)/shard_map/ppermute | solution.py:548
  53.3 5.8 %collective-permute-start.13 = (f32[1,64]{1,0:T(1,128)S(1)}, f32[1,64]{1,0:T(1,128)S(1)}, u32[]{:S(2)}, u32[]{:S(2)}) collective-permute-start(f32[1,64]{1,0:T(1,128)S(1)} %get-tuple-element.42), channel_id=1, source_target_pairs={{1,0},{2,1},{3,2},{4,3},{5,4},{6,5},{7,6},{8,7},{9,8},{10,9},{11,1... | collective-permute-start | bytes 776 | tf_op jit(solution)/shard_map/ppermute | solution.py:547

commit v3 on v2

--- a/solution.py
+++ b/solution.py
@@ -385,8 +385,8 @@
         focused_hbm, sums_ref, left_ref, right_ref = refs[:4]
         tiles = sums_ref.shape[0]
     else:
-        _, early_ref, from_left_ref, from_right_ref, inside_ref, focused_hbm, looked_ref = refs[:7]
-        tiles = looked_ref.shape[0]
+        _, focused_hbm, sums_ref = refs[:3]
+        tiles = sums_ref.shape[0]
     x_ref, v_ref, s_ref, power_ref, image_ref, sems = refs[-6:]
     total = max(source.shape[0] for source in sources)
     part = v_ref.shape[3]
@@ -445,18 +445,10 @@
     high, low = split(sums)
     mask = jnp.concatenate([range_ref[:, cell * CELL : (cell + 1) * CELL] for cell in cells], axis=1)
     sums = dot_nt(jnp.concatenate([mask, mask], axis=1), jnp.concatenate([high, low], axis=1))
+    sums_ref[...] = sums[:tiles]
     if first:
-        sums_ref[...] = sums[:tiles]
         left_ref[...] = sums[tiles : tiles + 1]
         right_ref[...] = sums[tiles + 1 : tiles + 2]
-    else:
-        row = lax.broadcasted_iota(jnp.int32, looked_ref.shape, 0)
-        looked_ref[...] = (
-            early_ref[...]
-            + sums[:tiles]
-            + jnp.where(row == 0, from_left_ref[...], 0.0)
-            + jnp.where(row == tiles - 1, from_right_ref[...], 0.0)
-        ) / inside_ref[...]
     for copy in copies:
         copy.wait()
 
@@ -474,7 +466,7 @@
     if first:
         shapes += [jax.ShapeDtypeStruct((1, pulse_tiles), F32)] * 2
     else:
-        in_specs += [anywhere] + [vmem] * 4
+        in_specs += [anywhere]
     direct = all(source.shape[0] % (16 * RADIX) == 0 for source in sources.values())
     x_shape = (RADIX, part, 2 * CELL) if direct else (pulses, 2 * CELL)
     return pl.pallas_call(
@@ -499,6 +491,24 @@
     )(me, forward, inverse, spectra, index, pulse_mask, range_mask, *sources.values(), *more)
 
 
+def looks_kernel(from_left_ref, from_right_ref, inside_ref, *refs):
+    sums = sum(ref[...] for ref in refs[:-1])
+    row = lax.broadcasted_iota(jnp.int32, sums.shape, 0)
+    sums += jnp.where(row == 0, from_left_ref[...], 0.0)
+    sums += jnp.where(row == sums.shape[0] - 1, from_right_ref[...], 0.0)
+    refs[-1][...] = sums / inside_ref[...]
+
+
+def looks(from_left, from_right, inside, *sums):
+    return pl.pallas_call(
+        looks_kernel,
+        out_shape=jax.ShapeDtypeStruct(inside.shape, F32),
+        compiler_params=pltpu.CompilerParams(vmem_limit_bytes=GATE_VMEM),
+        cost_estimate=SMALL_COST,
+        name="looks",
+    )(from_left, from_right, inside, *sums)
+
+
 def per_device(
     echoes, range_replica, azimuth_replicas, replica_index, azimuth_extent, range_extent
 ):
@@ -546,17 +556,15 @@
     )
     from_right = lax.ppermute(left, "row", [(i, i - 1) for i in range(1, count)])
     from_left = lax.ppermute(right, "row", [(i, i + 1) for i in range(count - 1)])
-    if not chunked:
-        pad = jnp.zeros((tiles - 2, sums.shape[1]), F32)
-        edges = jnp.concatenate([from_left, pad, from_right], axis=0)
-        return focused.reshape(pulses, 2, width), (sums + edges) / inside
-    places = {offset: list(range(len(LATE))) if offset in late else LATE for offset in received}
-    sources = {offset: received_late.get(offset, received[offset]) for offset in received}
-    more = (focused, sums, from_left, from_right, inside)
-    focused, looked = focus(
-        False, LATE, places, pulses, width, tiles, tables, sources, more
-    )
-    return focused.reshape(pulses, 2, width), looked
+    sums = [sums]
+    if chunked:
+        places = {offset: list(range(len(LATE))) if offset in late else LATE for offset in received}
+        sources = {offset: received_late.get(offset, received[offset]) for offset in received}
+        focused, late_sums = focus(
+            False, LATE, places, pulses, width, tiles, tables, sources, (focused,)
+        )
+        sums.append(late_sums)
+    return focused.reshape(pulses, 2, width), looks(from_left, from_right, inside, *sums)
 
 
 def solution(mesh):

time: 64.8 us -> 61.8 us (0.954)
  waiting for transfers between devices: 12.1 us -> 9.15 us
    ppermute x1, waiting for transfers between devices: 2.92 us -> 0.01 us  [per_device(): lax.ppermute(left, 'row', [(i, i - 1) for i in range(1, count)])]
  transfers between devices with their start and end apart: 14 -> 14, of which waited for: 6 -> 5; matrix products, arithmetic and copies ran while one was open for 1% -> 1% of each run, Pallas kernels for 24% -> 33%
where the time goes in v3:
time: 61.8 us; the launch traced here: 61.5 us
  starting transfers between devices  28.2 us (46%)
  Pallas kernels  21 us (34%)
  waiting for transfers between devices  9.15 us (15%)
  local copies, waits for them, and re-layouts  1.63 us (3%)
  between operations  0.8 us (1%)
  other arithmetic  0.69 us (1%)
    ppermute x12, starting transfers between devices, send(): return lax.ppermute(piece, 'row', [(i, i ^ offset) for i in range(count)])  20.5 us
    pallas_call x2, Pallas kernels, focus(): pl.pallas_call(functools.partial(focus_kernel, tuple(offsets), places, tu...  9.55 us
    ppermute x12, waiting for transfers between devices, send(): return lax.ppermute(piece, 'row', [(i, i ^ offset) for i in range(count)])  9.15 us
    pallas_call x2, Pallas kernels, compress(): pl.pallas_call(functools.partial(range_kernel, tuple(offsets), late, widt...  7.47 us
    ppermute x1, starting transfers between devices, per_device(): lax.ppermute(right, 'row', [(i, i + 1) for i in range(count - 1)])  5.75 us
    ppermute x1, starting transfers between devices, per_device(): lax.ppermute(left, 'row', [(i, i - 1) for i in range(1, count)])  1.92 us
    pallas_call x1, Pallas kernels, make_tables(): pl.pallas_call(tables_kernel, out_shape=[jax.ShapeDtypeStruct(*shape) for...  1.91 us
    unnamed x14, local copies, waits for them, and re-layouts  1.63 us
  transfers between devices with their start and end apart: 14, of which 5 were waited for; matrix products, arithmetic and copies ran while one was open for 1% of the time, Pallas kernels for 33%

profile of v3, /device:TPU:13, one launch (start us, length us, event | category | flops | bytes accessed | tf_op | source)
XLA Modules:
  0.0 61.5 jit_solution(56158137087179343)
XLA Ops:
  0.6 0.7 %collective-permute-start = (bf16[64,2,8192]{2,1,0:T(2,128)(2,1)}, bf16[64,2,8192]{2,1,0:T(2,128)(2,1)S(1)}, u32[]{:S(2)}, u32[]{:S(2)}) collective-permute-start(bf16[64,2,8192]{2,1,0:T(2,128)(2,1)} %x_ref.3), channel_id=1, source_target_pairs={{0,1},{1,0},{2,3},{3,2},{4,5},{5,4},{6,7},{7,6},{8,9},{9,8},{10,11... | collective-permute-start | bytes 6291464 | tf_op jit(solution)/shard_map/ppermute | solution.py:527
  1.4 0.7 %pad_convert_fusion.h_ref = f32[2,1280]{1,0:T(2,128)S(1)} fusion(bf16[2,1024]{1,0:T(2,128)(2,1)} %param.9), kind=kLoop, calls=%fused_computation | loop fusion | flops 2560 | bytes 14336 | tf_op jit(solution)/shard_map/jit(_pad)/pad | solution.py:530
  2.1 1.6 %copy-done = bf16[64,2,8192]{2,1,0:T(2,128)(2,1)S(1)} copy-done((bf16[64,2,8192]{2,1,0:T(2,128)(2,1)S(1)}, bf16[64,2,8192]{2,1,0:T(2,128)(2,1)}, u32[]{:S(2)}) %copy-start) | copy-done | bytes 2097176
  3.7 1.5 %range_compress_first.1 = (bf16[64,1024]{1,0:T(8,128)(2,1)S(1)}, bf16[64,1024]{1,0:T(8,128)(2,1)S(1)}) custom-call(s32[1]{0:T(128)} %bitcast.me_ref, bf16[64,2,8192]{2,1,0:T(2,128)(2,1)S(1)} %copy-done, f32[2,1280]{1,0:T(2,128)S(1)} %pad_convert_fusion.h_ref), custom_call_target="tpu_custom_call" | custom-call | flops 1342177280 | bytes 786432 | tf_op jit(solution)/shard_map/range_compress_first/pallas_call | solution.py:203
  5.2 2.3 %collective-permute-start.2 = (bf16[64,1024]{1,0:T(8,128)(2,1)S(1)}, bf16[64,1024]{1,0:T(8,128)(2,1)S(1)}, u32[]{:S(2)}, u32[]{:S(2)}) collective-permute-start(bf16[64,1024]{1,0:T(8,128)(2,1)S(1)} %get-tuple-element.30), channel_id=1, source_target_pairs={{0,9},{1,8},{2,11},{3,10},{4,13},{5,12},{6,15},{7,14},{8,1},{9,0},... | collective-permute-start | bytes 393224 | tf_op jit(solution)/shard_map/ppermute | solution.py:527
  7.4 0.2 collective-permute-start.1
  7.6 1.2 %range_compress.2 = (bf16[128,512]{1,0:T(8,128)(2,1)S(1)}, bf16[128,512]{1,0:T(8,128)(2,1)S(1)}) custom-call(s32[1]{0:T(128)} %bitcast.me_ref, bf16[64,2,8192]{2,1,0:T(2,128)(2,1)S(1)} %copy-done, bf16[64,2,8192]{2,1,0:T(2,128)(2,1)S(1)} %collective-permute-done.sibling_ref, f32[2,1280]{1,0:T(2,128)S(1)} %pad_convert_fusion.h_ref, ...), custom_call_target="tpu_custom_call" | custom-call | flops 1342177280 | bytes 786432 | tf_op jit(solution)/shard_map/range_compress/pallas_call | solution.py:235
  8.9 0.0 copy-start.1
  8.9 0.0 copy-start.2
  8.9 0.0 copy-start.4
  8.9 0.0 copy-start.5
  8.9 6.2 %range_compress.3 = (bf16[128,512]{1,0:T(8,128)(2,1)S(1)}, bf16[128,512]{1,0:T(8,128)(2,1)S(1)}, bf16[128,1024]{1,0:T(8,128)(2,1)S(1)}, bf16[128,512]{1,0:T(8,12...) custom-call(s32[1]{0:T(128)} %bitcast.me_ref, ...), custom_call_target="tpu_custom_call" | custom-call | flops 8053063680 | bytes 4718592 | tf_op jit(solution)/shard_map/range_compress/pallas_call | solution.py:235
  15.1 2.2 %collective-permute-start.10 = (bf16[128,512]{1,0:T(8,128)(2,1)S(1)}, bf16[128,512]{1,0:T(8,128)(2,1)S(1)}, u32[]{:S(2)}, u32[]{:S(2)}) collective-permute-start(bf16[128,512]{1,0:T(8,128)(2,1)S(1)} %get-tuple-element.37), channel_id=1, source_target_pairs={{0,10},{1,11},{2,8},{3,9},{4,14},{5,15},{6,12},{7,13},{8,2},{9,3},... | collective-permute-start | bytes 393224 | tf_op jit(solution)/shard_map/ppermute | solution.py:527
  17.3 1.3 %collective-permute-start.5 = (bf16[128,1024]{1,0:T(8,128)(2,1)S(1)}, bf16[128,1024]{1,0:T(8,128)(2,1)S(1)}, u32[]{:S(2)}, u32[]{:S(2)}) collective-permute-start(bf16[128,1024]{1,0:T(8,128)(2,1)S(1)} %get-tuple-element.32), channel_id=1, source_target_pairs={{0,2},{1,3},{2,0},{3,1},{4,6},{5,7},{6,4},{7,5},{8,10},{9,11},{10,... | collective-permute-start | bytes 786440 | tf_op jit(solution)/shard_map/ppermute | solution.py:527
  18.6 0.2 collective-permute-start.7
  18.7 1.2 %collective-permute-start.8 = (bf16[128,1024]{1,0:T(8,128)(2,1)S(1)}, bf16[128,1024]{1,0:T(8,128)(2,1)S(1)}, u32[]{:S(2)}, u32[]{:S(2)}) collective-permute-start(bf16[128,1024]{1,0:T(8,128)(2,1)S(1)} %get-tuple-element.35), channel_id=1, source_target_pairs={{0,6},{1,7},{2,4},{3,5},{4,2},{5,3},{6,0},{7,1},{8,14},{9,15},{10,... | collective-permute-start | bytes 786440 | tf_op jit(solution)/shard_map/ppermute | solution.py:527
  20.0 1.8 %collective-permute-done.1.refs_0_ = bf16[64,1024]{1,0:T(8,128)(2,1)S(1)} collective-permute-done((bf16[64,1024]{1,0:T(8,128)(2,1)S(1)}, bf16[64,1024]{1,0:T(8,128)(2,1)S(1)}, u32[]{:S(2)}, u32[]{:S(2)}) %collective-permute-start.1) | collective-permute-done | bytes 131104 | tf_op jit(solution)/shard_map/ppermute | solution.py:527
  21.8 2.9 %collective-permute-done.10.refs_3_ = bf16[128,512]{1,0:T(8,128)(2,1)S(1)} collective-permute-done((bf16[128,512]{1,0:T(8,128)(2,1)S(1)}, bf16[128,512]{1,0:T(8,128)(2,1)S(1)}, u32[]{:S(2)}, u32[]{:S(2)}) %collective-permute-start.10) | collective-permute-done | bytes 131104 | tf_op jit(solution)/shard_map/ppermute | solution.py:527
  24.7 0.0 copy-start.3
  24.7 0.0 copy-start.6
  24.8 1.9 %tables.1 = (bf16[4,512,32]{2,1,0:T(8,128)(2,1)S(1)}, bf16[64,1024]{1,0:T(8,128)(2,1)S(1)}, bf16[48,512]{1,0:T(8,128)(2,1)S(1)}, f32[32,64]{1,0:T(8,128)S(1)}) custom-call(s32[1]{0:T(128)} %bitcast.me_ref, bf16[16,2,512]{2,1,0:T(2,128)(2,1)S(1)} %copy-done.1, s32[1,64]{1,0:T(1,128)S(1)} %bitcast.8, s32[1,512]{1,0:T(1,128)S(1)} %bitcast.5, ...), custom_call_target="tpu_custom_call" | custom-call | flops 2147483648 | bytes 4194304 | tf_op jit(solution)/shard_map/tables/pallas_call | solution.py:343
  26.7 2.3 %collective-permute-done.11.refs_5_ = bf16[128,512]{1,0:T(8,128)(2,1)S(1)} collective-permute-done((bf16[128,512]{1,0:T(8,128)(2,1)S(1)}, bf16[128,512]{1,0:T(8,128)(2,1)S(1)}, u32[]{:S(2)}, u32[]{:S(2)}) %collective-permute-start.11) | collective-permute-done | bytes 131104 | tf_op jit(solution)/shard_map/ppermute | solution.py:527
  28.9 2.2 %collective-permute-start.3 = (bf16[128,512]{1,0:T(8,128)(2,1)S(1)}, bf16[128,512]{1,0:T(8,128)(2,1)S(1)}, u32[]{:S(2)}, u32[]{:S(2)}) collective-permute-start(bf16[128,512]{1,0:T(8,128)(2,1)S(1)} %get-tuple-element.25.after_ref), channel_id=1, source_target_pairs={{0,12},{1,13},{2,14},{3,15},{4,8},{5,9},{6,10},{7,11},{8,4},{9,5},... | collective-permute-start | bytes 393224 | tf_op jit(solution)/shard_map/ppermute | solution.py:527
  31.1 1.3 %collective-permute-done.9.refs_2_ = bf16[128,512]{1,0:T(8,128)(2,1)S(1)} collective-permute-done((bf16[128,512]{1,0:T(8,128)(2,1)S(1)}, bf16[128,512]{1,0:T(8,128)(2,1)S(1)}, u32[]{:S(2)}, u32[]{:S(2)}) %collective-permute-start.9) | collective-permute-done | bytes 131104 | tf_op jit(solution)/shard_map/ppermute | solution.py:527
  32.3 8.4 %collective-permute-start.4 = (bf16[128,512]{1,0:T(8,128)(2,1)S(1)}, bf16[128,512]{1,0:T(8,128)(2,1)S(1)}, u32[]{:S(2)}, u32[]{:S(2)}) collective-permute-start(bf16[128,512]{1,0:T(8,128)(2,1)S(1)} %get-tuple-element.31), channel_id=1, source_target_pairs={{0,10},{1,11},{2,8},{3,9},{4,14},{5,15},{6,12},{7,13},{8,2},{9,3},... | collective-permute-start | bytes 393224 | tf_op jit(solution)/shard_map/ppermute | solution.py:527
  40.7 2.0 %collective-permute-start.6 = (bf16[128,512]{1,0:T(8,128)(2,1)S(1)}, bf16[128,512]{1,0:T(8,128)(2,1)S(1)}, u32[]{:S(2)}, u32[]{:S(2)}) collective-permute-start(bf16[128,512]{1,0:T(8,128)(2,1)S(1)} %get-tuple-element.33), channel_id=1, source_target_pairs={{0,14},{1,15},{2,12},{3,13},{4,10},{5,11},{6,8},{7,9},{8,6},{9,7},... | collective-permute-start | bytes 393224 | tf_op jit(solution)/shard_map/ppermute | solution.py:527
  42.7 4.9 %azimuth_focus.2 = (bf16[256,4,2,512]{3,2,1,0:T(2,128)(2,1)}, f32[32,64]{1,0:T(8,128)S(1)}, f32[1,64]{1,0:T(1,128)S(1)}, f32[1,64]{1,0:T(1,128)S(1)}) custom-call(s32[1]{0:T(128)} %bitcast.me_ref, bf16[4,512,512]{2,1,0:T(8,128)(2,1)S(1)} %copy-done.5, bf16[4,512,512]{2,1,0:T(8,128)(2,1)S(1)} %copy-done.6, ...), custom_call_target="tpu_custom_call" | custom-call | flops 4294967296 | bytes 4194304 | tf_op jit(solution)/shard_map/azimuth_focus/pallas_call | solution.py:472
  47.6 5.7 %collective-permute-start.12 = (f32[1,64]{1,0:T(1,128)S(1)}, f32[1,64]{1,0:T(1,128)S(1)}, u32[]{:S(2)}, u32[]{:S(2)}) collective-permute-start(f32[1,64]{1,0:T(1,128)S(1)} %get-tuple-element.41), channel_id=1, source_target_pairs={{0,1},{1,2},{2,3},{3,4},{4,5},{5,6},{6,7},{7,8},{8,9},{9,10},{10,1... | collective-permute-start | bytes 776 | tf_op jit(solution)/shard_map/ppermute | solution.py:558
  53.3 1.9 %collective-permute-start.13 = (f32[1,64]{1,0:T(1,128)S(1)}, f32[1,64]{1,0:T(1,128)S(1)}, u32[]{:S(2)}, u32[]{:S(2)}) collective-permute-start(f32[1,64]{1,0:T(1,128)S(1)} %get-tuple-element.42), channel_id=1, source_target_pairs={{1,0},{2,1},{3,2},{4,3},{5,4},{6,5},{7,6},{8,7},{9,8},{10,9},{11,1... | collective-permute-start | bytes 776 | tf_op jit(solution)/shard_map/ppermute | solution.py:557
  55.3 0.9 %collective-permute-done.6.refs_5_ = bf16[128,512]{1,0:T(8,128)(2,1)S(1)} collective-permute-done((bf16[128,512]{1,0:T(8,128)(2,1)S(1)}, bf16[128,512]{1,0:T(8,128)(2,1)S(1)}, u32[]{:S(2)}, u32[]{:S(2)}) %collective-permute-start.6) | collective-permute-done | bytes 131104 | tf_op jit(solution)/shard_map/ppermute | solution.py:527
  56.2 4.7 %azimuth_focus.3 = (bf16[256,4,2,512]{3,2,1,0:T(2,128)(2,1)}, f32[32,64]{1,0:T(8,128)S(1)}) custom-call(s32[1]{0:T(128)} %bitcast.me_ref, bf16[4,512,512]{2,1,0:T(8,128)(2,1)S(1)} %copy-done.5, bf16[4,512,512]{2,1,0:T(8,128)(2,1)S(1)} %copy-done.6, bf16[4,512,32]{2,1,0:T(8,128)(2,1)S(1)} %get-tuple-element.27.spectra_ref, ...), custom_call_target="tpu_custom_call", output_to_operand_aliasing={{0}: (16, {})} | custom-call | flops 4294967296 | bytes 4194304 | tf_op jit(solution)/shard_map/azimuth_focus/pallas_call | solution.py:472
  60.9 0.6 %looks.1 = f32[32,64]{1,0:T(8,128)} custom-call(f32[1,64]{1,0:T(1,128)S(1)} %collective-permute-done.12.from_left_ref, f32[1,64]{1,0:T(1,128)S(1)} %collective-permute-done.13.from_right_ref, f32[32,64]{1,0:T(8,128)S(1)} %get-tuple-element.43.inside_ref, f32[32,64]{1,0:T(8,128)S(1)} %get-tuple-element.44.refs_0_, f32[32,64]{1,0:T(8,128)S(1)} %get-tuple-element.45.refs_1_), custom_call_target="tpu_custom_call" | custom-call | flops 1048576 | bytes 65536 | tf_op jit(solution)/shard_map/looks/pallas_call | solution.py:503
  (18 shorter events, 0.0 us)
Async XLA Ops:
  0.6 7.0 %collective-permute-start = (bf16[64,2,8192]{2,1,0:T(2,128)(2,1)}, bf16[64,2,8192]{2,1,0:T(2,128)(2,1)S(1)}, u32[]{:S(2)}, u32[]{:S(2)}) collective-permute-start(bf16[64,2,8192]{2,1,0:T(2,128)(2,1)} %x_ref.3), channel_id=1, source_target_pairs={{0,1},{1,0},{2,3},{3,2},{4,5},{5,4},{6,7},{7,6},{8,9},{9,8},{10,11... | collective-permute-start | bytes 6291464 | tf_op jit(solution)/shard_map/ppermute | solution.py:527
  2.1 1.6 %copy-start = (bf16[64,2,8192]{2,1,0:T(2,128)(2,1)S(1)}, bf16[64,2,8192]{2,1,0:T(2,128)(2,1)}, u32[]{:S(2)}) copy-start(bf16[64,2,8192]{2,1,0:T(2,128)(2,1)} %x_ref.3) | copy-start | bytes 6291460
  5.2 13.6 %collective-permute-start.2 = (bf16[64,1024]{1,0:T(8,128)(2,1)S(1)}, bf16[64,1024]{1,0:T(8,128)(2,1)S(1)}, u32[]{:S(2)}, u32[]{:S(2)}) collective-permute-start(bf16[64,1024]{1,0:T(8,128)(2,1)S(1)} %get-tuple-element.30), channel_id=1, source_target_pairs={{0,9},{1,8},{2,11},{3,10},{4,13},{5,12},{6,15},{7,14},{8,1},{9,0},... | collective-permute-start | bytes 393224 | tf_op jit(solution)/shard_map/ppermute | solution.py:527
  7.4 14.4 %collective-permute-start.1 = (bf16[64,1024]{1,0:T(8,128)(2,1)S(1)}, bf16[64,1024]{1,0:T(8,128)(2,1)S(1)}, u32[]{:S(2)}, u32[]{:S(2)}) collective-permute-start(bf16[64,1024]{1,0:T(8,128)(2,1)S(1)} %get-tuple-element.24.after_ref), channel_id=1, source_target_pairs={{0,8},{1,9},{2,10},{3,11},{4,12},{5,13},{6,14},{7,15},{8,0},{9,1},... | collective-permute-start | bytes 393224 | tf_op jit(solution)/shard_map/ppermute | solution.py:527
  8.9 15.9 %copy-start.1 = (bf16[16,2,512]{2,1,0:T(2,128)(2,1)S(1)}, bf16[16,2,512]{2,1,0:T(2,128)(2,1)}, u32[]{:S(2)}) copy-start(bf16[16,2,512]{2,1,0:T(2,128)(2,1)} %taps_ref.1) | copy-start | bytes 98308
  8.9 15.8 %copy-start.2 = (s32[512]{0:T(512)S(1)}, s32[512]{0:T(512)}, u32[]{:S(2)}) copy-start(s32[512]{0:T(512)} %param.13) | copy-start | bytes 6148
  8.9 15.8 %copy-start.4 = (s32[64]{0:T(128)S(1)}, s32[64]{0:T(128)}, u32[]{:S(2)}) copy-start(s32[64]{0:T(128)} %param.12) | copy-start | bytes 772
  8.9 15.8 %copy-start.5 = (bf16[4,512,512]{2,1,0:T(8,128)(2,1)S(1)}, bf16[4,512,512]{2,1,0:T(8,128)(2,1)}, u32[]{:S(2)}) copy-start(bf16[4,512,512]{2,1,0:T(8,128)(2,1)} %constant.12.clone.matrix_ref.forward_ref) | copy-start | bytes 6291460
  15.1 9.6 %collective-permute-start.10 = (bf16[128,512]{1,0:T(8,128)(2,1)S(1)}, bf16[128,512]{1,0:T(8,128)(2,1)S(1)}, u32[]{:S(2)}, u32[]{:S(2)}) collective-permute-start(bf16[128,512]{1,0:T(8,128)(2,1)S(1)} %get-tuple-element.37), channel_id=1, source_target_pairs={{0,10},{1,11},{2,8},{3,9},{4,14},{5,15},{6,12},{7,13},{8,2},{9,3},... | collective-permute-start | bytes 393224 | tf_op jit(solution)/shard_map/ppermute | solution.py:527
  17.3 23.4 %collective-permute-start.5 = (bf16[128,1024]{1,0:T(8,128)(2,1)S(1)}, bf16[128,1024]{1,0:T(8,128)(2,1)S(1)}, u32[]{:S(2)}, u32[]{:S(2)}) collective-permute-start(bf16[128,1024]{1,0:T(8,128)(2,1)S(1)} %get-tuple-element.32), channel_id=1, source_target_pairs={{0,2},{1,3},{2,0},{3,1},{4,6},{5,7},{6,4},{7,5},{8,10},{9,11},{10,... | collective-permute-start | bytes 786440 | tf_op jit(solution)/shard_map/ppermute | solution.py:527
  18.6 24.1 %collective-permute-start.7 = (bf16[128,1024]{1,0:T(8,128)(2,1)S(1)}, bf16[128,1024]{1,0:T(8,128)(2,1)S(1)}, u32[]{:S(2)}, u32[]{:S(2)}) collective-permute-start(bf16[128,1024]{1,0:T(8,128)(2,1)S(1)} %get-tuple-element.34), channel_id=1, source_target_pairs={{0,4},{1,5},{2,6},{3,7},{4,0},{5,1},{6,2},{7,3},{8,12},{9,13},{10,... | collective-permute-start | bytes 786440 | tf_op jit(solution)/shard_map/ppermute | solution.py:527
  18.7 23.9 %collective-permute-start.8 = (bf16[128,1024]{1,0:T(8,128)(2,1)S(1)}, bf16[128,1024]{1,0:T(8,128)(2,1)S(1)}, u32[]{:S(2)}, u32[]{:S(2)}) collective-permute-start(bf16[128,1024]{1,0:T(8,128)(2,1)S(1)} %get-tuple-element.35), channel_id=1, source_target_pairs={{0,6},{1,7},{2,4},{3,5},{4,2},{5,3},{6,0},{7,1},{8,14},{9,15},{10,... | collective-permute-start | bytes 786440 | tf_op jit(solution)/shard_map/ppermute | solution.py:527
  21.8 7.1 %collective-permute-start.11 = (bf16[128,512]{1,0:T(8,128)(2,1)S(1)}, bf16[128,512]{1,0:T(8,128)(2,1)S(1)}, u32[]{:S(2)}, u32[]{:S(2)}) collective-permute-start(bf16[128,512]{1,0:T(8,128)(2,1)S(1)} %get-tuple-element.38), channel_id=1, source_target_pairs={{0,14},{1,15},{2,12},{3,13},{4,10},{5,11},{6,8},{7,9},{8,6},{9,7},... | collective-permute-start | bytes 393224 | tf_op jit(solution)/shard_map/ppermute | solution.py:527
  24.7 7.6 %collective-permute-start.9 = (bf16[128,512]{1,0:T(8,128)(2,1)S(1)}, bf16[128,512]{1,0:T(8,128)(2,1)S(1)}, u32[]{:S(2)}, u32[]{:S(2)}) collective-permute-start(bf16[128,512]{1,0:T(8,128)(2,1)S(1)} %get-tuple-element.36), channel_id=1, source_target_pairs={{0,12},{1,13},{2,14},{3,15},{4,8},{5,9},{6,10},{7,11},{8,4},{9,5},... | collective-permute-start | bytes 393224 | tf_op jit(solution)/shard_map/ppermute | solution.py:527
  24.7 18.0 %copy-start.3 = (s32[512]{0:T(512)S(1)}, s32[512]{0:T(512)}, u32[]{:S(2)}) copy-start(s32[512]{0:T(512)} %param.11) | copy-start | bytes 6148
  24.7 18.0 %copy-start.6 = (bf16[4,512,512]{2,1,0:T(8,128)(2,1)S(1)}, bf16[4,512,512]{2,1,0:T(8,128)(2,1)}, u32[]{:S(2)}) copy-start(bf16[4,512,512]{2,1,0:T(8,128)(2,1)} %constant.13.clone.inverse_ref) | copy-start | bytes 6291460
  28.9 27.2 %collective-permute-start.3 = (bf16[128,512]{1,0:T(8,128)(2,1)S(1)}, bf16[128,512]{1,0:T(8,128)(2,1)S(1)}, u32[]{:S(2)}, u32[]{:S(2)}) collective-permute-start(bf16[128,512]{1,0:T(8,128)(2,1)S(1)} %get-tuple-element.25.after_ref), channel_id=1, source_target_pairs={{0,12},{1,13},{2,14},{3,15},{4,8},{5,9},{6,10},{7,11},{8,4},{9,5},... | collective-permute-start | bytes 393224 | tf_op jit(solution)/shard_map/ppermute | solution.py:527
  32.3 22.9 %collective-permute-start.4 = (bf16[128,512]{1,0:T(8,128)(2,1)S(1)}, bf16[128,512]{1,0:T(8,128)(2,1)S(1)}, u32[]{:S(2)}, u32[]{:S(2)}) collective-permute-start(bf16[128,512]{1,0:T(8,128)(2,1)S(1)} %get-tuple-element.31), channel_id=1, source_target_pairs={{0,10},{1,11},{2,8},{3,9},{4,14},{5,15},{6,12},{7,13},{8,2},{9,3},... | collective-permute-start | bytes 393224 | tf_op jit(solution)/shard_map/ppermute | solution.py:527
  40.7 15.4 %collective-permute-start.6 = (bf16[128,512]{1,0:T(8,128)(2,1)S(1)}, bf16[128,512]{1,0:T(8,128)(2,1)S(1)}, u32[]{:S(2)}, u32[]{:S(2)}) collective-permute-start(bf16[128,512]{1,0:T(8,128)(2,1)S(1)} %get-tuple-element.33), channel_id=1, source_target_pairs={{0,14},{1,15},{2,12},{3,13},{4,10},{5,11},{6,8},{7,9},{8,6},{9,7},... | collective-permute-start | bytes 393224 | tf_op jit(solution)/shard_map/ppermute | solution.py:527
  47.6 13.3 %collective-permute-start.12 = (f32[1,64]{1,0:T(1,128)S(1)}, f32[1,64]{1,0:T(1,128)S(1)}, u32[]{:S(2)}, u32[]{:S(2)}) collective-permute-start(f32[1,64]{1,0:T(1,128)S(1)} %get-tuple-element.41), channel_id=1, source_target_pairs={{0,1},{1,2},{2,3},{3,4},{4,5},{5,6},{6,7},{7,8},{8,9},{9,10},{10,1... | collective-permute-start | bytes 776 | tf_op jit(solution)/shard_map/ppermute | solution.py:558
  53.3 7.5 %collective-permute-start.13 = (f32[1,64]{1,0:T(1,128)S(1)}, f32[1,64]{1,0:T(1,128)S(1)}, u32[]{:S(2)}, u32[]{:S(2)}) collective-permute-start(f32[1,64]{1,0:T(1,128)S(1)} %get-tuple-element.42), channel_id=1, source_target_pairs={{1,0},{2,1},{3,2},{4,3},{5,4},{6,5},{7,6},{8,7},{9,8},{10,9},{11,1... | collective-permute-start | bytes 776 | tf_op jit(solution)/shard_map/ppermute | solution.py:557

commit v4 on v3

--- a/solution.py
+++ b/solution.py
@@ -273,7 +273,7 @@
 
 
 def tables_kernel(
-    me_ref, taps_ref, azimuth_ref, range_ref, matrix_ref, after_ref,
+    me_ref, taps_ref, index_ref, azimuth_ref, range_ref, matrix_ref, after_ref,
     spectra_ref, pulse_ref, mask_ref, inside_ref,
 ):
     del after_ref
@@ -287,6 +287,9 @@
     taps = dot(place.astype(F32).astype(BF16), taps).astype(BF16)
     m = lax.broadcasted_iota(jnp.int32, (part, tap_count), 0)
     tap = lax.broadcasted_iota(jnp.int32, (part, tap_count), 1)
+    bins = index_ref.shape[1]
+    row = lax.broadcasted_iota(jnp.int32, (2 * replicas, bins), 0)
+    chosen = (row % replicas == index_ref[...]).astype(F32).astype(BF16)
     values = []
     for q in range(RADIX):
         pick = (tap == RADIX * m + q).astype(F32).astype(BF16)
@@ -294,7 +297,8 @@
     for r in range(RADIX):
         spectrum = jnp.concatenate(spectrum_part(values, r), axis=0) * (1.0 / length)
         high, low = split(spectrum)
-        spectra_ref[r] = jnp.concatenate([high[:, :replicas], low[:, :replicas]], axis=1)
+        both = jnp.concatenate([high[:, :replicas], low[:, :replicas]], axis=1)
+        spectra_ref[r] = dot(both, chosen)
 
     def mask(starts, stops, at):
         at = at.astype(F32)
@@ -327,7 +331,7 @@
     inside_ref[...] = count[:tiles] * pulse_count
 
 
-def make_tables(me, azimuth_replicas, azimuth_extent, range_extent, matrix, after, width):
+def make_tables(me, azimuth_replicas, index, azimuth_extent, range_extent, matrix, after, width):
     part = matrix.shape[1] // 2
     replicas = azimuth_replicas.shape[0]
     pulse_tiles = azimuth_extent.shape[0]
@@ -335,7 +339,7 @@
     mask_rows = -(-(tiles + 2) // 16) * 16
     vmem = pl.BlockSpec(memory_space=pltpu.VMEM)
     shapes = [
-        ((RADIX, 2 * part, 2 * replicas), BF16),
+        ((RADIX, 2 * part, width), F32),
         ((pulse_tiles, RADIX * part), BF16),
         ((mask_rows, width), BF16),
         ((tiles, pulse_tiles), F32),
@@ -343,12 +347,12 @@
     return pl.pallas_call(
         tables_kernel,
         out_shape=[jax.ShapeDtypeStruct(*shape) for shape in shapes],
-        in_specs=[pl.BlockSpec(memory_space=pltpu.SMEM)] + [vmem] * 4 + [pl.BlockSpec(memory_space=pl.ANY)],
+        in_specs=[pl.BlockSpec(memory_space=pltpu.SMEM)] + [vmem] * 5 + [pl.BlockSpec(memory_space=pl.ANY)],
         out_specs=[vmem] * 4,
         compiler_params=pltpu.CompilerParams(vmem_limit_bytes=RANGE_VMEM),
         cost_estimate=pl.CostEstimate(flops=1 << 31, bytes_accessed=4 << 20, transcendentals=0),
         name="tables",
-    )(me, azimuth_replicas, azimuth_extent[None, :], range_extent[None, :], matrix, after)
+    )(me, azimuth_replicas, index, azimuth_extent[None, :], range_extent[None, :], matrix, after)
 
 
 def gather_pulses(offsets, places, n, sources, me, total, x_ref):
@@ -378,7 +382,7 @@
 
 
 def focus_kernel(
-    offsets, places, cells, first, me_ref, forward_ref, inverse_ref, spectra_ref, index_ref, pulse_ref, range_ref, *refs
+    offsets, places, cells, first, me_ref, forward_ref, inverse_ref, spectra_ref, pulse_ref, range_ref, *refs
 ):
     sources, refs = refs[: len(offsets)], refs[len(offsets) :]
     if first:
@@ -394,8 +398,6 @@
     steps = range(len(cells))
     for n in steps:
         gather_pulses(offsets, places, n, sources, me, total, x_ref.at[n])
-    replicas = spectra_ref.shape[2] // 2
-    row = lax.broadcasted_iota(jnp.int32, (2 * replicas, CELL), 0)
 
     def transform(n):
         for q in range(RADIX):
@@ -404,16 +406,14 @@
 
     def correlate_cell(n):
         lanes = slice(cells[n] * CELL, (cells[n] + 1) * CELL)
-        chosen = (row % replicas == index_ref[:, lanes]).astype(F32).astype(BF16)
         rows = part // RADIX
         for r in range(RADIX):
             span = slice(r * rows, (r + 1) * rows)
             x = butterfly([(v_ref[n, q, 0, span], v_ref[n, q, 1, span]) for q in range(RADIX)], -1)
-            replica = dot(spectra_ref[r], chosen)
             y = []
             for j, (sr, si) in enumerate(x):
-                gr = replica[j * rows : (j + 1) * rows]
-                gi = replica[part + j * rows : part + (j + 1) * rows]
+                gr = spectra_ref[r, j * rows : (j + 1) * rows, lanes]
+                gi = spectra_ref[r, part + j * rows : part + (j + 1) * rows, lanes]
                 y.append((sr * gr + si * gi, si * gr - sr * gi))
             for q, (re, im) in enumerate(butterfly(y, 1)):
                 s_ref[n, q, span, :CELL] = re.astype(BF16)
@@ -422,24 +422,24 @@
     copies = []
 
     def finish(n):
-        lanes = slice(cells[n] * CELL, (cells[n] + 1) * CELL)
+        lanes = slice(n * CELL, (n + 1) * CELL)
         for q in range(RADIX):
             re, im = complex_product(inverse_ref[q], s_ref[n, q])
             both = jnp.stack([re.astype(BF16), im.astype(BF16)], axis=0)
-            image_ref[n, q] = jnp.swapaxes(both, 0, 1)
+            image_ref[q, :, :, lanes] = jnp.swapaxes(both, 0, 1)
+            power_ref[q * part : (q + 1) * part, lanes] = (re * re + im * im).astype(BF16)
             copy = pltpu.make_async_copy(
-                image_ref.at[n, q], focused_hbm.at[:, q, :, lanes], sems.at[n, q]
+                image_ref.at[q, :, :, lanes],
+                focused_hbm.at[:, q, :, cells[n] * CELL : (cells[n] + 1) * CELL],
+                sems.at[n, q],
             )
             copy.start()
             copies.append(copy)
-            power = (re * re + im * im).astype(BF16)
-            power_ref[q * part : (q + 1) * part, n * CELL : (n + 1) * CELL] = power
 
     for n in steps:
         transform(n)
     for n in steps:
         correlate_cell(n)
-    for n in steps:
         finish(n)
     sums = dot(pulse_ref[...], power_ref[...])
     high, low = split(sums)
@@ -454,13 +454,13 @@
 
 
 def focus(first, cells, places, pulses, width, tiles, tables, sources, more):
-    me, forward, inverse, spectra, index, pulse_mask, range_mask = tables
+    me, forward, inverse, spectra, pulse_mask, range_mask = tables
     pulse_tiles = pulse_mask.shape[0]
     part = pulses // RADIX
     offsets = list(sources)
     vmem = pl.BlockSpec(memory_space=pltpu.VMEM)
     anywhere = pl.BlockSpec(memory_space=pl.ANY)
-    in_specs = [pl.BlockSpec(memory_space=pltpu.SMEM)] + [vmem] * (6 + len(offsets))
+    in_specs = [pl.BlockSpec(memory_space=pltpu.SMEM)] + [vmem] * (5 + len(offsets))
     shapes = [jax.ShapeDtypeStruct((part, RADIX, 2, width), BF16)]
     shapes += [jax.ShapeDtypeStruct((tiles, pulse_tiles), F32)]
     if first:
@@ -479,16 +479,16 @@
             pltpu.VMEM((len(cells), RADIX, 2, part, CELL), F32),
             pltpu.VMEM((len(cells), RADIX, part, 2 * CELL), BF16),
             pltpu.VMEM((pulses, len(cells) * CELL), BF16),
-            pltpu.VMEM((len(cells), RADIX, part, 2, CELL), BF16),
+            pltpu.VMEM((RADIX, part, 2, len(cells) * CELL), BF16),
             pltpu.SemaphoreType.DMA((len(cells), RADIX)),
         ],
-        input_output_aliases={} if first else {7 + len(offsets): 0},
+        input_output_aliases={} if first else {6 + len(offsets): 0},
         compiler_params=pltpu.CompilerParams(vmem_limit_bytes=FOCUS_VMEM),
         cost_estimate=pl.CostEstimate(
             flops=len(cells) << 31, bytes_accessed=len(cells) << 21, transcendentals=0
         ),
         name="azimuth_focus",
-    )(me, forward, inverse, spectra, index, pulse_mask, range_mask, *sources.values(), *more)
+    )(me, forward, inverse, spectra, pulse_mask, range_mask, *sources.values(), *more)
 
 
 def looks_kernel(from_left_ref, from_right_ref, inside_ref, *refs):
@@ -530,14 +530,14 @@
     replica = jnp.pad(range_replica.astype(F32), ((0, 0), (0, min(256, width))))
     if chunked:
         late = ()
-        late = (12, 10, 14)
+        late = (10, 14, 12)
         first = compress_first(me, echoes, replica, [8, 9], width)
         received = {offset: send(piece, offset) for offset, piece in first.items()}
         pieces = compress(me, echoes, sibling, replica, first[8], [12], late, width)
         others = [10, 2, 14, 4, 6, 0]
         pieces.update(compress(me, echoes, sibling, replica, pieces[12][1], others, late, width))
         received.update({offset: send(pieces[offset][0], offset) for offset in [12] + others})
-        received_late = {offset: send(pieces[offset][1], offset) for offset in late}
+        received_late = {offset: send(pieces[offset][1], offset) for offset in (10, 14, 12)}
     else:
         late = ()
         pieces = compress(me, echoes, sibling, replica, me, list(range(2, count, 2)) + [0], late, width)
@@ -546,9 +546,9 @@
     forward, inverse = (jnp.asarray(m) for m in phase_matrices(pulses))
     tiles = width // TILE
     spectra, pulse_mask, range_mask, inside = make_tables(
-        me, azimuth_replicas, azimuth_extent, range_extent, forward, received[0], width
+        me, azimuth_replicas, replica_index[None, :], azimuth_extent, range_extent, forward, received[0], width
     )
-    tables = (me, forward, inverse, spectra, replica_index[None, :], pulse_mask, range_mask)
+    tables = (me, forward, inverse, spectra, pulse_mask, range_mask)
     early = [cell for cell in cells if not (chunked and cell in LATE)]
     places = {offset: list(range(len(early))) if offset in late else early for offset in received}
     focused, sums, left, right = focus(

time: 61.8 us -> 61 us (0.987)
  Pallas kernels: 21 us -> 20 us
    pallas_call x2, Pallas kernels: 9.55 us -> 8 us  [focus(): pl.pallas_call(functools.partial(focus_kernel, tuple(offsets), places, tu...]
  transfers between devices with their start and end apart: 14 -> 14, of which waited for: 5 -> 5; matrix products, arithmetic and copies ran while one was open for 1% -> 1% of each run, Pallas kernels for 33% -> 32%
where the time goes in v4:
time: 61 us; the launch traced here: 60.7 us
  starting transfers between devices  28.1 us (46%)
  Pallas kernels  20 us (33%)
  waiting for transfers between devices  9.48 us (16%)
  local copies, waits for them, and re-layouts  1.63 us (3%)
  between operations  0.8 us (1%)
  other arithmetic  0.69 us (1%)
    ppermute x12, starting transfers between devices, send(): return lax.ppermute(piece, 'row', [(i, i ^ offset) for i in range(count)])  20.5 us
    ppermute x12, waiting for transfers between devices, send(): return lax.ppermute(piece, 'row', [(i, i ^ offset) for i in range(count)])  9.48 us
    pallas_call x2, Pallas kernels, focus(): pl.pallas_call(functools.partial(focus_kernel, tuple(offsets), places, tu...  8 us
    pallas_call x2, Pallas kernels, compress(): pl.pallas_call(functools.partial(range_kernel, tuple(offsets), late, widt...  7.47 us
    ppermute x1, starting transfers between devices, per_device(): lax.ppermute(right, 'row', [(i, i + 1) for i in range(count - 1)])  5.73 us
    pallas_call x1, Pallas kernels, make_tables(): pl.pallas_call(tables_kernel, out_shape=[jax.ShapeDtypeStruct(*shape) for...  2.4 us
    ppermute x1, starting transfers between devices, per_device(): lax.ppermute(left, 'row', [(i, i - 1) for i in range(1, count)])  1.92 us
    unnamed x14, local copies, waits for them, and re-layouts  1.63 us
  transfers between devices with their start and end apart: 14, of which 5 were waited for; matrix products, arithmetic and copies ran while one was open for 1% of the time, Pallas kernels for 32%

profile of v4, /device:TPU:13, one launch (start us, length us, event | category | flops | bytes accessed | tf_op | source)
XLA Modules:
  0.0 60.7 jit_solution(6679113710743050374)
XLA Ops:
  0.6 0.7 %collective-permute-start = (bf16[64,2,8192]{2,1,0:T(2,128)(2,1)}, bf16[64,2,8192]{2,1,0:T(2,128)(2,1)S(1)}, u32[]{:S(2)}, u32[]{:S(2)}) collective-permute-start(bf16[64,2,8192]{2,1,0:T(2,128)(2,1)} %x_ref.3), channel_id=1, source_target_pairs={{0,1},{1,0},{2,3},{3,2},{4,5},{5,4},{6,7},{7,6},{8,9},{9,8},{10,11... | collective-permute-start | bytes 6291464 | tf_op jit(solution)/shard_map/ppermute | solution.py:527
  1.4 0.7 %pad_convert_fusion.h_ref = f32[2,1280]{1,0:T(2,128)S(1)} fusion(bf16[2,1024]{1,0:T(2,128)(2,1)} %param.9), kind=kLoop, calls=%fused_computation | loop fusion | flops 2560 | bytes 14336 | tf_op jit(solution)/shard_map/jit(_pad)/pad | solution.py:530
  2.1 1.6 %copy-done = bf16[64,2,8192]{2,1,0:T(2,128)(2,1)S(1)} copy-done((bf16[64,2,8192]{2,1,0:T(2,128)(2,1)S(1)}, bf16[64,2,8192]{2,1,0:T(2,128)(2,1)}, u32[]{:S(2)}) %copy-start) | copy-done | bytes 2097176
  3.7 1.5 %range_compress_first.1 = (bf16[64,1024]{1,0:T(8,128)(2,1)S(1)}, bf16[64,1024]{1,0:T(8,128)(2,1)S(1)}) custom-call(s32[1]{0:T(128)} %bitcast.me_ref, bf16[64,2,8192]{2,1,0:T(2,128)(2,1)S(1)} %copy-done, f32[2,1280]{1,0:T(2,128)S(1)} %pad_convert_fusion.h_ref), custom_call_target="tpu_custom_call" | custom-call | flops 1342177280 | bytes 786432 | tf_op jit(solution)/shard_map/range_compress_first/pallas_call | solution.py:203
  5.2 2.3 %collective-permute-start.2 = (bf16[64,1024]{1,0:T(8,128)(2,1)S(1)}, bf16[64,1024]{1,0:T(8,128)(2,1)S(1)}, u32[]{:S(2)}, u32[]{:S(2)}) collective-permute-start(bf16[64,1024]{1,0:T(8,128)(2,1)S(1)} %get-tuple-element.30), channel_id=1, source_target_pairs={{0,9},{1,8},{2,11},{3,10},{4,13},{5,12},{6,15},{7,14},{8,1},{9,0},... | collective-permute-start | bytes 393224 | tf_op jit(solution)/shard_map/ppermute | solution.py:527
  7.4 0.2 collective-permute-start.1
  7.6 1.2 %range_compress.2 = (bf16[128,512]{1,0:T(8,128)(2,1)S(1)}, bf16[128,512]{1,0:T(8,128)(2,1)S(1)}) custom-call(s32[1]{0:T(128)} %bitcast.me_ref, bf16[64,2,8192]{2,1,0:T(2,128)(2,1)S(1)} %copy-done, bf16[64,2,8192]{2,1,0:T(2,128)(2,1)S(1)} %collective-permute-done.sibling_ref, f32[2,1280]{1,0:T(2,128)S(1)} %pad_convert_fusion.h_ref, ...), custom_call_target="tpu_custom_call" | custom-call | flops 1342177280 | bytes 786432 | tf_op jit(solution)/shard_map/range_compress/pallas_call | solution.py:235
  8.9 0.0 copy-start.1
  8.9 0.0 copy-start.2
  8.9 0.0 copy-start.3
  8.9 0.0 copy-start.4
  8.9 0.0 copy-start.5
  8.9 6.2 %range_compress.3 = (bf16[128,512]{1,0:T(8,128)(2,1)S(1)}, bf16[128,512]{1,0:T(8,128)(2,1)S(1)}, bf16[128,1024]{1,0:T(8,128)(2,1)S(1)}, bf16[128,512]{1,0:T(8,12...) custom-call(s32[1]{0:T(128)} %bitcast.me_ref, ...), custom_call_target="tpu_custom_call" | custom-call | flops 8053063680 | bytes 4718592 | tf_op jit(solution)/shard_map/range_compress/pallas_call | solution.py:235
  15.2 2.2 %collective-permute-start.10 = (bf16[128,512]{1,0:T(8,128)(2,1)S(1)}, bf16[128,512]{1,0:T(8,128)(2,1)S(1)}, u32[]{:S(2)}, u32[]{:S(2)}) collective-permute-start(bf16[128,512]{1,0:T(8,128)(2,1)S(1)} %get-tuple-element.37), channel_id=1, source_target_pairs={{0,10},{1,11},{2,8},{3,9},{4,14},{5,15},{6,12},{7,13},{8,2},{9,3},... | collective-permute-start | bytes 393224 | tf_op jit(solution)/shard_map/ppermute | solution.py:527
  17.3 1.3 %collective-permute-start.5 = (bf16[128,1024]{1,0:T(8,128)(2,1)S(1)}, bf16[128,1024]{1,0:T(8,128)(2,1)S(1)}, u32[]{:S(2)}, u32[]{:S(2)}) collective-permute-start(bf16[128,1024]{1,0:T(8,128)(2,1)S(1)} %get-tuple-element.32), channel_id=1, source_target_pairs={{0,2},{1,3},{2,0},{3,1},{4,6},{5,7},{6,4},{7,5},{8,10},{9,11},{10,... | collective-permute-start | bytes 786440 | tf_op jit(solution)/shard_map/ppermute | solution.py:527
  18.6 0.2 collective-permute-start.7
  18.8 1.2 %collective-permute-start.8 = (bf16[128,1024]{1,0:T(8,128)(2,1)S(1)}, bf16[128,1024]{1,0:T(8,128)(2,1)S(1)}, u32[]{:S(2)}, u32[]{:S(2)}) collective-permute-start(bf16[128,1024]{1,0:T(8,128)(2,1)S(1)} %get-tuple-element.35), channel_id=1, source_target_pairs={{0,6},{1,7},{2,4},{3,5},{4,2},{5,3},{6,0},{7,1},{8,14},{9,15},{10,... | collective-permute-start | bytes 786440 | tf_op jit(solution)/shard_map/ppermute | solution.py:527
  20.0 1.8 %collective-permute-done.1.refs_0_ = bf16[64,1024]{1,0:T(8,128)(2,1)S(1)} collective-permute-done((bf16[64,1024]{1,0:T(8,128)(2,1)S(1)}, bf16[64,1024]{1,0:T(8,128)(2,1)S(1)}, u32[]{:S(2)}, u32[]{:S(2)}) %collective-permute-start.1) | collective-permute-done | bytes 131104 | tf_op jit(solution)/shard_map/ppermute | solution.py:527
  21.8 2.9 %collective-permute-done.10.refs_3_ = bf16[128,512]{1,0:T(8,128)(2,1)S(1)} collective-permute-done((bf16[128,512]{1,0:T(8,128)(2,1)S(1)}, bf16[128,512]{1,0:T(8,128)(2,1)S(1)}, u32[]{:S(2)}, u32[]{:S(2)}) %collective-permute-start.10) | collective-permute-done | bytes 131104 | tf_op jit(solution)/shard_map/ppermute | solution.py:527
  24.7 0.0 copy-start.6
  24.8 2.4 %tables.1 = (f32[4,512,512]{2,1,0:T(8,128)S(1)}, bf16[64,1024]{1,0:T(8,128)(2,1)S(1)}, bf16[48,512]{1,0:T(8,128)(2,1)S(1)}, f32[32,64]{1,0:T(8,128)S(1)}) custom-call(s32[1]{0:T(128)} %bitcast.me_ref, bf16[16,2,512]{2,1,0:T(2,128)(2,1)S(1)} %copy-done.1, s32[1,512]{1,0:T(1,128)S(1)} %bitcast.5, s32[1,64]{1,0:T(1,128)S(1)} %bitcast.7, s32[1,512]{1,0:T(1,128)S(1)} %bitcast.6, ...), custom_call_target="tpu_custom_call" | custom-call | flops 2147483648 | bytes 4194304 | tf_op jit(solution)/shard_map/tables/pallas_call | solution.py:347
  27.2 1.8 %collective-permute-done.11.refs_5_ = bf16[128,512]{1,0:T(8,128)(2,1)S(1)} collective-permute-done((bf16[128,512]{1,0:T(8,128)(2,1)S(1)}, bf16[128,512]{1,0:T(8,128)(2,1)S(1)}, u32[]{:S(2)}, u32[]{:S(2)}) %collective-permute-start.11) | collective-permute-done | bytes 131104 | tf_op jit(solution)/shard_map/ppermute | solution.py:527
  28.9 2.1 %collective-permute-start.3 = (bf16[128,512]{1,0:T(8,128)(2,1)S(1)}, bf16[128,512]{1,0:T(8,128)(2,1)S(1)}, u32[]{:S(2)}, u32[]{:S(2)}) collective-permute-start(bf16[128,512]{1,0:T(8,128)(2,1)S(1)} %get-tuple-element.25.after_ref), channel_id=1, source_target_pairs={{0,12},{1,13},{2,14},{3,15},{4,8},{5,9},{6,10},{7,11},{8,4},{9,5},... | collective-permute-start | bytes 393224 | tf_op jit(solution)/shard_map/ppermute | solution.py:527
  31.1 1.3 %collective-permute-done.9.refs_2_ = bf16[128,512]{1,0:T(8,128)(2,1)S(1)} collective-permute-done((bf16[128,512]{1,0:T(8,128)(2,1)S(1)}, bf16[128,512]{1,0:T(8,128)(2,1)S(1)}, u32[]{:S(2)}, u32[]{:S(2)}) %collective-permute-start.9) | collective-permute-done | bytes 131104 | tf_op jit(solution)/shard_map/ppermute | solution.py:527
  32.4 8.4 %collective-permute-start.4 = (bf16[128,512]{1,0:T(8,128)(2,1)S(1)}, bf16[128,512]{1,0:T(8,128)(2,1)S(1)}, u32[]{:S(2)}, u32[]{:S(2)}) collective-permute-start(bf16[128,512]{1,0:T(8,128)(2,1)S(1)} %get-tuple-element.31), channel_id=1, source_target_pairs={{0,10},{1,11},{2,8},{3,9},{4,14},{5,15},{6,12},{7,13},{8,2},{9,3},... | collective-permute-start | bytes 393224 | tf_op jit(solution)/shard_map/ppermute | solution.py:527
  40.7 2.0 %collective-permute-start.6 = (bf16[128,512]{1,0:T(8,128)(2,1)S(1)}, bf16[128,512]{1,0:T(8,128)(2,1)S(1)}, u32[]{:S(2)}, u32[]{:S(2)}) collective-permute-start(bf16[128,512]{1,0:T(8,128)(2,1)S(1)} %get-tuple-element.33), channel_id=1, source_target_pairs={{0,14},{1,15},{2,12},{3,13},{4,10},{5,11},{6,8},{7,9},{8,6},{9,7},... | collective-permute-start | bytes 393224 | tf_op jit(solution)/shard_map/ppermute | solution.py:527
  42.7 4.1 %azimuth_focus.2 = (bf16[256,4,2,512]{3,2,1,0:T(2,128)(2,1)}, f32[32,64]{1,0:T(8,128)S(1)}, f32[1,64]{1,0:T(1,128)S(1)}, f32[1,64]{1,0:T(1,128)S(1)}) custom-call(s32[1]{0:T(128)} %bitcast.me_ref, bf16[4,512,512]{2,1,0:T(8,128)(2,1)S(1)} %copy-done.5, bf16[4,512,512]{2,1,0:T(8,128)(2,1)S(1)} %copy-done.6, f32[4,512,512]{2,1,0:T(8,128)S(1)} %get-tuple-element.27.spectra_ref, ...), custom_call_target="tpu_custom_call" | custom-call | flops 4294967296 | bytes 4194304 | tf_op jit(solution)/shard_map/azimuth_focus/pallas_call | solution.py:472
  46.8 5.7 %collective-permute-start.12 = (f32[1,64]{1,0:T(1,128)S(1)}, f32[1,64]{1,0:T(1,128)S(1)}, u32[]{:S(2)}, u32[]{:S(2)}) collective-permute-start(f32[1,64]{1,0:T(1,128)S(1)} %get-tuple-element.41), channel_id=1, source_target_pairs={{0,1},{1,2},{2,3},{3,4},{4,5},{5,6},{6,7},{7,8},{8,9},{9,10},{10,1... | collective-permute-start | bytes 776 | tf_op jit(solution)/shard_map/ppermute | solution.py:558
  52.5 1.9 %collective-permute-start.13 = (f32[1,64]{1,0:T(1,128)S(1)}, f32[1,64]{1,0:T(1,128)S(1)}, u32[]{:S(2)}, u32[]{:S(2)}) collective-permute-start(f32[1,64]{1,0:T(1,128)S(1)} %get-tuple-element.42), channel_id=1, source_target_pairs={{1,0},{2,1},{3,2},{4,3},{5,4},{6,5},{7,6},{8,7},{9,8},{10,9},{11,1... | collective-permute-start | bytes 776 | tf_op jit(solution)/shard_map/ppermute | solution.py:557
  54.5 1.7 %collective-permute-done.6.refs_5_ = bf16[128,512]{1,0:T(8,128)(2,1)S(1)} collective-permute-done((bf16[128,512]{1,0:T(8,128)(2,1)S(1)}, bf16[128,512]{1,0:T(8,128)(2,1)S(1)}, u32[]{:S(2)}, u32[]{:S(2)}) %collective-permute-start.6) | collective-permute-done | bytes 131104 | tf_op jit(solution)/shard_map/ppermute | solution.py:527
  56.2 3.9 %azimuth_focus.3 = (bf16[256,4,2,512]{3,2,1,0:T(2,128)(2,1)}, f32[32,64]{1,0:T(8,128)S(1)}) custom-call(s32[1]{0:T(128)} %bitcast.me_ref, bf16[4,512,512]{2,1,0:T(8,128)(2,1)S(1)} %copy-done.5, bf16[4,512,512]{2,1,0:T(8,128)(2,1)S(1)} %copy-done.6, f32[4,512,512]{2,1,0:T(8,128)S(1)} %get-tuple-element.27.spectra_ref, ...), custom_call_target="tpu_custom_call", output_to_operand_aliasing={{0}: (15, {})} | custom-call | flops 4294967296 | bytes 4194304 | tf_op jit(solution)/shard_map/azimuth_focus/pallas_call | solution.py:472
  60.1 0.6 %looks.1 = f32[32,64]{1,0:T(8,128)} custom-call(f32[1,64]{1,0:T(1,128)S(1)} %collective-permute-done.12.from_left_ref, f32[1,64]{1,0:T(1,128)S(1)} %collective-permute-done.13.from_right_ref, f32[32,64]{1,0:T(8,128)S(1)} %get-tuple-element.43.inside_ref, f32[32,64]{1,0:T(8,128)S(1)} %get-tuple-element.44.refs_0_, f32[32,64]{1,0:T(8,128)S(1)} %get-tuple-element.45.refs_1_), custom_call_target="tpu_custom_call" | custom-call | flops 1048576 | bytes 65536 | tf_op jit(solution)/shard_map/looks/pallas_call | solution.py:503
  (18 shorter events, 0.0 us)
Async XLA Ops:
  0.6 7.0 %collective-permute-start = (bf16[64,2,8192]{2,1,0:T(2,128)(2,1)}, bf16[64,2,8192]{2,1,0:T(2,128)(2,1)S(1)}, u32[]{:S(2)}, u32[]{:S(2)}) collective-permute-start(bf16[64,2,8192]{2,1,0:T(2,128)(2,1)} %x_ref.3), channel_id=1, source_target_pairs={{0,1},{1,0},{2,3},{3,2},{4,5},{5,4},{6,7},{7,6},{8,9},{9,8},{10,11... | collective-permute-start | bytes 6291464 | tf_op jit(solution)/shard_map/ppermute | solution.py:527
  2.1 1.6 %copy-start = (bf16[64,2,8192]{2,1,0:T(2,128)(2,1)S(1)}, bf16[64,2,8192]{2,1,0:T(2,128)(2,1)}, u32[]{:S(2)}) copy-start(bf16[64,2,8192]{2,1,0:T(2,128)(2,1)} %x_ref.3) | copy-start | bytes 6291460
  5.2 13.6 %collective-permute-start.2 = (bf16[64,1024]{1,0:T(8,128)(2,1)S(1)}, bf16[64,1024]{1,0:T(8,128)(2,1)S(1)}, u32[]{:S(2)}, u32[]{:S(2)}) collective-permute-start(bf16[64,1024]{1,0:T(8,128)(2,1)S(1)} %get-tuple-element.30), channel_id=1, source_target_pairs={{0,9},{1,8},{2,11},{3,10},{4,13},{5,12},{6,15},{7,14},{8,1},{9,0},... | collective-permute-start | bytes 393224 | tf_op jit(solution)/shard_map/ppermute | solution.py:527
  7.4 14.4 %collective-permute-start.1 = (bf16[64,1024]{1,0:T(8,128)(2,1)S(1)}, bf16[64,1024]{1,0:T(8,128)(2,1)S(1)}, u32[]{:S(2)}, u32[]{:S(2)}) collective-permute-start(bf16[64,1024]{1,0:T(8,128)(2,1)S(1)} %get-tuple-element.24.after_ref), channel_id=1, source_target_pairs={{0,8},{1,9},{2,10},{3,11},{4,12},{5,13},{6,14},{7,15},{8,0},{9,1},... | collective-permute-start | bytes 393224 | tf_op jit(solution)/shard_map/ppermute | solution.py:527
  8.9 15.9 %copy-start.1 = (bf16[16,2,512]{2,1,0:T(2,128)(2,1)S(1)}, bf16[16,2,512]{2,1,0:T(2,128)(2,1)}, u32[]{:S(2)}) copy-start(bf16[16,2,512]{2,1,0:T(2,128)(2,1)} %taps_ref.1) | copy-start | bytes 98308
  8.9 15.8 %copy-start.2 = (s32[512]{0:T(512)S(1)}, s32[512]{0:T(512)}, u32[]{:S(2)}) copy-start(s32[512]{0:T(512)} %param.11) | copy-start | bytes 6148
  8.9 15.8 %copy-start.3 = (s32[512]{0:T(512)S(1)}, s32[512]{0:T(512)}, u32[]{:S(2)}) copy-start(s32[512]{0:T(512)} %param.13) | copy-start | bytes 6148
  8.9 15.8 %copy-start.4 = (s32[64]{0:T(128)S(1)}, s32[64]{0:T(128)}, u32[]{:S(2)}) copy-start(s32[64]{0:T(128)} %param.12) | copy-start | bytes 772
  8.9 15.8 %copy-start.5 = (bf16[4,512,512]{2,1,0:T(8,128)(2,1)S(1)}, bf16[4,512,512]{2,1,0:T(8,128)(2,1)}, u32[]{:S(2)}) copy-start(bf16[4,512,512]{2,1,0:T(8,128)(2,1)} %constant.12.clone.matrix_ref.forward_ref) | copy-start | bytes 6291460
  15.2 9.5 %collective-permute-start.10 = (bf16[128,512]{1,0:T(8,128)(2,1)S(1)}, bf16[128,512]{1,0:T(8,128)(2,1)S(1)}, u32[]{:S(2)}, u32[]{:S(2)}) collective-permute-start(bf16[128,512]{1,0:T(8,128)(2,1)S(1)} %get-tuple-element.37), channel_id=1, source_target_pairs={{0,10},{1,11},{2,8},{3,9},{4,14},{5,15},{6,12},{7,13},{8,2},{9,3},... | collective-permute-start | bytes 393224 | tf_op jit(solution)/shard_map/ppermute | solution.py:527
  17.3 23.4 %collective-permute-start.5 = (bf16[128,1024]{1,0:T(8,128)(2,1)S(1)}, bf16[128,1024]{1,0:T(8,128)(2,1)S(1)}, u32[]{:S(2)}, u32[]{:S(2)}) collective-permute-start(bf16[128,1024]{1,0:T(8,128)(2,1)S(1)} %get-tuple-element.32), channel_id=1, source_target_pairs={{0,2},{1,3},{2,0},{3,1},{4,6},{5,7},{6,4},{7,5},{8,10},{9,11},{10,... | collective-permute-start | bytes 786440 | tf_op jit(solution)/shard_map/ppermute | solution.py:527
  18.6 24.1 %collective-permute-start.7 = (bf16[128,1024]{1,0:T(8,128)(2,1)S(1)}, bf16[128,1024]{1,0:T(8,128)(2,1)S(1)}, u32[]{:S(2)}, u32[]{:S(2)}) collective-permute-start(bf16[128,1024]{1,0:T(8,128)(2,1)S(1)} %get-tuple-element.34), channel_id=1, source_target_pairs={{0,4},{1,5},{2,6},{3,7},{4,0},{5,1},{6,2},{7,3},{8,12},{9,13},{10,... | collective-permute-start | bytes 786440 | tf_op jit(solution)/shard_map/ppermute | solution.py:527
  18.8 23.9 %collective-permute-start.8 = (bf16[128,1024]{1,0:T(8,128)(2,1)S(1)}, bf16[128,1024]{1,0:T(8,128)(2,1)S(1)}, u32[]{:S(2)}, u32[]{:S(2)}) collective-permute-start(bf16[128,1024]{1,0:T(8,128)(2,1)S(1)} %get-tuple-element.35), channel_id=1, source_target_pairs={{0,6},{1,7},{2,4},{3,5},{4,2},{5,3},{6,0},{7,1},{8,14},{9,15},{10,... | collective-permute-start | bytes 786440 | tf_op jit(solution)/shard_map/ppermute | solution.py:527
  21.8 7.1 %collective-permute-start.11 = (bf16[128,512]{1,0:T(8,128)(2,1)S(1)}, bf16[128,512]{1,0:T(8,128)(2,1)S(1)}, u32[]{:S(2)}, u32[]{:S(2)}) collective-permute-start(bf16[128,512]{1,0:T(8,128)(2,1)S(1)} %get-tuple-element.38), channel_id=1, source_target_pairs={{0,14},{1,15},{2,12},{3,13},{4,10},{5,11},{6,8},{7,9},{8,6},{9,7},... | collective-permute-start | bytes 393224 | tf_op jit(solution)/shard_map/ppermute | solution.py:527
  24.7 7.7 %collective-permute-start.9 = (bf16[128,512]{1,0:T(8,128)(2,1)S(1)}, bf16[128,512]{1,0:T(8,128)(2,1)S(1)}, u32[]{:S(2)}, u32[]{:S(2)}) collective-permute-start(bf16[128,512]{1,0:T(8,128)(2,1)S(1)} %get-tuple-element.36), channel_id=1, source_target_pairs={{0,12},{1,13},{2,14},{3,15},{4,8},{5,9},{6,10},{7,11},{8,4},{9,5},... | collective-permute-start | bytes 393224 | tf_op jit(solution)/shard_map/ppermute | solution.py:527
  24.7 18.0 %copy-start.6 = (bf16[4,512,512]{2,1,0:T(8,128)(2,1)S(1)}, bf16[4,512,512]{2,1,0:T(8,128)(2,1)}, u32[]{:S(2)}) copy-start(bf16[4,512,512]{2,1,0:T(8,128)(2,1)} %constant.13.clone.inverse_ref) | copy-start | bytes 6291460
  28.9 27.3 %collective-permute-start.3 = (bf16[128,512]{1,0:T(8,128)(2,1)S(1)}, bf16[128,512]{1,0:T(8,128)(2,1)S(1)}, u32[]{:S(2)}, u32[]{:S(2)}) collective-permute-start(bf16[128,512]{1,0:T(8,128)(2,1)S(1)} %get-tuple-element.25.after_ref), channel_id=1, source_target_pairs={{0,12},{1,13},{2,14},{3,15},{4,8},{5,9},{6,10},{7,11},{8,4},{9,5},... | collective-permute-start | bytes 393224 | tf_op jit(solution)/shard_map/ppermute | solution.py:527
  32.4 22.1 %collective-permute-start.4 = (bf16[128,512]{1,0:T(8,128)(2,1)S(1)}, bf16[128,512]{1,0:T(8,128)(2,1)S(1)}, u32[]{:S(2)}, u32[]{:S(2)}) collective-permute-start(bf16[128,512]{1,0:T(8,128)(2,1)S(1)} %get-tuple-element.31), channel_id=1, source_target_pairs={{0,10},{1,11},{2,8},{3,9},{4,14},{5,15},{6,12},{7,13},{8,2},{9,3},... | collective-permute-start | bytes 393224 | tf_op jit(solution)/shard_map/ppermute | solution.py:527
  40.7 15.4 %collective-permute-start.6 = (bf16[128,512]{1,0:T(8,128)(2,1)S(1)}, bf16[128,512]{1,0:T(8,128)(2,1)S(1)}, u32[]{:S(2)}, u32[]{:S(2)}) collective-permute-start(bf16[128,512]{1,0:T(8,128)(2,1)S(1)} %get-tuple-element.33), channel_id=1, source_target_pairs={{0,14},{1,15},{2,12},{3,13},{4,10},{5,11},{6,8},{7,9},{8,6},{9,7},... | collective-permute-start | bytes 393224 | tf_op jit(solution)/shard_map/ppermute | solution.py:527
  46.8 13.3 %collective-permute-start.12 = (f32[1,64]{1,0:T(1,128)S(1)}, f32[1,64]{1,0:T(1,128)S(1)}, u32[]{:S(2)}, u32[]{:S(2)}) collective-permute-start(f32[1,64]{1,0:T(1,128)S(1)} %get-tuple-element.41), channel_id=1, source_target_pairs={{0,1},{1,2},{2,3},{3,4},{4,5},{5,6},{6,7},{7,8},{8,9},{9,10},{10,1... | collective-permute-start | bytes 776 | tf_op jit(solution)/shard_map/ppermute | solution.py:558
  52.5 7.6 %collective-permute-start.13 = (f32[1,64]{1,0:T(1,128)S(1)}, f32[1,64]{1,0:T(1,128)S(1)}, u32[]{:S(2)}, u32[]{:S(2)}) collective-permute-start(f32[1,64]{1,0:T(1,128)S(1)} %get-tuple-element.42), channel_id=1, source_target_pairs={{1,0},{2,1},{3,2},{4,3},{5,4},{6,5},{7,6},{8,7},{9,8},{10,9},{11,1... | collective-permute-start | bytes 776 | tf_op jit(solution)/shard_map/ppermute | solution.py:557

commit v5 on v4

--- a/solution.py
+++ b/solution.py
@@ -396,8 +396,6 @@
     part = v_ref.shape[3]
     me = me_ref[0]
     steps = range(len(cells))
-    for n in steps:
-        gather_pulses(offsets, places, n, sources, me, total, x_ref.at[n])
 
     def transform(n):
         for q in range(RADIX):
@@ -437,6 +435,7 @@
             copies.append(copy)
 
     for n in steps:
+        gather_pulses(offsets, places, n, sources, me, total, x_ref.at[n])
         transform(n)
     for n in steps:
         correlate_cell(n)

time: 61 us -> 60.9 us (level)
  no operation moved by 1% of the time
where the time goes in v5:
time: 60.9 us; the launch traced here: 60.7 us
  starting transfers between devices  28.1 us (46%)
  Pallas kernels  19.9 us (33%)
  waiting for transfers between devices  9.5 us (16%)
  local copies, waits for them, and re-layouts  1.63 us (3%)
  between operations  0.8 us (1%)
  other arithmetic  0.69 us (1%)
    ppermute x12, starting transfers between devices, send(): return lax.ppermute(piece, 'row', [(i, i ^ offset) for i in range(count)])  20.5 us
    ppermute x12, waiting for transfers between devices, send(): return lax.ppermute(piece, 'row', [(i, i ^ offset) for i in range(count)])  9.49 us
    pallas_call x2, Pallas kernels, focus(): pl.pallas_call(functools.partial(focus_kernel, tuple(offsets), places, tu...  7.95 us
    pallas_call x2, Pallas kernels, compress(): pl.pallas_call(functools.partial(range_kernel, tuple(offsets), late, widt...  7.47 us
    ppermute x1, starting transfers between devices, per_device(): lax.ppermute(right, 'row', [(i, i + 1) for i in range(count - 1)])  5.73 us
    pallas_call x1, Pallas kernels, make_tables(): pl.pallas_call(tables_kernel, out_shape=[jax.ShapeDtypeStruct(*shape) for...  2.4 us
    ppermute x1, starting transfers between devices, per_device(): lax.ppermute(left, 'row', [(i, i - 1) for i in range(1, count)])  1.92 us
    unnamed x14, local copies, waits for them, and re-layouts  1.63 us
  transfers between devices with their start and end apart: 14, of which 5 were waited for; matrix products, arithmetic and copies ran while one was open for 1% of the time, Pallas kernels for 32%

profile of v5, /device:TPU:13, one launch (start us, length us, event | category | flops | bytes accessed | tf_op | source)
XLA Modules:
  0.0 60.7 jit_solution(13747575251347734366)
XLA Ops:
  0.6 0.7 %collective-permute-start = (bf16[64,2,8192]{2,1,0:T(2,128)(2,1)}, bf16[64,2,8192]{2,1,0:T(2,128)(2,1)S(1)}, u32[]{:S(2)}, u32[]{:S(2)}) collective-permute-start(bf16[64,2,8192]{2,1,0:T(2,128)(2,1)} %x_ref.3), channel_id=1, source_target_pairs={{0,1},{1,0},{2,3},{3,2},{4,5},{5,4},{6,7},{7,6},{8,9},{9,8},{10,11... | collective-permute-start | bytes 6291464 | tf_op jit(solution)/shard_map/ppermute | solution.py:526
  1.4 0.7 %pad_convert_fusion.h_ref = f32[2,1280]{1,0:T(2,128)S(1)} fusion(bf16[2,1024]{1,0:T(2,128)(2,1)} %param.9), kind=kLoop, calls=%fused_computation | loop fusion | flops 2560 | bytes 14336 | tf_op jit(solution)/shard_map/jit(_pad)/pad | solution.py:529
  2.1 1.6 %copy-done = bf16[64,2,8192]{2,1,0:T(2,128)(2,1)S(1)} copy-done((bf16[64,2,8192]{2,1,0:T(2,128)(2,1)S(1)}, bf16[64,2,8192]{2,1,0:T(2,128)(2,1)}, u32[]{:S(2)}) %copy-start) | copy-done | bytes 2097176
  3.7 1.5 %range_compress_first.1 = (bf16[64,1024]{1,0:T(8,128)(2,1)S(1)}, bf16[64,1024]{1,0:T(8,128)(2,1)S(1)}) custom-call(s32[1]{0:T(128)} %bitcast.me_ref, bf16[64,2,8192]{2,1,0:T(2,128)(2,1)S(1)} %copy-done, f32[2,1280]{1,0:T(2,128)S(1)} %pad_convert_fusion.h_ref), custom_call_target="tpu_custom_call" | custom-call | flops 1342177280 | bytes 786432 | tf_op jit(solution)/shard_map/range_compress_first/pallas_call | solution.py:203
  5.2 2.3 %collective-permute-start.2 = (bf16[64,1024]{1,0:T(8,128)(2,1)S(1)}, bf16[64,1024]{1,0:T(8,128)(2,1)S(1)}, u32[]{:S(2)}, u32[]{:S(2)}) collective-permute-start(bf16[64,1024]{1,0:T(8,128)(2,1)S(1)} %get-tuple-element.30), channel_id=1, source_target_pairs={{0,9},{1,8},{2,11},{3,10},{4,13},{5,12},{6,15},{7,14},{8,1},{9,0},... | collective-permute-start | bytes 393224 | tf_op jit(solution)/shard_map/ppermute | solution.py:526
  7.4 0.2 collective-permute-start.1
  7.6 1.2 %range_compress.2 = (bf16[128,512]{1,0:T(8,128)(2,1)S(1)}, bf16[128,512]{1,0:T(8,128)(2,1)S(1)}) custom-call(s32[1]{0:T(128)} %bitcast.me_ref, bf16[64,2,8192]{2,1,0:T(2,128)(2,1)S(1)} %copy-done, bf16[64,2,8192]{2,1,0:T(2,128)(2,1)S(1)} %collective-permute-done.sibling_ref, f32[2,1280]{1,0:T(2,128)S(1)} %pad_convert_fusion.h_ref, ...), custom_call_target="tpu_custom_call" | custom-call | flops 1342177280 | bytes 786432 | tf_op jit(solution)/shard_map/range_compress/pallas_call | solution.py:235
  8.9 0.0 copy-start.1
  8.9 0.0 copy-start.2
  8.9 0.0 copy-start.3
  8.9 0.0 copy-start.4
  8.9 0.0 copy-start.5
  8.9 6.2 %range_compress.3 = (bf16[128,512]{1,0:T(8,128)(2,1)S(1)}, bf16[128,512]{1,0:T(8,128)(2,1)S(1)}, bf16[128,1024]{1,0:T(8,128)(2,1)S(1)}, bf16[128,512]{1,0:T(8,12...) custom-call(s32[1]{0:T(128)} %bitcast.me_ref, ...), custom_call_target="tpu_custom_call" | custom-call | flops 8053063680 | bytes 4718592 | tf_op jit(solution)/shard_map/range_compress/pallas_call | solution.py:235
  15.2 2.2 %collective-permute-start.10 = (bf16[128,512]{1,0:T(8,128)(2,1)S(1)}, bf16[128,512]{1,0:T(8,128)(2,1)S(1)}, u32[]{:S(2)}, u32[]{:S(2)}) collective-permute-start(bf16[128,512]{1,0:T(8,128)(2,1)S(1)} %get-tuple-element.37), channel_id=1, source_target_pairs={{0,10},{1,11},{2,8},{3,9},{4,14},{5,15},{6,12},{7,13},{8,2},{9,3},... | collective-permute-start | bytes 393224 | tf_op jit(solution)/shard_map/ppermute | solution.py:526
  17.3 1.3 %collective-permute-start.5 = (bf16[128,1024]{1,0:T(8,128)(2,1)S(1)}, bf16[128,1024]{1,0:T(8,128)(2,1)S(1)}, u32[]{:S(2)}, u32[]{:S(2)}) collective-permute-start(bf16[128,1024]{1,0:T(8,128)(2,1)S(1)} %get-tuple-element.32), channel_id=1, source_target_pairs={{0,2},{1,3},{2,0},{3,1},{4,6},{5,7},{6,4},{7,5},{8,10},{9,11},{10,... | collective-permute-start | bytes 786440 | tf_op jit(solution)/shard_map/ppermute | solution.py:526
  18.6 0.2 collective-permute-start.7
  18.8 1.2 %collective-permute-start.8 = (bf16[128,1024]{1,0:T(8,128)(2,1)S(1)}, bf16[128,1024]{1,0:T(8,128)(2,1)S(1)}, u32[]{:S(2)}, u32[]{:S(2)}) collective-permute-start(bf16[128,1024]{1,0:T(8,128)(2,1)S(1)} %get-tuple-element.35), channel_id=1, source_target_pairs={{0,6},{1,7},{2,4},{3,5},{4,2},{5,3},{6,0},{7,1},{8,14},{9,15},{10,... | collective-permute-start | bytes 786440 | tf_op jit(solution)/shard_map/ppermute | solution.py:526
  20.0 1.8 %collective-permute-done.1.refs_0_ = bf16[64,1024]{1,0:T(8,128)(2,1)S(1)} collective-permute-done((bf16[64,1024]{1,0:T(8,128)(2,1)S(1)}, bf16[64,1024]{1,0:T(8,128)(2,1)S(1)}, u32[]{:S(2)}, u32[]{:S(2)}) %collective-permute-start.1) | collective-permute-done | bytes 131104 | tf_op jit(solution)/shard_map/ppermute | solution.py:526
  21.8 2.9 %collective-permute-done.10.refs_3_ = bf16[128,512]{1,0:T(8,128)(2,1)S(1)} collective-permute-done((bf16[128,512]{1,0:T(8,128)(2,1)S(1)}, bf16[128,512]{1,0:T(8,128)(2,1)S(1)}, u32[]{:S(2)}, u32[]{:S(2)}) %collective-permute-start.10) | collective-permute-done | bytes 131104 | tf_op jit(solution)/shard_map/ppermute | solution.py:526
  24.7 0.0 copy-start.6
  24.8 2.4 %tables.1 = (f32[4,512,512]{2,1,0:T(8,128)S(1)}, bf16[64,1024]{1,0:T(8,128)(2,1)S(1)}, bf16[48,512]{1,0:T(8,128)(2,1)S(1)}, f32[32,64]{1,0:T(8,128)S(1)}) custom-call(s32[1]{0:T(128)} %bitcast.me_ref, bf16[16,2,512]{2,1,0:T(2,128)(2,1)S(1)} %copy-done.1, s32[1,512]{1,0:T(1,128)S(1)} %bitcast.5, s32[1,64]{1,0:T(1,128)S(1)} %bitcast.7, s32[1,512]{1,0:T(1,128)S(1)} %bitcast.6, ...), custom_call_target="tpu_custom_call" | custom-call | flops 2147483648 | bytes 4194304 | tf_op jit(solution)/shard_map/tables/pallas_call | solution.py:347
  27.2 1.8 %collective-permute-done.11.refs_5_ = bf16[128,512]{1,0:T(8,128)(2,1)S(1)} collective-permute-done((bf16[128,512]{1,0:T(8,128)(2,1)S(1)}, bf16[128,512]{1,0:T(8,128)(2,1)S(1)}, u32[]{:S(2)}, u32[]{:S(2)}) %collective-permute-start.11) | collective-permute-done | bytes 131104 | tf_op jit(solution)/shard_map/ppermute | solution.py:526
  28.9 2.1 %collective-permute-start.3 = (bf16[128,512]{1,0:T(8,128)(2,1)S(1)}, bf16[128,512]{1,0:T(8,128)(2,1)S(1)}, u32[]{:S(2)}, u32[]{:S(2)}) collective-permute-start(bf16[128,512]{1,0:T(8,128)(2,1)S(1)} %get-tuple-element.25.after_ref), channel_id=1, source_target_pairs={{0,12},{1,13},{2,14},{3,15},{4,8},{5,9},{6,10},{7,11},{8,4},{9,5},... | collective-permute-start | bytes 393224 | tf_op jit(solution)/shard_map/ppermute | solution.py:526
  31.1 1.3 %collective-permute-done.9.refs_2_ = bf16[128,512]{1,0:T(8,128)(2,1)S(1)} collective-permute-done((bf16[128,512]{1,0:T(8,128)(2,1)S(1)}, bf16[128,512]{1,0:T(8,128)(2,1)S(1)}, u32[]{:S(2)}, u32[]{:S(2)}) %collective-permute-start.9) | collective-permute-done | bytes 131104 | tf_op jit(solution)/shard_map/ppermute | solution.py:526
  32.4 8.4 %collective-permute-start.4 = (bf16[128,512]{1,0:T(8,128)(2,1)S(1)}, bf16[128,512]{1,0:T(8,128)(2,1)S(1)}, u32[]{:S(2)}, u32[]{:S(2)}) collective-permute-start(bf16[128,512]{1,0:T(8,128)(2,1)S(1)} %get-tuple-element.31), channel_id=1, source_target_pairs={{0,10},{1,11},{2,8},{3,9},{4,14},{5,15},{6,12},{7,13},{8,2},{9,3},... | collective-permute-start | bytes 393224 | tf_op jit(solution)/shard_map/ppermute | solution.py:526
  40.7 2.0 %collective-permute-start.6 = (bf16[128,512]{1,0:T(8,128)(2,1)S(1)}, bf16[128,512]{1,0:T(8,128)(2,1)S(1)}, u32[]{:S(2)}, u32[]{:S(2)}) collective-permute-start(bf16[128,512]{1,0:T(8,128)(2,1)S(1)} %get-tuple-element.33), channel_id=1, source_target_pairs={{0,14},{1,15},{2,12},{3,13},{4,10},{5,11},{6,8},{7,9},{8,6},{9,7},... | collective-permute-start | bytes 393224 | tf_op jit(solution)/shard_map/ppermute | solution.py:526
  42.7 4.1 %azimuth_focus.2 = (bf16[256,4,2,512]{3,2,1,0:T(2,128)(2,1)}, f32[32,64]{1,0:T(8,128)S(1)}, f32[1,64]{1,0:T(1,128)S(1)}, f32[1,64]{1,0:T(1,128)S(1)}) custom-call(s32[1]{0:T(128)} %bitcast.me_ref, bf16[4,512,512]{2,1,0:T(8,128)(2,1)S(1)} %copy-done.5, bf16[4,512,512]{2,1,0:T(8,128)(2,1)S(1)} %copy-done.6, f32[4,512,512]{2,1,0:T(8,128)S(1)} %get-tuple-element.27.spectra_ref, ...), custom_call_target="tpu_custom_call" | custom-call | flops 4294967296 | bytes 4194304 | tf_op jit(solution)/shard_map/azimuth_focus/pallas_call | solution.py:471
  46.8 5.7 %collective-permute-start.12 = (f32[1,64]{1,0:T(1,128)S(1)}, f32[1,64]{1,0:T(1,128)S(1)}, u32[]{:S(2)}, u32[]{:S(2)}) collective-permute-start(f32[1,64]{1,0:T(1,128)S(1)} %get-tuple-element.41), channel_id=1, source_target_pairs={{0,1},{1,2},{2,3},{3,4},{4,5},{5,6},{6,7},{7,8},{8,9},{9,10},{10,1... | collective-permute-start | bytes 776 | tf_op jit(solution)/shard_map/ppermute | solution.py:557
  52.5 1.9 %collective-permute-start.13 = (f32[1,64]{1,0:T(1,128)S(1)}, f32[1,64]{1,0:T(1,128)S(1)}, u32[]{:S(2)}, u32[]{:S(2)}) collective-permute-start(f32[1,64]{1,0:T(1,128)S(1)} %get-tuple-element.42), channel_id=1, source_target_pairs={{1,0},{2,1},{3,2},{4,3},{5,4},{6,5},{7,6},{8,7},{9,8},{10,9},{11,1... | collective-permute-start | bytes 776 | tf_op jit(solution)/shard_map/ppermute | solution.py:556
  54.5 1.7 %collective-permute-done.6.refs_5_ = bf16[128,512]{1,0:T(8,128)(2,1)S(1)} collective-permute-done((bf16[128,512]{1,0:T(8,128)(2,1)S(1)}, bf16[128,512]{1,0:T(8,128)(2,1)S(1)}, u32[]{:S(2)}, u32[]{:S(2)}) %collective-permute-start.6) | collective-permute-done | bytes 131104 | tf_op jit(solution)/shard_map/ppermute | solution.py:526
  56.2 3.9 %azimuth_focus.3 = (bf16[256,4,2,512]{3,2,1,0:T(2,128)(2,1)}, f32[32,64]{1,0:T(8,128)S(1)}) custom-call(s32[1]{0:T(128)} %bitcast.me_ref, bf16[4,512,512]{2,1,0:T(8,128)(2,1)S(1)} %copy-done.5, bf16[4,512,512]{2,1,0:T(8,128)(2,1)S(1)} %copy-done.6, f32[4,512,512]{2,1,0:T(8,128)S(1)} %get-tuple-element.27.spectra_ref, ...), custom_call_target="tpu_custom_call", output_to_operand_aliasing={{0}: (15, {})} | custom-call | flops 4294967296 | bytes 4194304 | tf_op jit(solution)/shard_map/azimuth_focus/pallas_call | solution.py:471
  60.1 0.6 %looks.1 = f32[32,64]{1,0:T(8,128)} custom-call(f32[1,64]{1,0:T(1,128)S(1)} %collective-permute-done.12.from_left_ref, f32[1,64]{1,0:T(1,128)S(1)} %collective-permute-done.13.from_right_ref, f32[32,64]{1,0:T(8,128)S(1)} %get-tuple-element.43.inside_ref, f32[32,64]{1,0:T(8,128)S(1)} %get-tuple-element.44.refs_0_, f32[32,64]{1,0:T(8,128)S(1)} %get-tuple-element.45.refs_1_), custom_call_target="tpu_custom_call" | custom-call | flops 1048576 | bytes 65536 | tf_op jit(solution)/shard_map/looks/pallas_call | solution.py:502
  (18 shorter events, 0.0 us)
Async XLA Ops:
  0.6 7.0 %collective-permute-start = (bf16[64,2,8192]{2,1,0:T(2,128)(2,1)}, bf16[64,2,8192]{2,1,0:T(2,128)(2,1)S(1)}, u32[]{:S(2)}, u32[]{:S(2)}) collective-permute-start(bf16[64,2,8192]{2,1,0:T(2,128)(2,1)} %x_ref.3), channel_id=1, source_target_pairs={{0,1},{1,0},{2,3},{3,2},{4,5},{5,4},{6,7},{7,6},{8,9},{9,8},{10,11... | collective-permute-start | bytes 6291464 | tf_op jit(solution)/shard_map/ppermute | solution.py:526
  2.1 1.6 %copy-start = (bf16[64,2,8192]{2,1,0:T(2,128)(2,1)S(1)}, bf16[64,2,8192]{2,1,0:T(2,128)(2,1)}, u32[]{:S(2)}) copy-start(bf16[64,2,8192]{2,1,0:T(2,128)(2,1)} %x_ref.3) | copy-start | bytes 6291460
  5.2 13.6 %collective-permute-start.2 = (bf16[64,1024]{1,0:T(8,128)(2,1)S(1)}, bf16[64,1024]{1,0:T(8,128)(2,1)S(1)}, u32[]{:S(2)}, u32[]{:S(2)}) collective-permute-start(bf16[64,1024]{1,0:T(8,128)(2,1)S(1)} %get-tuple-element.30), channel_id=1, source_target_pairs={{0,9},{1,8},{2,11},{3,10},{4,13},{5,12},{6,15},{7,14},{8,1},{9,0},... | collective-permute-start | bytes 393224 | tf_op jit(solution)/shard_map/ppermute | solution.py:526
  7.4 14.4 %collective-permute-start.1 = (bf16[64,1024]{1,0:T(8,128)(2,1)S(1)}, bf16[64,1024]{1,0:T(8,128)(2,1)S(1)}, u32[]{:S(2)}, u32[]{:S(2)}) collective-permute-start(bf16[64,1024]{1,0:T(8,128)(2,1)S(1)} %get-tuple-element.24.after_ref), channel_id=1, source_target_pairs={{0,8},{1,9},{2,10},{3,11},{4,12},{5,13},{6,14},{7,15},{8,0},{9,1},... | collective-permute-start | bytes 393224 | tf_op jit(solution)/shard_map/ppermute | solution.py:526
  8.9 15.9 %copy-start.1 = (bf16[16,2,512]{2,1,0:T(2,128)(2,1)S(1)}, bf16[16,2,512]{2,1,0:T(2,128)(2,1)}, u32[]{:S(2)}) copy-start(bf16[16,2,512]{2,1,0:T(2,128)(2,1)} %taps_ref.1) | copy-start | bytes 98308
  8.9 15.8 %copy-start.2 = (s32[512]{0:T(512)S(1)}, s32[512]{0:T(512)}, u32[]{:S(2)}) copy-start(s32[512]{0:T(512)} %param.11) | copy-start | bytes 6148
  8.9 15.8 %copy-start.3 = (s32[512]{0:T(512)S(1)}, s32[512]{0:T(512)}, u32[]{:S(2)}) copy-start(s32[512]{0:T(512)} %param.13) | copy-start | bytes 6148
  8.9 15.8 %copy-start.4 = (s32[64]{0:T(128)S(1)}, s32[64]{0:T(128)}, u32[]{:S(2)}) copy-start(s32[64]{0:T(128)} %param.12) | copy-start | bytes 772
  8.9 15.8 %copy-start.5 = (bf16[4,512,512]{2,1,0:T(8,128)(2,1)S(1)}, bf16[4,512,512]{2,1,0:T(8,128)(2,1)}, u32[]{:S(2)}) copy-start(bf16[4,512,512]{2,1,0:T(8,128)(2,1)} %constant.12.clone.matrix_ref.forward_ref) | copy-start | bytes 6291460
  15.2 9.5 %collective-permute-start.10 = (bf16[128,512]{1,0:T(8,128)(2,1)S(1)}, bf16[128,512]{1,0:T(8,128)(2,1)S(1)}, u32[]{:S(2)}, u32[]{:S(2)}) collective-permute-start(bf16[128,512]{1,0:T(8,128)(2,1)S(1)} %get-tuple-element.37), channel_id=1, source_target_pairs={{0,10},{1,11},{2,8},{3,9},{4,14},{5,15},{6,12},{7,13},{8,2},{9,3},... | collective-permute-start | bytes 393224 | tf_op jit(solution)/shard_map/ppermute | solution.py:526
  17.3 23.4 %collective-permute-start.5 = (bf16[128,1024]{1,0:T(8,128)(2,1)S(1)}, bf16[128,1024]{1,0:T(8,128)(2,1)S(1)}, u32[]{:S(2)}, u32[]{:S(2)}) collective-permute-start(bf16[128,1024]{1,0:T(8,128)(2,1)S(1)} %get-tuple-element.32), channel_id=1, source_target_pairs={{0,2},{1,3},{2,0},{3,1},{4,6},{5,7},{6,4},{7,5},{8,10},{9,11},{10,... | collective-permute-start | bytes 786440 | tf_op jit(solution)/shard_map/ppermute | solution.py:526
  18.6 24.1 %collective-permute-start.7 = (bf16[128,1024]{1,0:T(8,128)(2,1)S(1)}, bf16[128,1024]{1,0:T(8,128)(2,1)S(1)}, u32[]{:S(2)}, u32[]{:S(2)}) collective-permute-start(bf16[128,1024]{1,0:T(8,128)(2,1)S(1)} %get-tuple-element.34), channel_id=1, source_target_pairs={{0,4},{1,5},{2,6},{3,7},{4,0},{5,1},{6,2},{7,3},{8,12},{9,13},{10,... | collective-permute-start | bytes 786440 | tf_op jit(solution)/shard_map/ppermute | solution.py:526
  18.8 23.9 %collective-permute-start.8 = (bf16[128,1024]{1,0:T(8,128)(2,1)S(1)}, bf16[128,1024]{1,0:T(8,128)(2,1)S(1)}, u32[]{:S(2)}, u32[]{:S(2)}) collective-permute-start(bf16[128,1024]{1,0:T(8,128)(2,1)S(1)} %get-tuple-element.35), channel_id=1, source_target_pairs={{0,6},{1,7},{2,4},{3,5},{4,2},{5,3},{6,0},{7,1},{8,14},{9,15},{10,... | collective-permute-start | bytes 786440 | tf_op jit(solution)/shard_map/ppermute | solution.py:526
  21.8 7.1 %collective-permute-start.11 = (bf16[128,512]{1,0:T(8,128)(2,1)S(1)}, bf16[128,512]{1,0:T(8,128)(2,1)S(1)}, u32[]{:S(2)}, u32[]{:S(2)}) collective-permute-start(bf16[128,512]{1,0:T(8,128)(2,1)S(1)} %get-tuple-element.38), channel_id=1, source_target_pairs={{0,14},{1,15},{2,12},{3,13},{4,10},{5,11},{6,8},{7,9},{8,6},{9,7},... | collective-permute-start | bytes 393224 | tf_op jit(solution)/shard_map/ppermute | solution.py:526
  24.7 7.7 %collective-permute-start.9 = (bf16[128,512]{1,0:T(8,128)(2,1)S(1)}, bf16[128,512]{1,0:T(8,128)(2,1)S(1)}, u32[]{:S(2)}, u32[]{:S(2)}) collective-permute-start(bf16[128,512]{1,0:T(8,128)(2,1)S(1)} %get-tuple-element.36), channel_id=1, source_target_pairs={{0,12},{1,13},{2,14},{3,15},{4,8},{5,9},{6,10},{7,11},{8,4},{9,5},... | collective-permute-start | bytes 393224 | tf_op jit(solution)/shard_map/ppermute | solution.py:526
  24.7 18.0 %copy-start.6 = (bf16[4,512,512]{2,1,0:T(8,128)(2,1)S(1)}, bf16[4,512,512]{2,1,0:T(8,128)(2,1)}, u32[]{:S(2)}) copy-start(bf16[4,512,512]{2,1,0:T(8,128)(2,1)} %constant.13.clone.inverse_ref) | copy-start | bytes 6291460
  28.9 27.3 %collective-permute-start.3 = (bf16[128,512]{1,0:T(8,128)(2,1)S(1)}, bf16[128,512]{1,0:T(8,128)(2,1)S(1)}, u32[]{:S(2)}, u32[]{:S(2)}) collective-permute-start(bf16[128,512]{1,0:T(8,128)(2,1)S(1)} %get-tuple-element.25.after_ref), channel_id=1, source_target_pairs={{0,12},{1,13},{2,14},{3,15},{4,8},{5,9},{6,10},{7,11},{8,4},{9,5},... | collective-permute-start | bytes 393224 | tf_op jit(solution)/shard_map/ppermute | solution.py:526
  32.4 22.1 %collective-permute-start.4 = (bf16[128,512]{1,0:T(8,128)(2,1)S(1)}, bf16[128,512]{1,0:T(8,128)(2,1)S(1)}, u32[]{:S(2)}, u32[]{:S(2)}) collective-permute-start(bf16[128,512]{1,0:T(8,128)(2,1)S(1)} %get-tuple-element.31), channel_id=1, source_target_pairs={{0,10},{1,11},{2,8},{3,9},{4,14},{5,15},{6,12},{7,13},{8,2},{9,3},... | collective-permute-start | bytes 393224 | tf_op jit(solution)/shard_map/ppermute | solution.py:526
  40.7 15.4 %collective-permute-start.6 = (bf16[128,512]{1,0:T(8,128)(2,1)S(1)}, bf16[128,512]{1,0:T(8,128)(2,1)S(1)}, u32[]{:S(2)}, u32[]{:S(2)}) collective-permute-start(bf16[128,512]{1,0:T(8,128)(2,1)S(1)} %get-tuple-element.33), channel_id=1, source_target_pairs={{0,14},{1,15},{2,12},{3,13},{4,10},{5,11},{6,8},{7,9},{8,6},{9,7},... | collective-permute-start | bytes 393224 | tf_op jit(solution)/shard_map/ppermute | solution.py:526
  46.8 13.3 %collective-permute-start.12 = (f32[1,64]{1,0:T(1,128)S(1)}, f32[1,64]{1,0:T(1,128)S(1)}, u32[]{:S(2)}, u32[]{:S(2)}) collective-permute-start(f32[1,64]{1,0:T(1,128)S(1)} %get-tuple-element.41), channel_id=1, source_target_pairs={{0,1},{1,2},{2,3},{3,4},{4,5},{5,6},{6,7},{7,8},{8,9},{9,10},{10,1... | collective-permute-start | bytes 776 | tf_op jit(solution)/shard_map/ppermute | solution.py:557
  52.5 7.5 %collective-permute-start.13 = (f32[1,64]{1,0:T(1,128)S(1)}, f32[1,64]{1,0:T(1,128)S(1)}, u32[]{:S(2)}, u32[]{:S(2)}) collective-permute-start(f32[1,64]{1,0:T(1,128)S(1)} %get-tuple-element.42), channel_id=1, source_target_pairs={{1,0},{2,1},{3,2},{4,3},{5,4},{6,5},{7,6},{8,7},{9,8},{10,9},{11,1... | collective-permute-start | bytes 776 | tf_op jit(solution)/shard_map/ppermute | solution.py:556
